TPU v7x, 256 devices: a whole 4x4x8 slice. The times are simulated.
256 devices in a mesh: row: 16 (over y, x_lo, core), col: 16 (over z, x_hi).
Axes of the slice: x: 4 (x_hi: 2, x_lo: 2; x = x_hi * 2 + x_lo), y: 4, z: 8, core: 2. Of those that a mesh axis runs over, the one named last changes fastest.
Arguments:
- features: bfloat16 [1024, 128], P(('row', 'col')), may hold values from -6 to 6
- w_left: bfloat16 [128, 128], replicated, may hold values from -0.5 to 0.5
- w_right: bfloat16 [128, 128], replicated, may hold values from -0.5 to 0.5
- w_in: bfloat16 [32, 128], replicated, may hold values from -0.5 to 0.5
- pair_input: bfloat16 [32, 1024, 1024], P(None, 'row', 'col'), may hold values from -6 to 6
- conv_w: bfloat16 [3, 32, 288], replicated, may hold values from -0.375 to 0.375
- w_out: bfloat16 [32], replicated, may hold values from -1 to 1
- dilation: int32 [3], replicated, may hold values from 1 to 8, as said below
- cotangent: float32 [1024, 1024], P('row', 'col'), may hold values from -6 to 6
Outputs:
- logits: float32 [1024, 1024], P('row', 'col')
- grad_rows: float32 [1024, 128], P('row')
- grad_cols: float32 [1024, 128], P('col')
- conv_grads: float32 [3, 32, 288], replicated
Inputs may be any that keep to these rules, and one draw needn't show every extreme that they name: `dilation`: every layer's rate lies in 1 .. 8; at least one layer has rate 8 and another layer has rate 1.
All inputs are finite; a program needn't handle non-finite values.
Results may differ from a plain program's by a relative error of at most 0.02.
Values may be sent and summed in bfloat16 or wider, within the bound.
No kernel may reach another device: no remote copies, remote signals or barrier semaphores. Data moves between devices by JAX's collectives and lax.ppermute only.
A program may use at most 128 MiB of HBM per device.

v0:
```python
import jax
import jax.numpy as jnp
from jax import lax
from jax.sharding import PartitionSpec as P

RMAX = 8


K_ROOT = 0.7978845608028654
CUBIC = 0.044715


def swapped(value, axis, stride):
    mask = 2**stride
    pairs = [(source, source ^ mask) for source in range(lax.axis_size(axis))]
    return lax.ppermute(value, axis, pairs)


def broadcast(value, axis, source):
    kept = jnp.where(lax.axis_index(axis) == source, value, 0).astype(value.dtype)
    return lax.psum(kept, axis)


def extended(cells, sides, width):
    for axis, dim in sides:
        count = lax.axis_size(axis)
        ends = count - 1
        head = lax.slice_in_dim(cells, 0, width, axis=dim)
        tail = lax.slice_in_dim(cells, cells.shape[dim] - width, cells.shape[dim], axis=dim)
        cells = jnp.concatenate(
            [
                lax.ppermute(tail, axis, [(i, (i + 1) % count) for i in range(ends)]),
                cells,
                lax.ppermute(head, axis, [((i + 1) % count, i) for i in range(ends)]),
            ],
            axis=dim,
        )
    return cells


def gelu_pair(value):
    inner = K_ROOT * (value + CUBIC * value * value * value)
    tangent = jnp.tanh(inner)
    result = 0.5 * value * (1.0 + tangent)
    slope = 0.5 * (1.0 + tangent) + 0.5 * value * (1.0 - tangent * tangent) * K_ROOT * (
        1.0 + 3.0 * CUBIC * value * value
    )
    return (result, slope)


def patches(padded, rate, sign, rows, cols):
    depth = padded.shape[0]
    pieces = []
    for down in (-1, 0, 1):
        for across in (-1, 0, 1):
            first = RMAX + sign * down * rate
            second = RMAX + sign * across * rate
            pieces.append(
                lax.dynamic_slice(padded, (jnp.int32(0), first, second), (depth, rows, cols))
            )
    return jnp.concatenate(pieces, 0).reshape(9 * depth, rows * cols)


def flipped(weight):
    channels = weight.shape[0]
    return weight.reshape(channels, 9, channels).transpose(2, 1, 0).reshape(channels, 9 * channels)


def mirror(tile):
    rows_here = tile.shape[0]
    ratio = lax.axis_size("row") // lax.axis_size("col")
    row_at = lax.axis_index("row")
    col_at = lax.axis_index("col")
    low_bits = ratio.bit_length() - 1
    col_bits = lax.axis_size("col").bit_length() - 1
    groups = tile.T.reshape(ratio, rows_here, rows_here)
    for bit in range(col_bits):
        across = swapped(groups, "col", bit)
        moved = swapped(across, "row", bit + low_bits)
        differ = row_at // (ratio * 2**bit) % 2 != col_at // 2**bit % 2
        groups = jnp.where(differ, moved, groups)
    return groups.transpose(1, 0, 2).reshape(rows_here, ratio * rows_here)


def on_device(features, w_left, w_right, w_in, pair_input, conv_w, w_out, dilation, cotangent):
    rows_here = cotangent.shape[0]
    cols_here = cotangent.shape[1]
    channels = w_in.shape[0]
    width = w_in.shape[1]
    ratio = lax.axis_size("row") // lax.axis_size("col")
    length = rows_here * lax.axis_size("row")
    col_at = lax.axis_index("col")
    row_feats = lax.all_gather(features, "col", axis=0, tiled=True)
    col_pieces = broadcast(row_feats, "row", ratio * col_at + 0)
    mirrored_grad = mirror(cotangent)
    row_project = jnp.dot(row_feats, w_left, preferred_element_type=jnp.float32)
    col_project = jnp.dot(col_pieces, w_right, preferred_element_type=jnp.float32)
    outer = row_project.T[:, :, None] + col_project.T[:, None, :]
    hidden, outer_slope = gelu_pair(outer)
    mixed = jnp.dot(
        w_in,
        hidden.astype(jnp.bfloat16).reshape(width, rows_here * cols_here),
        preferred_element_type=jnp.float32,
    )
    state = (mixed.reshape(channels, rows_here, cols_here) + pair_input.astype(jnp.float32)).astype(
        jnp.bfloat16
    )
    saved_state = []
    saved_pad = []
    for layer in range(conv_w.shape[0]):
        activated = gelu_pair(state.astype(jnp.float32))[0].astype(jnp.bfloat16)
        padded = extended(activated, (("row", 1), ("col", 2)), RMAX)
        update = jnp.dot(
            conv_w[layer],
            patches(padded, dilation[layer], 1, rows_here, cols_here),
            preferred_element_type=jnp.float32,
        )
        saved_state.append(state)
        saved_pad.append(padded)
        state = (state.astype(jnp.float32) + update.reshape(channels, rows_here, cols_here)).astype(
            jnp.bfloat16
        )
    direct = jnp.dot(
        w_out, state.reshape(channels, rows_here * cols_here), preferred_element_type=jnp.float32
    ).reshape(rows_here, cols_here)
    logits = 0.5 * (direct + mirror(direct))
    upstream = 0.5 * (cotangent + mirrored_grad)
    grad_state = upstream[None, :, :] * w_out.astype(jnp.float32)[:, None, None]
    weight_grads = []
    for layer in reversed(range(conv_w.shape[0])):
        rounded = grad_state.astype(jnp.bfloat16)
        grad_pad = extended(rounded, (("row", 1), ("col", 2)), RMAX)
        rate = dilation[layer]
        term = lax.dot_general(
            rounded.reshape(channels, rows_here * cols_here),
            patches(saved_pad[layer], rate, 1, rows_here, cols_here),
            (((1,), (1,)), ((), ())),
            preferred_element_type=jnp.float32,
        )
        weight_grads.insert(0, term)
        back = jnp.dot(
            flipped(conv_w[layer]),
            patches(grad_pad, rate, -1, rows_here, cols_here),
            preferred_element_type=jnp.float32,
        )
        slope = gelu_pair(saved_state[layer].astype(jnp.float32))[1]
        grad_state = grad_state + back.reshape(channels, rows_here, cols_here) * slope
    rounded_start = grad_state.astype(jnp.bfloat16).reshape(channels, rows_here * cols_here)
    hidden_grad = lax.dot_general(
        w_in, rounded_start, (((0,), (0,)), ((), ())), preferred_element_type=jnp.float32
    )
    outer_grad = hidden_grad.reshape(width, rows_here, cols_here) * outer_slope
    row_part = jnp.sum(outer_grad, 2).T
    col_part = jnp.sum(outer_grad, 1).T
    left_back = w_left.astype(jnp.float32).T
    right_back = w_right.astype(jnp.float32).T
    row_sum = lax.psum(row_part, "col")
    col_sum = lax.psum(col_part, "row")
    grad_rows = jnp.dot(row_sum, left_back, precision=lax.Precision.HIGHEST)
    grad_cols = jnp.dot(col_sum, right_back, precision=lax.Precision.HIGHEST)
    conv_grads = lax.psum(jnp.stack(weight_grads), ("row", "col")) / length
    return (logits, grad_rows, grad_cols, conv_grads)


def solution(mesh):
    return jax.shard_map(
        on_device,
        mesh=mesh,
        in_specs=(
            P(("row", "col"), None),
            P(),
            P(),
            P(),
            P(None, "row", "col"),
            P(),
            P(),
            P(),
            P("row", "col"),
        ),
        out_specs=(P("row", "col"), P("row", None), P("col", None), P()),
        check_vma=False,
    )
```

profile of v0, /device:TPU:40, one launch (start us, length us, event | category | flops | bytes accessed | tf_op | source)
XLA Modules:
  0.0 825.7 jit_solution(14000583751666826969)
XLA Ops:
  11.2 39.0 %all-gather = bf16[16,4,128]{2,1,0:T(4,128)(2,1)S(1)} all-gather(bf16[1,4,128]{2,1,0:T(4,128)(2,1)} %bitcast.149), channel_id=1, replica_groups=mesh['row'=16,'col'=16] {'col'}, dimensions={0}, use_global_device_ids=true | all-gather | bytes 17408 | tf_op jit(solution)/shard_map/all_gather | solution.py:93
  50.2 46.2 %psum.28 = bf16[64,128]{1,0:T(8,128)(2,1)S(1)} all-reduce(bf16[64,128]{1,0:T(8,128)(2,1)S(1)} %broadcast_select_fusion.6), channel_id=1, replica_groups=mesh['row'=16,'col'=16] {'row'}, use_global_device_ids=true, to_apply=%region_0.1 | all-reduce | flops 8192 | bytes 32768 | tf_op jit(solution)/shard_map/psum | solution.py:21
  101.8 4.5 collective-permute-start.1
  127.5 4.8 collective-permute-done.2
  143.5 7.9 copy.211
  164.8 4.5 collective-permute-start.5
  194.4 4.9 collective-permute-start.29
  215.3 8.7 %copy.217 = bf16[288,64,64]{0,2,1:T(8,128)(2,1)} copy(bf16[288,64,64]{2,1,0:T(8,128)(2,1)} %dynamic-slice_dynamic-update-slice_fusion.32) | data formatting | bytes 4718592 | tf_op jit(solution)/shard_map/concatenate | solution.py:61
  230.4 4.8 collective-permute-start.31
  259.8 8.7 %copy.232 = bf16[288,64,64]{0,2,1:T(8,128)(2,1)} copy(bf16[288,64,64]{2,1,0:T(8,128)(2,1)} %dynamic-slice_dynamic-update-slice_fusion.16) | data formatting | bytes 4718592 | tf_op jit(solution)/shard_map/concatenate | solution.py:61
  280.7 4.5 collective-permute-start.9
  287.9 4.5 collective-permute-start.33
  299.0 5.7 collective-permute-start.11
  313.1 6.3 collective-permute-start.35
  337.2 8.9 %copy.223 = bf16[288,64,64]{0,2,1:T(8,128)(2,1)} copy(bf16[288,64,64]{2,1,0:T(8,128)(2,1)} %dynamic-slice_dynamic-update-slice_fusion.24) | data formatting | bytes 4718592 | tf_op jit(solution)/shard_map/concatenate | solution.py:61
  369.8 8.7 %copy.238 = bf16[288,64,64]{0,2,1:T(8,128)(2,1)} copy(bf16[288,64,64]{2,1,0:T(8,128)(2,1)} %dynamic-slice_dynamic-update-slice_fusion.8) | data formatting | bytes 4718592 | tf_op jit(solution)/shard_map/concatenate | solution.py:61
  384.7 4.9 fusion.65
  409.5 4.9 collective-permute-start.39
  417.0 230.7 %all-reduce.2.cloned.1.call-done = f32[3,32,288]{2,1,0:T(8,128)} async-done(((f32[3,32,288]{2,1,0:T(8,128)}), f32[3,32,288]{2,1,0:T(8,128)}) %all-reduce.2.cloned.1.call-update) | async-done | bytes 110608 | tf_op jit(solution)/shard_map/psum | solution.py:161
  662.6 7.9 copy.244
  678.5 49.5 %psum.30 = f32[64,128]{1,0:T(8,128)S(1)} all-reduce(f32[64,128]{1,0:T(8,128)S(1)} %bitcast.144), channel_id=1, replica_groups=mesh['row'=16,'col'=16] {'row'}, use_global_device_ids=true, to_apply=%region_4.5 | all-reduce | flops 8192 | bytes 65536 | tf_op jit(solution)/shard_map/psum | solution.py:158
  728.0 7.3 collective-permute-start.17
  739.2 73.3 %psum.29 = f32[64,128]{1,0:T(8,128)S(1)} all-reduce(f32[64,128]{1,0:T(8,128)S(1)} %bitcast.143), channel_id=1, replica_groups=mesh['row'=16,'col'=16] {'col'}, use_global_device_ids=true, to_apply=%region_2.3 | all-reduce | flops 8192 | bytes 65536 | tf_op jit(solution)/shard_map/psum | solution.py:157
  813.4 4.6 collective-permute-done.19
  (290 shorter events, 248.7 us)
Async XLA Ops:
  7.2 640.5 %all-reduce.2.cloned.1.call-start = ((), (), s32[]{:S(2)}) async-start(), calls=%async_computation | async-start | bytes 294912 | tf_op jit(solution)/shard_map/psum | solution.py:161
  8.1 98.3 %collective-permute-start.20 = (f32[1,64,64]{2,1,0:T(8,128)S(1)}, f32[1,64,64]{2,1,0:T(8,128)S(1)}, u32[]{:S(2)}, u32[]{:S(2)}) collective-permute-start(f32[1,64,64]{2,1,0:T(8,128)S(1)} %bitcast.145), channel_id=1, source_target_pairs={{0,1},{1,0},{2,3},{3,2},{4,5},{5,4},{6,7},{7,6},{8,9},{9,8},{10,11... | collective-permute-start | bytes 49160 | tf_op jit(solution)/shard_map/ppermute | solution.py:16
  99.9 17.2 %collective-permute-start = (bf16[32,8,64]{2,1,0:T(8,128)(2,1)S(1)}, bf16[32,8,64]{2,1,0:T(8,128)(2,1)S(1)}, u32[]{:S(2)}, u32[]{:S(2)}) collective-permute-start(bf16[32,8,64]{2,1,0:T(8,128)(2,1)S(1)} %get-tuple-element.35), channel_id=1, source_target_pairs={{0,16},{16,32},{32,48},{48,64},{64,80},{80,96},{96,112},{112,128},... | collective-permute-start | bytes 98312 | tf_op jit(solution)/shard_map/ppermute | solution.py:32
  101.8 15.3 %collective-permute-start.1 = (bf16[32,8,64]{2,1,0:T(8,128)(2,1)S(1)}, bf16[32,8,64]{2,1,0:T(8,128)(2,1)S(1)}, u32[]{:S(2)}, u32[]{:S(2)}) collective-permute-start(bf16[32,8,64]{2,1,0:T(8,128)(2,1)S(1)} %get-tuple-element.36), channel_id=1, source_target_pairs={{16,0},{32,16},{48,32},{64,48},{80,64},{96,80},{112,96},{128,112},... | collective-permute-start | bytes 98312 | tf_op jit(solution)/shard_map/ppermute | solution.py:34
  119.9 12.8 %collective-permute-start.3 = (bf16[32,80,8]{1,2,0:T(8,128)(2,1)S(1)}, bf16[32,80,8]{1,2,0:T(8,128)(2,1)S(1)}, u32[]{:S(2)}, u32[]{:S(2)}) collective-permute-start(bf16[32,80,8]{1,2,0:T(8,128)(2,1)S(1)} %copy.208), channel_id=1, source_target_pairs={{1,0},{2,1},{3,2},{4,3},{5,4},{6,5},{7,6},{8,7},{9,8},{10,9},{11,1... | collective-permute-start | bytes 122888 | tf_op jit(solution)/shard_map/ppermute | solution.py:34
  127.3 31.1 %collective-permute-start.24 = (f32[1,64,64]{2,1,0:T(8,128)S(1)}, f32[1,64,64]{2,1,0:T(8,128)S(1)}, u32[]{:S(2)}, u32[]{:S(2)}) collective-permute-start(f32[1,64,64]{2,1,0:T(8,128)S(1)} %broadcast_select_fusion.2), channel_id=1, source_target_pairs={{0,4},{1,5},{2,6},{3,7},{4,0},{5,1},{6,2},{7,3},{8,12},{9,13},{10,... | collective-permute-start | bytes 49160 | tf_op jit(solution)/shard_map/ppermute | solution.py:16
  182.7 18.6 %collective-permute-start.7 = (bf16[32,80,8]{1,2,0:T(8,128)(2,1)}, bf16[32,80,8]{1,2,0:T(8,128)(2,1)}, u32[]{:S(2)}, u32[]{:S(2)}) collective-permute-start(bf16[32,80,8]{1,2,0:T(8,128)(2,1)} %copy.214), channel_id=1, source_target_pairs={{1,0},{2,1},{3,2},{4,3},{5,4},{6,5},{7,6},{8,7},{9,8},{10,9},{11,1... | collective-permute-start | bytes 122888 | tf_op jit(solution)/shard_map/ppermute | solution.py:34
  192.5 31.5 %collective-permute-start.28 = (bf16[32,8,64]{2,1,0:T(8,128)(2,1)}, bf16[32,8,64]{2,1,0:T(8,128)(2,1)}, u32[]{:S(2)}, u32[]{:S(2)}) collective-permute-start(bf16[32,8,64]{2,1,0:T(8,128)(2,1)} %get-tuple-element.37), channel_id=1, source_target_pairs={{0,16},{16,32},{32,48},{48,64},{64,80},{80,96},{96,112},{112,128},... | collective-permute-start | bytes 98312 | tf_op jit(solution)/shard_map/ppermute | solution.py:32
  194.4 29.6 %collective-permute-start.29 = (bf16[32,8,64]{2,1,0:T(8,128)(2,1)}, bf16[32,8,64]{2,1,0:T(8,128)(2,1)}, u32[]{:S(2)}, u32[]{:S(2)}) collective-permute-start(bf16[32,8,64]{2,1,0:T(8,128)(2,1)} %get-tuple-element.38), channel_id=1, source_target_pairs={{16,0},{32,16},{48,32},{64,48},{80,64},{96,80},{112,96},{128,112},... | collective-permute-start | bytes 98312 | tf_op jit(solution)/shard_map/ppermute | solution.py:34
  230.4 15.7 %collective-permute-start.31 = (bf16[32,80,8]{1,2,0:T(8,128)(2,1)}, bf16[32,80,8]{1,2,0:T(8,128)(2,1)}, u32[]{:S(2)}, u32[]{:S(2)}) collective-permute-start(bf16[32,80,8]{1,2,0:T(8,128)(2,1)} %copy.229), channel_id=1, source_target_pairs={{1,0},{2,1},{3,2},{4,3},{5,4},{6,5},{7,6},{8,7},{9,8},{10,9},{11,1... | collective-permute-start | bytes 122888 | tf_op jit(solution)/shard_map/ppermute | solution.py:34
  278.8 13.6 %collective-permute-start.8 = (bf16[32,8,64]{2,1,0:T(8,128)(2,1)S(1)}, bf16[32,8,64]{2,1,0:T(8,128)(2,1)S(1)}, u32[]{:S(2)}, u32[]{:S(2)}) collective-permute-start(bf16[32,8,64]{2,1,0:T(8,128)(2,1)S(1)} %get-tuple-element.31), channel_id=1, source_target_pairs={{0,16},{16,32},{32,48},{48,64},{64,80},{80,96},{96,112},{112,128},... | collective-permute-start | bytes 98312 | tf_op jit(solution)/shard_map/ppermute | solution.py:32
  285.9 20.7 %collective-permute-start.32 = (bf16[32,8,64]{2,1,0:T(8,128)(2,1)}, bf16[32,8,64]{2,1,0:T(8,128)(2,1)}, u32[]{:S(2)}, u32[]{:S(2)}) collective-permute-start(bf16[32,8,64]{2,1,0:T(8,128)(2,1)} %get-tuple-element.29), channel_id=1, source_target_pairs={{0,16},{16,32},{32,48},{48,64},{64,80},{80,96},{96,112},{112,128},... | collective-permute-start | bytes 98312 | tf_op jit(solution)/shard_map/ppermute | solution.py:32
  287.9 18.8 %collective-permute-start.33 = (bf16[32,8,64]{2,1,0:T(8,128)(2,1)}, bf16[32,8,64]{2,1,0:T(8,128)(2,1)}, u32[]{:S(2)}, u32[]{:S(2)}) collective-permute-start(bf16[32,8,64]{2,1,0:T(8,128)(2,1)} %get-tuple-element.30), channel_id=1, source_target_pairs={{16,0},{32,16},{48,32},{64,48},{80,64},{96,80},{112,96},{128,112},... | collective-permute-start | bytes 98312 | tf_op jit(solution)/shard_map/ppermute | solution.py:34
  299.0 24.2 %collective-permute-start.11 = (bf16[32,80,8]{1,2,0:T(8,128)(2,1)}, bf16[32,80,8]{1,2,0:T(8,128)(2,1)}, u32[]{:S(2)}, u32[]{:S(2)}) collective-permute-start(bf16[32,80,8]{1,2,0:T(8,128)(2,1)} %copy.220), channel_id=1, source_target_pairs={{1,0},{2,1},{3,2},{4,3},{5,4},{6,5},{7,6},{8,7},{9,8},{10,9},{11,1... | collective-permute-start | bytes 122888 | tf_op jit(solution)/shard_map/ppermute | solution.py:34
  304.7 16.6 %collective-permute-start.10 = (bf16[32,80,8]{1,2,0:T(8,128)(2,1)}, bf16[32,80,8]{1,2,0:T(8,128)(2,1)}, u32[]{:S(2)}, u32[]{:S(2)}) collective-permute-start(bf16[32,80,8]{1,2,0:T(8,128)(2,1)} %copy.219), channel_id=1, source_target_pairs={{0,1},{1,2},{2,3},{3,4},{4,5},{5,6},{6,7},{7,8},{8,9},{9,10},{10,1... | collective-permute-start | bytes 122888 | tf_op jit(solution)/shard_map/ppermute | solution.py:32
  313.1 43.1 %collective-permute-start.35 = (bf16[32,80,8]{1,2,0:T(8,128)(2,1)}, bf16[32,80,8]{1,2,0:T(8,128)(2,1)}, u32[]{:S(2)}, u32[]{:S(2)}) collective-permute-start(bf16[32,80,8]{1,2,0:T(8,128)(2,1)} %copy.235), channel_id=1, source_target_pairs={{1,0},{2,1},{3,2},{4,3},{5,4},{6,5},{7,6},{8,7},{9,8},{10,9},{11,1... | collective-permute-start | bytes 122888 | tf_op jit(solution)/shard_map/ppermute | solution.py:34
  319.4 34.8 %collective-permute-start.34 = (bf16[32,80,8]{1,2,0:T(8,128)(2,1)}, bf16[32,80,8]{1,2,0:T(8,128)(2,1)}, u32[]{:S(2)}, u32[]{:S(2)}) collective-permute-start(bf16[32,80,8]{1,2,0:T(8,128)(2,1)} %copy.234), channel_id=1, source_target_pairs={{0,1},{1,2},{2,3},{3,4},{4,5},{5,6},{6,7},{7,8},{8,9},{9,10},{10,1... | collective-permute-start | bytes 122888 | tf_op jit(solution)/shard_map/ppermute | solution.py:32
  391.3 14.6 %collective-permute-start.36 = (bf16[32,8,64]{2,1,0:T(8,128)(2,1)S(1)}, bf16[32,8,64]{2,1,0:T(8,128)(2,1)S(1)}, u32[]{:S(2)}, u32[]{:S(2)}) collective-permute-start(bf16[32,8,64]{2,1,0:T(8,128)(2,1)S(1)} %get-tuple-element.26), channel_id=1, source_target_pairs={{0,16},{16,32},{32,48},{48,64},{64,80},{80,96},{96,112},{112,128},... | collective-permute-start | bytes 98312 | tf_op jit(solution)/shard_map/ppermute | solution.py:32
  393.2 12.7 %collective-permute-start.37 = (bf16[32,8,64]{2,1,0:T(8,128)(2,1)S(1)}, bf16[32,8,64]{2,1,0:T(8,128)(2,1)S(1)}, u32[]{:S(2)}, u32[]{:S(2)}) collective-permute-start(bf16[32,8,64]{2,1,0:T(8,128)(2,1)S(1)} %get-tuple-element.27), channel_id=1, source_target_pairs={{16,0},{32,16},{48,32},{64,48},{80,64},{96,80},{112,96},{128,112},... | collective-permute-start | bytes 98312 | tf_op jit(solution)/shard_map/ppermute | solution.py:34
  409.5 242.6 %collective-permute-start.39 = (bf16[32,80,8]{1,2,0:T(8,128)(2,1)S(1)}, bf16[32,80,8]{1,2,0:T(8,128)(2,1)S(1)}, u32[]{:S(2)}, u32[]{:S(2)}) collective-permute-start(bf16[32,80,8]{1,2,0:T(8,128)(2,1)S(1)} %copy.241), channel_id=1, source_target_pairs={{1,0},{2,1},{3,2},{4,3},{5,4},{6,5},{7,6},{8,7},{9,8},{10,9},{11,1... | collective-permute-start | bytes 122888 | tf_op jit(solution)/shard_map/ppermute | solution.py:34
  414.4 237.4 %collective-permute-start.38 = (bf16[32,80,8]{1,2,0:T(8,128)(2,1)S(1)}, bf16[32,80,8]{1,2,0:T(8,128)(2,1)S(1)}, u32[]{:S(2)}, u32[]{:S(2)}) collective-permute-start(bf16[32,80,8]{1,2,0:T(8,128)(2,1)S(1)} %copy.240), channel_id=1, source_target_pairs={{0,1},{1,2},{2,3},{3,4},{4,5},{5,6},{6,7},{7,8},{8,9},{9,10},{10,1... | collective-permute-start | bytes 122888 | tf_op jit(solution)/shard_map/ppermute | solution.py:32
  416.9 232.4 %collective-permute-start.15 = (f32[1,64,64]{2,1,0:T(8,128)S(1)}, f32[1,64,64]{2,1,0:T(8,128)S(1)}, u32[]{:S(2)}, u32[]{:S(2)}) collective-permute-start(f32[1,64,64]{2,1,0:T(8,128)S(1)} %collective-permute-done.14), channel_id=1, source_target_pairs={{0,32},{16,48},{32,0},{48,16},{64,96},{80,112},{96,64},{112,80},{1... | collective-permute-start | bytes 49160 | tf_op jit(solution)/shard_map/ppermute | solution.py:16
  649.2 78.8 %collective-permute-start.16 = (f32[1,64,64]{2,1,0:T(8,128)S(1)}, f32[1,64,64]{2,1,0:T(8,128)S(1)}, u32[]{:S(2)}, u32[]{:S(2)}) collective-permute-start(f32[1,64,64]{2,1,0:T(8,128)S(1)} %broadcast_select_fusion.3), channel_id=1, source_target_pairs={{0,4},{1,5},{2,6},{3,7},{4,0},{5,1},{6,2},{7,3},{8,12},{9,13},{10,... | collective-permute-start | bytes 49160 | tf_op jit(solution)/shard_map/ppermute | solution.py:16
  737.2 75.4 %collective-permute-start.18 = (f32[1,64,64]{2,1,0:T(8,128)S(1)}, f32[1,64,64]{2,1,0:T(8,128)S(1)}, u32[]{:S(2)}, u32[]{:S(2)}) collective-permute-start(f32[1,64,64]{2,1,0:T(8,128)S(1)} %broadcast_select_fusion.5), channel_id=1, source_target_pairs={{0,8},{1,9},{2,10},{3,11},{4,12},{5,13},{6,14},{7,15},{8,0},{9,1},... | collective-permute-start | bytes 49160 | tf_op jit(solution)/shard_map/ppermute | solution.py:16
  (47 other events, 1214.9 us)
Sparse Core Ops, SparseCore 0:
  404.8 242.8 all-reduce.1
where the time goes:
time: 837 us; the launch traced here: 826 us
  waiting for transfers between devices  248 us (30%)
  blocking collectives  208 us (25%)
  local copies, waits for them, and re-layouts  167 us (20%)
  starting transfers between devices  116 us (14%)
  other arithmetic  38.6 us (5%)
  matrix products  27.2 us (3%)
  between operations  21 us (3%)
    psum x1, waiting for transfers between devices, on_device(): conv_grads = lax.psum(jnp.stack(weight_grads), ('row', 'col')) / length  231 us
    psum x1, blocking collectives, on_device(): row_sum = lax.psum(row_part, 'col')  73.3 us
    concatenate x12, local copies, waits for them, and re-layouts, patches(): return jnp.concatenate(pieces, 0).reshape(9 * depth, rows * cols)  57.6 us
    ppermute x12, starting transfers between devices, extended(): lax.ppermute(head, axis, [((i + 1) % count, i) for i in range(ends)])  57.2 us
    unnamed x108, local copies, waits for them, and re-layouts  50.8 us
    psum x1, blocking collectives, on_device(): col_sum = lax.psum(col_part, 'row')  49.5 us
    psum x1, blocking collectives, broadcast(): return lax.psum(kept, axis)  46.2 us
    all_gather x1, blocking collectives, on_device(): row_feats = lax.all_gather(features, 'col', axis=0, tiled=True)  39 us
  transfers between devices with their start and end apart: 41, of which 8 were waited for; matrix products, arithmetic and copies ran while one was open for 19% of the time, Pallas kernels for 0%

commit v1 on v0

v1 whole, which is shorter than its diff:
```python
import jax
import jax.numpy as jnp
from jax import lax
from jax.experimental import pallas as pl
from jax.experimental.pallas import tpu as pltpu
from jax.sharding import PartitionSpec as P

F32 = jnp.float32
BF16 = jnp.bfloat16
K_ROOT = 0.7978845608028654
CUBIC = 0.044715
TILE = 64
HALO = 32
WIDE = TILE + 2 * HALO
CH = 32
VMEM = pl.BlockSpec(memory_space=pltpu.VMEM)
SMEM = pl.BlockSpec(memory_space=pltpu.SMEM)


def gelu(value):
    inner = value * (K_ROOT + (K_ROOT * CUBIC) * (value * value))
    half = 0.5 * value
    return half + half * jnp.tanh(inner)


def gelu_pair(value):
    square = value * value
    tangent = jnp.tanh(value * (K_ROOT + (K_ROOT * CUBIC) * square))
    half = 0.5 * value
    up = 0.5 + 0.5 * tangent
    result = value * up
    slope = up + half * (1.0 - tangent * tangent) * (K_ROOT + (3.0 * K_ROOT * CUBIC) * square)
    return result, slope


def split(value):
    high = value.astype(BF16)
    return high, (value - high.astype(F32)).astype(BF16)


def edges_kernel(pair_ref, cot_ref, own_ref, left_ref, right_ref):
    own = jnp.swapaxes(pair_ref[...].astype(F32), 0, 1)
    own_ref[...] = own.astype(BF16)
    cot = cot_ref[...]
    for out_ref, first in ((left_ref, 0), (right_ref, TILE - HALO)):
        last = first + HALO
        for q in range(16):
            out_ref[q] = jnp.concatenate(
                [own[q + 16 * m, :, first:last] for m in range(4)], axis=1
            ).astype(BF16)
        edge = jnp.concatenate([cot[16 * m : 16 * m + 16, first:last] for m in range(4)], axis=1)
        high, low = split(edge)
        out_ref[16, 0:16, :] = high
        out_ref[16, 16:32, :] = low


def widen_kernel(own_ref, cot_ref, from_left_ref, from_right_ref, upper_ref, lower_ref):
    cot = cot_ref[...]
    for m in range(4):
        out_ref = (upper_ref, lower_ref)[m // 2]
        lanes = slice(HALO * m, HALO * m + HALO)
        base = 16 * (m % 2)
        for q in range(16):
            out_ref[base + q] = jnp.concatenate(
                [
                    own_ref[16 * m + q].astype(F32),
                    from_right_ref[q].astype(F32)[:, lanes],
                    from_left_ref[q].astype(F32)[:, lanes],
                ],
                axis=1,
            ).astype(BF16)
        high, low = split(cot[16 * m : 16 * m + 16, :])
        for part, row, at in ((high, 32, 0), (low, 33, 16)):
            out_ref[row, base : base + 16, :] = jnp.concatenate(
                [
                    part.astype(F32),
                    from_right_ref[16, at : at + 16, :].astype(F32)[:, lanes],
                    from_left_ref[16, at : at + 16, :].astype(F32)[:, lanes],
                ],
                axis=1,
            ).astype(BF16)


def mixed_kernel(place_ref, feat_ref, w_left_ref, w_right_ref, w_in_ref, mixed_ref, rows_ref, cols_ref):
    row = place_ref[0]
    col = place_ref[1]
    row_chunks = [jnp.maximum(2 * row - 1, 0), 2 * row, 2 * row + 1, jnp.minimum(2 * row + 2, 31)]
    col_chunks = [2 * col, 2 * col + 1, jnp.minimum(2 * col + 2, 31), jnp.maximum(2 * col - 1, 0)]
    for chunks, weight_ref, out_ref in (
        (row_chunks, w_left_ref, rows_ref),
        (col_chunks, w_right_ref, cols_ref),
    ):
        picked = jnp.concatenate([feat_ref[chunk] for chunk in chunks], axis=0)
        out_ref[...] = jnp.dot(picked, weight_ref[...], preferred_element_type=F32)
    w_in = w_in_ref[...]

    def body(step, carry):
        for k in range(2):
            pair = []
            for i in range(2):
                outer = rows_ref[pl.ds(4 * step + 2 * k + i, 1), :] + cols_ref[...]
                pair.append(gelu(outer).astype(BF16))
            out = lax.dot_general(
                w_in, jnp.concatenate(pair, 0), (((1,), (1,)), ((), ())), preferred_element_type=F32
            )
            for i in range(2):
                mixed_ref[4 * step + 2 * k + i] = out[:, WIDE * i : WIDE * i + WIDE]
        return carry

    lax.fori_loop(0, WIDE // 4, body, 0)


def shifted(value, rate):
    return jnp.concatenate(
        [pltpu.roll(value, rate, 1), value, pltpu.roll(value, WIDE - rate, 1)], axis=0
    ).astype(BF16)


def lane_mask(col):
    lane = lax.broadcasted_iota(jnp.int32, (1, WIDE), 1)
    bin_at = TILE * col + jnp.where(lane < TILE + HALO, lane, lane - WIDE)
    return jnp.where((bin_at >= 0) & (bin_at < 1024), 1.0, 0.0).astype(F32)


def row_valid(row, i):
    at = TILE * row - HALO + i
    return jnp.where((at >= 0) & (at < 1024), 1.0, 0.0).astype(F32)


def gather_taps(z_ref, i, rate):
    return z_ref[i - rate, 0:CH, :] + z_ref[i, CH : 2 * CH, :] + z_ref[i + rate, 2 * CH : 3 * CH, :]


def rows_loop(first, last, one, many):
    def body(step, carry):
        base = first + 4 * step
        for k in range(2):
            i = base + 2 * k
            many(i, jnp.concatenate([one(i), one(i + 1)], axis=1))
        return carry

    lax.fori_loop(0, (last - first) // 4, body, 0)


def main_kernel(
    place_ref,
    mixed_ref,
    part0_ref,
    part1_ref,
    part2_ref,
    part3_ref,
    mirror_ref,
    forward_ref,
    backward_ref,
    w_out_ref,
    direct_ref,
    terms_ref,
    grad_ref,
    round_ref,
    slope0_ref,
    state_ref,
    slope1_ref,
    slope2_ref,
    za_ref,
    zb_ref,
    patch0_ref,
    patch1_ref,
    patch2_ref,
    masked_ref,
    upstream_ref,
    grad2_ref,
):
    row = place_ref[0]
    col = place_ref[1]
    rates = [place_ref[2], place_ref[3], place_ref[4]]
    inside = lane_mask(col)
    patch_refs = (patch0_ref, patch1_ref, patch2_ref)
    parts = (part0_ref, part1_ref, part2_ref, part3_ref)
    w_out = w_out_ref[...]
    z_refs = (za_ref, zb_ref)

    for n in range(4):

        def start(q, carry, n=n):
            given = parts[n][q].astype(F32)
            state_ref[HALO * n + q] = (mixed_ref[HALO * n + q] + given).astype(BF16)
            return carry

        lax.fori_loop(0, HALO, start, 0, unroll=4)

    def activate(layer, i, state):
        act, slope = gelu_pair(state)
        if layer == 0:
            slope0_ref[i] = slope
        else:
            (slope1_ref, slope2_ref)[layer - 1][i] = slope
        return shifted(act * (inside * row_valid(row, i)), rates[layer])

    for layer in range(3):
        z_now = z_refs[layer % 2]
        z_last = z_refs[(layer + 1) % 2]

        def one(i, layer=layer, z_last=z_last):
            if layer == 0:
                state = state_ref[i].astype(F32)
            else:
                new = state_ref[i].astype(F32) + gather_taps(z_last, i, rates[layer - 1])
                new = new.astype(BF16)
                state_ref[i] = new
                state = new.astype(F32)
            out = activate(layer, i, state)
            patch_refs[layer][i] = out
            return out

        def many(i, pair, layer=layer, z_now=z_now):
            z = jnp.dot(forward_ref[layer], pair, preferred_element_type=F32)
            z_now[i] = z[:, :WIDE]
            z_now[i + 1] = z[:, WIDE:]

        rows_loop(8 * layer, WIDE - 8 * layer, one, many)

    def finish(i, carry):
        new = state_ref[i].astype(F32) + gather_taps(za_ref, i, rates[2])
        new = new.astype(BF16).astype(F32)
        direct_ref[pl.ds(i - HALO, 1), :] = jnp.sum(new * w_out, axis=0, keepdims=True)[:, :TILE]
        return carry

    lax.fori_loop(HALO, HALO + TILE, finish, 0, unroll=4)

    other = mirror_ref[...].T
    other = jnp.concatenate([other[96:128], other[0:96]], axis=0)
    other = jnp.concatenate([other[:, 32:128], other[:, 0:32]], axis=1)
    for n in range(4):
        mine = parts[n][32].astype(F32) + parts[n][33].astype(F32)
        rows = slice(HALO * n, HALO * n + HALO)
        upstream_ref[rows, :] = 0.5 * (mine + other[rows, :])

    tile_lanes = jnp.where(lax.broadcasted_iota(jnp.int32, (1, WIDE), 1) < TILE, 1.0, 0.0).astype(F32)
    terms_ref[...] = jnp.zeros_like(terms_ref)
    masked_ref[...] = jnp.zeros_like(masked_ref)

    def weight_terms(layer):
        def keep(i, carry):
            masked_ref[i] = (round_ref[i].astype(F32) * tile_lanes).astype(BF16)
            return carry

        lax.fori_loop(HALO, HALO + TILE, keep, 0, unroll=4)
        rate = rates[layer]

        def body(step, total):
            base = 24 + 4 * step
            left = jnp.concatenate(
                [
                    jnp.concatenate([masked_ref[base + k + off] for k in range(4)], axis=1)
                    for off in (rate, 0, -rate)
                ],
                axis=0,
            )
            right = jnp.concatenate([patch_refs[layer][base + k] for k in range(4)], axis=1)
            return total + lax.dot_general(
                left, right, (((1,), (1,)), ((), ())), preferred_element_type=F32
            )

        terms_ref[layer] = lax.fori_loop(0, 20, body, jnp.zeros((96, 96), F32))

    def back(layer, first, last, one_grad, z_now):
        def one(i):
            rounded = one_grad(i).astype(BF16)
            round_ref[i] = rounded
            return shifted(rounded.astype(F32), rates[layer])

        def many(i, pair):
            z = jnp.dot(backward_ref[layer], pair, preferred_element_type=F32)
            z_now[i] = z[:, :WIDE]
            z_now[i + 1] = z[:, WIDE:]

        rows_loop(first, last, one, many)
        weight_terms(layer)

    def first_grad(i):
        return upstream_ref[pl.ds(i, 1), :] * w_out

    def second_grad(i):
        new = first_grad(i) + gather_taps(zb_ref, i, rates[2]) * slope2_ref[i]
        new = new * (inside * row_valid(row, i))
        grad2_ref[i] = new
        return new

    back(2, 8, 120, first_grad, zb_ref)
    back(1, 16, 112, second_grad, za_ref)

    def third_grad(i, carry):
        new = grad2_ref[i] + gather_taps(za_ref, i, rates[1]) * slope1_ref[i]
        new = new * (inside * row_valid(row, i))
        grad_ref[i] = new
        round_ref[i] = new.astype(BF16)
        return carry

    lax.fori_loop(24, 104, third_grad, 0, unroll=4)
    weight_terms(0)


def last_kernel(
    place_ref,
    grad_ref,
    round_ref,
    slope0_ref,
    rows_ref,
    cols_ref,
    backward_ref,
    w_in_ref,
    row_ref,
    col_ref,
    z_ref,
):
    rate = place_ref[2]

    def one(i):
        return shifted(round_ref[i].astype(F32), rate)

    def many(i, pair):
        z = jnp.dot(backward_ref[0], pair, preferred_element_type=F32)
        z_ref[i] = z[:, :WIDE]
        z_ref[i + 1] = z[:, WIDE:]

    rows_loop(24, 104, one, many)
    w_in = w_in_ref[...]
    cols = cols_ref[0:TILE, :]

    def body(step, total):
        for k in range(2):
            i = HALO + 2 * step + k
            start = grad_ref[i] + gather_taps(z_ref, i, rate) * slope0_ref[i]
            hidden = lax.dot_general(
                start[:, :TILE].astype(BF16), w_in, (((0,), (0,)), ((), ())), preferred_element_type=F32
            )
            slope = gelu_pair(rows_ref[pl.ds(i, 1), :] + cols)[1]
            outer = hidden * slope
            row_ref[pl.ds(i - HALO, 1), :] = jnp.sum(outer, axis=0, keepdims=True)
            total = total + outer
        return total

    col_ref[...] = lax.fori_loop(0, TILE // 2, body, jnp.zeros((TILE, 128), F32))


def shape(*dims, dtype=F32):
    return jax.ShapeDtypeStruct(dims, dtype)


def call(kernel, outs, specs, scratch=()):
    return pl.pallas_call(
        kernel,
        out_shape=outs,
        in_specs=specs,
        out_specs=[VMEM] * len(outs),
        scratch_shapes=list(scratch),
        compiler_params=pltpu.CompilerParams(vmem_limit_bytes=56 * 2**20),
    )


def flips(axis, bit):
    return [(i, i ^ bit) for i in range(lax.axis_size(axis))]


def on_device(features, w_left, w_right, w_in, pair_input, conv_w, w_out, dilation, cotangent):
    n_row = lax.axis_size("row")
    n_col = lax.axis_size("col")
    row_at = lax.axis_index("row").astype(jnp.int32)
    col_at = lax.axis_index("col").astype(jnp.int32)
    place = jnp.concatenate([jnp.stack([row_at, col_at]), dilation, jnp.zeros((3,), jnp.int32)])
    up = [(i, i + 1) for i in range(n_row - 1)]
    down = [(i + 1, i) for i in range(n_row - 1)]
    swap = [(r * n_col + c, c * n_col + r) for r in range(n_row) for c in range(n_col)]

    own, left_edge, right_edge = call(
        edges_kernel,
        [shape(TILE, CH, TILE, dtype=BF16)] + [shape(17, CH, WIDE, dtype=BF16)] * 2,
        [VMEM] * 2,
    )(pair_input, cotangent)
    from_left = lax.ppermute(right_edge, "col", up)
    from_right = lax.ppermute(left_edge, "col", down)

    sent = jnp.broadcast_to(features.reshape(1, 1, 512), (n_row * n_col, 1, 512))
    gathered = lax.all_to_all(sent, ("row", "col"), 0, 0).reshape(32, 32, 128)

    upper, lower = call(
        widen_kernel, [shape(HALO + 2, CH, WIDE, dtype=BF16)] * 2, [VMEM] * 4
    )(own, cotangent, from_left, from_right)
    above = lax.ppermute(lower, "row", up)
    below = lax.ppermute(upper, "row", down)

    mixed, row_project, col_project = call(
        mixed_kernel,
        [shape(WIDE, CH, WIDE), shape(WIDE, 128), shape(WIDE, 128)],
        [SMEM] + [VMEM] * 4,
    )(place, gathered, w_left, w_right, w_in)

    wide_cot = jnp.concatenate(
        [part[32].astype(F32) + part[33].astype(F32) for part in (above, upper, lower, below)], axis=0
    )
    mirrored = lax.ppermute(wide_cot, ("row", "col"), swap)

    forward_w = conv_w.reshape(3, CH, 3, 3 * CH).transpose(0, 2, 1, 3).reshape(3, 96, 96)
    backward_w = (
        conv_w.reshape(3, CH, 3, 3, CH)[:, :, ::-1, ::-1, :].transpose(0, 2, 4, 3, 1).reshape(3, 96, 96)
    )
    w_out_wide = jnp.broadcast_to(w_out.astype(F32)[:, None], (CH, WIDE))
    big = (WIDE, CH, WIDE)
    direct, terms, grad, rounded, slope0 = call(
        main_kernel,
        [shape(TILE, TILE), shape(3, 96, 96), shape(*big), shape(*big, dtype=BF16), shape(*big)],
        [SMEM] + [VMEM] * 9,
        [
            pltpu.VMEM(big, BF16),
            pltpu.VMEM(big, F32),
            pltpu.VMEM(big, F32),
            pltpu.VMEM((WIDE, 96, WIDE), F32),
            pltpu.VMEM((WIDE, 96, WIDE), F32),
            pltpu.VMEM((WIDE, 96, WIDE), BF16),
            pltpu.VMEM((WIDE, 96, WIDE), BF16),
            pltpu.VMEM((WIDE, 96, WIDE), BF16),
            pltpu.VMEM(big, BF16),
            pltpu.VMEM((WIDE, WIDE), F32),
            pltpu.VMEM(big, F32),
        ],
    )(place, mixed, above, upper, lower, below, mirrored, forward_w, backward_w, w_out_wide)

    row_part, col_part = call(
        last_kernel,
        [shape(TILE, 128), shape(TILE, 128)],
        [SMEM] + [VMEM] * 7,
        [pltpu.VMEM((WIDE, 96, WIDE), F32)],
    )(place, grad, rounded, slope0, row_project, col_project, backward_w, w_in)

    other = lax.ppermute(direct, ("row", "col"), swap)
    logits = 0.5 * (direct + other.T)

    def summed(value, axis, bit):
        value = value.astype(BF16)
        return value.astype(F32) + lax.ppermute(value, axis, flips(axis, bit)).astype(F32)

    packed = terms.reshape(216, 128)
    for bit in (1, 2, 4, 8):
        packed = summed(packed, "row", bit)
        row_part = summed(row_part, "col", bit)
        col_part = summed(col_part, "row", bit)
    for bit in (1, 2, 4, 8):
        packed = summed(packed, "col", bit)
    conv_grads = (
        packed.reshape(3, 3, CH, 96).transpose(0, 2, 1, 3).reshape(3, CH, 288) / (TILE * n_row)
    )
    grad_rows = jnp.dot(row_part, w_left.astype(F32).T, precision=lax.Precision.HIGHEST)
    grad_cols = jnp.dot(col_part, w_right.astype(F32).T, precision=lax.Precision.HIGHEST)
    return (logits, grad_rows, grad_cols, conv_grads)


def solution(mesh):
    return jax.shard_map(
        on_device,
        mesh=mesh,
        in_specs=(
            P(("row", "col"), None),
            P(),
            P(),
            P(),
            P(None, "row", "col"),
            P(),
            P(),
            P(),
            P("row", "col"),
        ),
        out_specs=(P("row", "col"), P("row", None), P("col", None), P()),
        check_vma=False,
    )
```

time: 837 us -> 198 us (0.24)
  waiting for transfers between devices: 248 us -> 20.4 us
  blocking collectives: 208 us -> 0 us
  local copies, waits for them, and re-layouts: 167 us -> 8.55 us
  Pallas kernels: 0 us -> 80.7 us
  starting transfers between devices: 116 us -> 73 us
  other arithmetic: 38.6 us -> 9.04 us
  matrix products: 27.2 us -> 1.62 us
  between operations: 21 us -> 0.99 us
    psum x1 -> x0, waiting for transfers between devices: 231 us -> none  [on_device(): conv_grads = lax.psum(jnp.stack(weight_grads), ('row', 'col')) / length]
    psum x3 -> x0, blocking collectives: 169 us -> none  [the longest x1 73.3 us: on_device(): row_sum = lax.psum(row_part, 'col')]
    pallas_call x0 -> x5, Pallas kernels: none -> 80.7 us  [the longest x1 52.5 us: on_device(): call(main_kernel, [shape(TILE, TILE), shape(3, 96, 96), shape(*big), shap...]
    ppermute x40 -> x22, starting transfers between devices: 116 us -> 57.3 us  [the longest x16 38.1 us: summed(): lax.ppermute(value, axis, flips(axis, bit)).astype(F32)]
    concatenate x12 -> x0, local copies, waits for them, and re-layouts: 57.6 us -> none  [patches(): return jnp.concatenate(pieces, 0).reshape(9 * depth, rows * cols)]
    unnamed x108 -> x28, local copies, waits for them, and re-layouts: 50.8 us -> 1.68 us
    all_gather x1 -> x0, blocking collectives: 39 us -> none  [on_device(): row_feats = lax.all_gather(features, 'col', axis=0, tiled=True)]
    dot_general x16 -> x2, matrix products: 27.2 us -> 1.62 us  [the longest x1 0.81 us: on_device(): jnp.dot(row_part, w_left.astype(F32).T, precision=lax.Precision.HIGHEST)]
  transfers between devices with their start and end apart: 41 -> 23, of which waited for: 8 -> 8; matrix products, arithmetic and copies ran while one was open for 19% -> 8% of each run, Pallas kernels for 0% -> 5%
where the time goes in v1:
time: 198 us; the launch traced here: 194 us
  Pallas kernels  80.7 us (41%)
  starting transfers between devices  73 us (37%)
  waiting for transfers between devices  20.4 us (10%)
  other arithmetic  9.04 us (5%)
  local copies, waits for them, and re-layouts  8.55 us (4%)
    pallas_call x1, Pallas kernels, on_device(): call(main_kernel, [shape(TILE, TILE), shape(3, 96, 96), shape(*big), shap...  52.5 us
    ppermute x16, starting transfers between devices, summed(): lax.ppermute(value, axis, flips(axis, bit)).astype(F32)  38.1 us
    all_to_all x1, starting transfers between devices, on_device(): gathered = lax.all_to_all(sent, ('row', 'col'), 0, 0).reshape(32, 32, 128)  15.7 us
    pallas_call x1, Pallas kernels, on_device(): call(last_kernel, [shape(TILE, 128), shape(TILE, 128)], [SMEM] + [VMEM] *...  14.3 us
    ppermute x16, waiting for transfers between devices, summed(): lax.ppermute(value, axis, flips(axis, bit)).astype(F32)  11.2 us
    pallas_call x1, Pallas kernels, on_device(): call(mixed_kernel, [shape(WIDE, CH, WIDE), shape(WIDE, 128), shape(WIDE,...  9.31 us
    ppermute x1, starting transfers between devices, on_device(): from_left = lax.ppermute(right_edge, 'col', up)  4.92 us
  transfers between devices with their start and end apart: 23, of which 8 were waited for; matrix products, arithmetic and copies ran while one was open for 8% of the time, Pallas kernels for 5%

profile of v1, /device:TPU:40, one launch (start us, length us, event | category | flops | bytes accessed | tf_op | source)
XLA Modules:
  0.0 194.3 jit_solution(6583140392529418033)
XLA Ops:
  0.6 2.3 %shard_map.121 = (bf16[64,32,64]{2,1,0:T(8,128)(2,1)}, bf16[17,32,128]{2,1,0:T(8,128)(2,1)}, bf16[17,32,128]{2,1,0:T(8,128)(2,1)}) custom-call(bf16[32,64,64]{2,1,0:T(8,128)(2,1)} %pair_ref.1, f32[64,64]{1,0:T(8,128)} %cot_ref.3), custom_call_target="tpu_custom_call" | custom-call | tf_op jit(solution)/shard_map/pallas_call | solution.py:375
  3.0 4.9 %collective-permute-start = (bf16[17,32,128]{2,1,0:T(8,128)(2,1)}, bf16[17,32,128]{2,1,0:T(8,128)(2,1)S(1)}, u32[]{:S(2)}, u32[]{:S(2)}) collective-permute-start(bf16[17,32,128]{2,1,0:T(8,128)(2,1)} %get-tuple-element.21), channel_id=1, source_target_pairs={{0,1},{1,2},{2,3},{3,4},{4,5},{5,6},{6,7},{7,8},{8,9},{9,10},{10,1... | collective-permute-start | bytes 417800 | tf_op jit(solution)/shard_map/ppermute | solution.py:380
  7.9 3.3 %collective-permute-start.1 = (bf16[17,32,128]{2,1,0:T(8,128)(2,1)}, bf16[17,32,128]{2,1,0:T(8,128)(2,1)S(1)}, u32[]{:S(2)}, u32[]{:S(2)}) collective-permute-start(bf16[17,32,128]{2,1,0:T(8,128)(2,1)} %get-tuple-element.22), channel_id=1, source_target_pairs={{1,0},{2,1},{3,2},{4,3},{5,4},{6,5},{7,6},{8,7},{9,8},{10,9},{11,1... | collective-permute-start | bytes 417800 | tf_op jit(solution)/shard_map/ppermute | solution.py:381
  12.9 3.8 %collective-permute-done.1.from_right_ref = bf16[17,32,128]{2,1,0:T(8,128)(2,1)S(1)} collective-permute-done((bf16[17,32,128]{2,1,0:T(8,128)(2,1)}, bf16[17,32,128]{2,1,0:T(8,128)(2,1)S(1)}, u32[]{:S(2)}, u32[]{:S(2)}) %collective-permute-start.1) | collective-permute-done | bytes 139296 | tf_op jit(solution)/shard_map/ppermute | solution.py:381
  17.3 2.2 %shard_map.122 = (bf16[34,32,128]{2,1,0:T(8,128)(2,1)}, bf16[34,32,128]{2,1,0:T(8,128)(2,1)}) custom-call(bf16[64,32,64]{2,1,0:T(8,128)(2,1)} %get-tuple-element.20.own_ref, f32[64,64]{1,0:T(8,128)} %cot_ref.3, bf16[17,32,128]{2,1,0:T(8,128)(2,1)} %copy-done.5, bf16[17,32,128]{2,1,0:T(8,128)(2,1)} %copy-done.6), custom_call_target="tpu_custom_call" | custom-call | tf_op jit(solution)/shard_map/pallas_call | solution.py:386
  22.9 2.2 %reduce.1 = bf16[256,512]{1,0:T(8,128)(2,1)S(1)} reduce(bf16[256,1,512]{2,1,0:T(2,128)(2,1)S(1)} %broadcast_in_dim.14, bf16[]{:T(256)} %broadcast.14), dimensions={1}, to_apply=%broadcast_in_dim.14.reduce_sub_computation | reduce | bytes 524290 | tf_op jit(solution)/shard_map/broadcast_in_dim | solution.py:383
  25.9 15.7 %all-to-all-start = ((bf16[256,2,256]{2,1,0:T(2,128)(2,1)}), bf16[256,2,256]{2,1,0:T(2,128)(2,1)S(1)}, u32[]{:S(2)}, u32[]{:S(2)}) async-start(bf16[256,2,256]{2,1,0:T(2,128)(2,1)} %reshape.54), calls=%async_computation | async-start | bytes 524288 | tf_op jit(solution)/shard_map/all_to_all | solution.py:384
  44.3 3.1 %collective-permute-start.3 = (bf16[34,32,128]{2,1,0:T(8,128)(2,1)S(1)}, bf16[34,32,128]{2,1,0:T(8,128)(2,1)S(1)}, u32[]{:S(2)}, u32[]{:S(2)}) collective-permute-start(bf16[34,32,128]{2,1,0:T(8,128)(2,1)S(1)} %copy-done), channel_id=1, source_target_pairs={{16,0},{32,16},{48,32},{64,48},{80,64},{96,80},{112,96},{128,112},... | collective-permute-start | bytes 835592 | tf_op jit(solution)/shard_map/ppermute | solution.py:390
  48.2 3.8 %collective-permute-done.3.part3_ref = bf16[34,32,128]{2,1,0:T(8,128)(2,1)S(1)} collective-permute-done((bf16[34,32,128]{2,1,0:T(8,128)(2,1)S(1)}, bf16[34,32,128]{2,1,0:T(8,128)(2,1)S(1)}, u32[]{:S(2)}, u32[]{:S(2)}) %collective-permute-start.3) | collective-permute-done | bytes 278560 | tf_op jit(solution)/shard_map/ppermute | solution.py:390
  51.9 3.6 %collective-permute-start.4 = (f32[128,128]{1,0:T(8,128)S(1)}, f32[128,128]{1,0:T(8,128)S(1)}, u32[]{:S(2)}, u32[]{:S(2)}) collective-permute-start(f32[128,128]{1,0:T(8,128)S(1)} %pad_maximum_fusion), channel_id=1, source_target_pairs={{0,0},{1,16},{2,32},{3,48},{4,64},{5,80},{6,96},{7,112},{8,128},{9... | collective-permute-start | bytes 196616 | tf_op jit(solution)/shard_map/ppermute | solution.py:401
  58.9 9.3 %shard_map.120 = (f32[128,32,128]{2,1,0:T(8,128)}, f32[128,128]{1,0:T(8,128)}, f32[128,128]{1,0:T(8,128)}) custom-call(s32[8]{0:T(128)} %pad_add_fusion.place_ref, bf16[32,32,128]{2,1,0:T(8,128)(2,1)} %reshape.48.feat_ref, bf16[128,128]{1,0:T(8,128)(2,1)} %w_left_ref.1, bf16[128,128]{1,0:T(8,128)(2,1)} %w_right_ref.1, bf16[32,128]{1,0:T(8,128)(2,1)} %w_in_ref.3), custom_call_target="tpu_custom_call" | custom-call | tf_op jit(solution)/shard_map/pallas_call | solution.py:392
  68.9 52.5 %shard_map.123 = (f32[64,64]{1,0:T(8,128)}, f32[3,96,96]{2,1,0:T(8,128)}, f32[128,32,128]{2,1,0:T(8,128)}, bf16[128,32,128]{2,1,0:T(8,128)(2,1)}, f32[128,32,128]{2,1,0:T(8,128)}) custom-call(s32[8]{0:T(128)} %pad_add_fusion.place_ref, f32[128,32,128]{2,1,0:T(8,128)} %get-tuple-element.19.mixed_ref, bf16[34,32,128]{2,1,0:T(8,128)(2,1)} %copy-done.1, ...), custom_call_target="tpu_custom_call" | custom-call | tf_op jit(solution)/shard_map/pallas_call | solution.py:409
  121.4 14.3 %shard_map.124 = (f32[64,128]{1,0:T(8,128)}, f32[64,128]{1,0:T(8,128)}) custom-call(s32[8]{0:T(128)} %pad_add_fusion.place_ref, f32[128,32,128]{2,1,0:T(8,128)} %get-tuple-element.26.grad_ref, bf16[128,32,128]{2,1,0:T(8,128)(2,1)} %get-tuple-element.27.round_ref, f32[128,32,128]{2,1,0:T(8,128)} %get-tuple-element.28.slope0_ref, ...), custom_call_target="tpu_custom_call" | custom-call | tf_op jit(solution)/shard_map/pallas_call | solution.py:428
  138.9 3.5 %collective-permute-start.6 = (bf16[64,128]{1,0:T(8,128)(2,1)S(1)}, bf16[64,128]{1,0:T(8,128)(2,1)S(1)}, u32[]{:S(2)}, u32[]{:S(2)}) collective-permute-start(bf16[64,128]{1,0:T(8,128)(2,1)S(1)} %convert_element_type.193), channel_id=1, source_target_pairs={{0,1},{1,0},{2,3},{3,2},{4,5},{5,4},{6,7},{7,6},{8,9},{9,8},{10,11... | collective-permute-start | bytes 49160 | tf_op jit(solution)/shard_map/ppermute | solution.py:440
  142.4 2.4 %collective-permute-start.5 = (f32[64,64]{0,1:T(8,128)S(1)}, f32[64,64]{0,1:T(8,128)S(1)}, u32[]{:S(2)}, u32[]{:S(2)}) collective-permute-start(f32[64,64]{0,1:T(8,128)S(1)} %copy.30), channel_id=1, source_target_pairs={{0,0},{1,16},{2,32},{3,48},{4,64},{5,80},{6,96},{7,112},{8,128},{9... | collective-permute-start | bytes 49160 | tf_op jit(solution)/shard_map/ppermute | solution.py:435
  146.1 2.6 %collective-permute-start.11 = (bf16[64,128]{1,0:T(8,128)(2,1)S(1)}, bf16[64,128]{1,0:T(8,128)(2,1)S(1)}, u32[]{:S(2)}, u32[]{:S(2)}) collective-permute-start(bf16[64,128]{1,0:T(8,128)(2,1)S(1)} %add_convert_fusion.9), channel_id=1, source_target_pairs={{0,32},{16,48},{32,0},{48,16},{64,96},{80,112},{96,64},{112,80},{1... | collective-permute-start | bytes 49160 | tf_op jit(solution)/shard_map/ppermute | solution.py:440
  152.5 3.5 %collective-permute-done.15 = bf16[216,128]{1,0:T(8,128)(2,1)S(1)} collective-permute-done((bf16[216,128]{1,0:T(8,128)(2,1)S(1)}, bf16[216,128]{1,0:T(8,128)(2,1)S(1)}, u32[]{:S(2)}, u32[]{:S(2)}) %collective-permute-start.15) | collective-permute-done | bytes 55328 | tf_op jit(solution)/shard_map/ppermute | solution.py:440
  160.2 4.1 %collective-permute-start.17 = (bf16[216,128]{1,0:T(8,128)(2,1)S(1)}, bf16[216,128]{1,0:T(8,128)(2,1)S(1)}, u32[]{:S(2)}, u32[]{:S(2)}) collective-permute-start(bf16[216,128]{1,0:T(8,128)(2,1)S(1)} %add_convert_fusion.4), channel_id=1, source_target_pairs={{0,128},{16,144},{32,160},{48,176},{64,192},{80,208},{96,224},{112... | collective-permute-start | bytes 165896 | tf_op jit(solution)/shard_map/ppermute | solution.py:440
  164.3 3.4 %collective-permute-start.8 = (bf16[64,128]{1,0:T(8,128)(2,1)S(1)}, bf16[64,128]{1,0:T(8,128)(2,1)S(1)}, u32[]{:S(2)}, u32[]{:S(2)}) collective-permute-start(bf16[64,128]{1,0:T(8,128)(2,1)S(1)} %add_convert_fusion.11), channel_id=1, source_target_pairs={{0,4},{1,5},{2,6},{3,7},{4,0},{5,1},{6,2},{7,3},{8,12},{9,13},{10,... | collective-permute-start | bytes 49160 | tf_op jit(solution)/shard_map/ppermute | solution.py:440
  169.5 3.6 %collective-permute-start.13 = (bf16[64,128]{1,0:T(8,128)(2,1)S(1)}, bf16[64,128]{1,0:T(8,128)(2,1)S(1)}, u32[]{:S(2)}, u32[]{:S(2)}) collective-permute-start(bf16[64,128]{1,0:T(8,128)(2,1)S(1)} %add_convert_fusion.7), channel_id=1, source_target_pairs={{0,128},{16,144},{32,160},{48,176},{64,192},{80,208},{96,224},{112... | collective-permute-start | bytes 49160 | tf_op jit(solution)/shard_map/ppermute | solution.py:440
  175.3 4.3 %collective-permute-start.9 = (bf16[64,128]{1,0:T(8,128)(2,1)S(1)}, bf16[64,128]{1,0:T(8,128)(2,1)S(1)}, u32[]{:S(2)}, u32[]{:S(2)}) collective-permute-start(bf16[64,128]{1,0:T(8,128)(2,1)S(1)} %add_convert_fusion.10), channel_id=1, source_target_pairs={{0,8},{1,9},{2,10},{3,11},{4,12},{5,13},{6,14},{7,15},{8,0},{9,1},... | collective-permute-start | bytes 49160 | tf_op jit(solution)/shard_map/ppermute | solution.py:440
  179.7 2.8 %collective-permute-start.20 = (bf16[216,128]{1,0:T(8,128)(2,1)S(1)}, bf16[216,128]{1,0:T(8,128)(2,1)S(1)}, u32[]{:S(2)}, u32[]{:S(2)}) collective-permute-start(bf16[216,128]{1,0:T(8,128)(2,1)S(1)} %add_convert_fusion.1), channel_id=1, source_target_pairs={{0,4},{1,5},{2,6},{3,7},{4,0},{5,1},{6,2},{7,3},{8,12},{9,13},{10,... | collective-permute-start | bytes 165896 | tf_op jit(solution)/shard_map/ppermute | solution.py:440
  185.2 3.8 %collective-permute-start.21 = (bf16[216,128]{1,0:T(8,128)(2,1)S(1)}, bf16[216,128]{1,0:T(8,128)(2,1)S(1)}, u32[]{:S(2)}, u32[]{:S(2)}) collective-permute-start(bf16[216,128]{1,0:T(8,128)(2,1)S(1)} %add_convert_fusion), channel_id=1, source_target_pairs={{0,8},{1,9},{2,10},{3,11},{4,12},{5,13},{6,14},{7,15},{8,0},{9,1},... | collective-permute-start | bytes 165896 | tf_op jit(solution)/shard_map/ppermute | solution.py:440
  189.8 3.5 %collective-permute-done.21 = bf16[216,128]{1,0:T(8,128)(2,1)S(1)} collective-permute-done((bf16[216,128]{1,0:T(8,128)(2,1)S(1)}, bf16[216,128]{1,0:T(8,128)(2,1)S(1)}, u32[]{:S(2)}, u32[]{:S(2)}) %collective-permute-start.21) | collective-permute-done | bytes 55328 | tf_op jit(solution)/shard_map/ppermute | solution.py:440
  (98 shorter events, 34.8 us)
Async XLA Ops:
  3.0 9.9 %collective-permute-start = (bf16[17,32,128]{2,1,0:T(8,128)(2,1)}, bf16[17,32,128]{2,1,0:T(8,128)(2,1)S(1)}, u32[]{:S(2)}, u32[]{:S(2)}) collective-permute-start(bf16[17,32,128]{2,1,0:T(8,128)(2,1)} %get-tuple-element.21), channel_id=1, source_target_pairs={{0,1},{1,2},{2,3},{3,4},{4,5},{5,6},{6,7},{7,8},{8,9},{9,10},{10,1... | collective-permute-start | bytes 417800 | tf_op jit(solution)/shard_map/ppermute | solution.py:380
  7.9 8.7 %collective-permute-start.1 = (bf16[17,32,128]{2,1,0:T(8,128)(2,1)}, bf16[17,32,128]{2,1,0:T(8,128)(2,1)S(1)}, u32[]{:S(2)}, u32[]{:S(2)}) collective-permute-start(bf16[17,32,128]{2,1,0:T(8,128)(2,1)} %get-tuple-element.22), channel_id=1, source_target_pairs={{1,0},{2,1},{3,2},{4,3},{5,4},{6,5},{7,6},{8,7},{9,8},{10,9},{11,1... | collective-permute-start | bytes 417800 | tf_op jit(solution)/shard_map/ppermute | solution.py:381
  19.5 28.6 %collective-permute-start.2 = (bf16[34,32,128]{2,1,0:T(8,128)(2,1)}, bf16[34,32,128]{2,1,0:T(8,128)(2,1)S(1)}, u32[]{:S(2)}, u32[]{:S(2)}) collective-permute-start(bf16[34,32,128]{2,1,0:T(8,128)(2,1)} %get-tuple-element.23.part2_ref), channel_id=1, source_target_pairs={{0,16},{16,32},{32,48},{48,64},{64,80},{80,96},{96,112},{112,128},... | collective-permute-start | bytes 835592 | tf_op jit(solution)/shard_map/ppermute | solution.py:389
  25.9 30.3 %all-to-all-start = ((bf16[256,2,256]{2,1,0:T(2,128)(2,1)}), bf16[256,2,256]{2,1,0:T(2,128)(2,1)S(1)}, u32[]{:S(2)}, u32[]{:S(2)}) async-start(bf16[256,2,256]{2,1,0:T(2,128)(2,1)} %reshape.54), calls=%async_computation | async-start | bytes 524288 | tf_op jit(solution)/shard_map/all_to_all | solution.py:384
  44.3 7.6 %collective-permute-start.3 = (bf16[34,32,128]{2,1,0:T(8,128)(2,1)S(1)}, bf16[34,32,128]{2,1,0:T(8,128)(2,1)S(1)}, u32[]{:S(2)}, u32[]{:S(2)}) collective-permute-start(bf16[34,32,128]{2,1,0:T(8,128)(2,1)S(1)} %copy-done), channel_id=1, source_target_pairs={{16,0},{32,16},{48,32},{64,48},{80,64},{96,80},{112,96},{128,112},... | collective-permute-start | bytes 835592 | tf_op jit(solution)/shard_map/ppermute | solution.py:390
  51.9 16.3 %collective-permute-start.4 = (f32[128,128]{1,0:T(8,128)S(1)}, f32[128,128]{1,0:T(8,128)S(1)}, u32[]{:S(2)}, u32[]{:S(2)}) collective-permute-start(f32[128,128]{1,0:T(8,128)S(1)} %pad_maximum_fusion), channel_id=1, source_target_pairs={{0,0},{1,16},{2,32},{3,48},{4,64},{5,80},{6,96},{7,112},{8,128},{9... | collective-permute-start | bytes 196616 | tf_op jit(solution)/shard_map/ppermute | solution.py:401
  121.4 61.1 %copy-start.8 = (bf16[128,128]{1,0:T(8,128)(2,1)S(1)}, bf16[128,128]{1,0:T(8,128)(2,1)}, u32[]{:S(2)}) copy-start(bf16[128,128]{1,0:T(8,128)(2,1)} %w_right_ref.1) | copy-start | bytes 98308
  136.5 8.8 %collective-permute-start.10 = (bf16[64,128]{1,0:T(8,128)(2,1)S(1)}, bf16[64,128]{1,0:T(8,128)(2,1)S(1)}, u32[]{:S(2)}, u32[]{:S(2)}) collective-permute-start(bf16[64,128]{1,0:T(8,128)(2,1)S(1)} %convert_element_type.205), channel_id=1, source_target_pairs={{0,16},{16,0},{32,48},{48,32},{64,80},{80,64},{96,112},{112,96},{1... | collective-permute-start | bytes 49160 | tf_op jit(solution)/shard_map/ppermute | solution.py:440
  138.9 9.8 %collective-permute-start.6 = (bf16[64,128]{1,0:T(8,128)(2,1)S(1)}, bf16[64,128]{1,0:T(8,128)(2,1)S(1)}, u32[]{:S(2)}, u32[]{:S(2)}) collective-permute-start(bf16[64,128]{1,0:T(8,128)(2,1)S(1)} %convert_element_type.193), channel_id=1, source_target_pairs={{0,1},{1,0},{2,3},{3,2},{4,5},{5,4},{6,7},{7,6},{8,9},{9,8},{10,11... | collective-permute-start | bytes 49160 | tf_op jit(solution)/shard_map/ppermute | solution.py:440
  142.4 9.4 %collective-permute-start.5 = (f32[64,64]{0,1:T(8,128)S(1)}, f32[64,64]{0,1:T(8,128)S(1)}, u32[]{:S(2)}, u32[]{:S(2)}) collective-permute-start(f32[64,64]{0,1:T(8,128)S(1)} %copy.30), channel_id=1, source_target_pairs={{0,0},{1,16},{2,32},{3,48},{4,64},{5,80},{6,96},{7,112},{8,128},{9... | collective-permute-start | bytes 49160 | tf_op jit(solution)/shard_map/ppermute | solution.py:435
  145.0 6.5 %collective-permute-start.14 = (bf16[216,128]{1,0:T(8,128)(2,1)S(1)}, bf16[216,128]{1,0:T(8,128)(2,1)S(1)}, u32[]{:S(2)}, u32[]{:S(2)}) collective-permute-start(bf16[216,128]{1,0:T(8,128)(2,1)S(1)} %convert_element_type.218), channel_id=1, source_target_pairs={{0,16},{16,0},{32,48},{48,32},{64,80},{80,64},{96,112},{112,96},{1... | collective-permute-start | bytes 165896 | tf_op jit(solution)/shard_map/ppermute | solution.py:440
  146.1 10.0 %collective-permute-start.11 = (bf16[64,128]{1,0:T(8,128)(2,1)S(1)}, bf16[64,128]{1,0:T(8,128)(2,1)S(1)}, u32[]{:S(2)}, u32[]{:S(2)}) collective-permute-start(bf16[64,128]{1,0:T(8,128)(2,1)S(1)} %add_convert_fusion.9), channel_id=1, source_target_pairs={{0,32},{16,48},{32,0},{48,16},{64,96},{80,112},{96,64},{112,80},{1... | collective-permute-start | bytes 49160 | tf_op jit(solution)/shard_map/ppermute | solution.py:440
  149.4 14.9 %collective-permute-start.7 = (bf16[64,128]{1,0:T(8,128)(2,1)S(1)}, bf16[64,128]{1,0:T(8,128)(2,1)S(1)}, u32[]{:S(2)}, u32[]{:S(2)}) collective-permute-start(bf16[64,128]{1,0:T(8,128)(2,1)S(1)} %add_convert_fusion.12), channel_id=1, source_target_pairs={{0,2},{1,3},{2,0},{3,1},{4,6},{5,7},{6,4},{7,5},{8,10},{9,11},{10,... | collective-permute-start | bytes 49160 | tf_op jit(solution)/shard_map/ppermute | solution.py:440
  151.5 4.4 %collective-permute-start.15 = (bf16[216,128]{1,0:T(8,128)(2,1)S(1)}, bf16[216,128]{1,0:T(8,128)(2,1)S(1)}, u32[]{:S(2)}, u32[]{:S(2)}) collective-permute-start(bf16[216,128]{1,0:T(8,128)(2,1)S(1)} %add_convert_fusion.6), channel_id=1, source_target_pairs={{0,32},{16,48},{32,0},{48,16},{64,96},{80,112},{96,64},{112,80},{1... | collective-permute-start | bytes 165896 | tf_op jit(solution)/shard_map/ppermute | solution.py:440
  156.0 4.2 %collective-permute-start.16 = (bf16[216,128]{1,0:T(8,128)(2,1)S(1)}, bf16[216,128]{1,0:T(8,128)(2,1)S(1)}, u32[]{:S(2)}, u32[]{:S(2)}) collective-permute-start(bf16[216,128]{1,0:T(8,128)(2,1)S(1)} %add_convert_fusion.5), channel_id=1, source_target_pairs={{0,64},{16,80},{32,96},{48,112},{64,0},{80,16},{96,32},{112,48},{1... | collective-permute-start | bytes 165896 | tf_op jit(solution)/shard_map/ppermute | solution.py:440
  156.1 13.4 %collective-permute-start.12 = (bf16[64,128]{1,0:T(8,128)(2,1)S(1)}, bf16[64,128]{1,0:T(8,128)(2,1)S(1)}, u32[]{:S(2)}, u32[]{:S(2)}) collective-permute-start(bf16[64,128]{1,0:T(8,128)(2,1)S(1)} %add_convert_fusion.8), channel_id=1, source_target_pairs={{0,64},{16,80},{32,96},{48,112},{64,0},{80,16},{96,32},{112,48},{1... | collective-permute-start | bytes 49160 | tf_op jit(solution)/shard_map/ppermute | solution.py:440
  160.2 7.4 %collective-permute-start.17 = (bf16[216,128]{1,0:T(8,128)(2,1)S(1)}, bf16[216,128]{1,0:T(8,128)(2,1)S(1)}, u32[]{:S(2)}, u32[]{:S(2)}) collective-permute-start(bf16[216,128]{1,0:T(8,128)(2,1)S(1)} %add_convert_fusion.4), channel_id=1, source_target_pairs={{0,128},{16,144},{32,160},{48,176},{64,192},{80,208},{96,224},{112... | collective-permute-start | bytes 165896 | tf_op jit(solution)/shard_map/ppermute | solution.py:440
  164.3 11.0 %collective-permute-start.8 = (bf16[64,128]{1,0:T(8,128)(2,1)S(1)}, bf16[64,128]{1,0:T(8,128)(2,1)S(1)}, u32[]{:S(2)}, u32[]{:S(2)}) collective-permute-start(bf16[64,128]{1,0:T(8,128)(2,1)S(1)} %add_convert_fusion.11), channel_id=1, source_target_pairs={{0,4},{1,5},{2,6},{3,7},{4,0},{5,1},{6,2},{7,3},{8,12},{9,13},{10,... | collective-permute-start | bytes 49160 | tf_op jit(solution)/shard_map/ppermute | solution.py:440
  167.7 5.7 %collective-permute-start.18 = (bf16[216,128]{1,0:T(8,128)(2,1)S(1)}, bf16[216,128]{1,0:T(8,128)(2,1)S(1)}, u32[]{:S(2)}, u32[]{:S(2)}) collective-permute-start(bf16[216,128]{1,0:T(8,128)(2,1)S(1)} %add_convert_fusion.3), channel_id=1, source_target_pairs={{0,1},{1,0},{2,3},{3,2},{4,5},{5,4},{6,7},{7,6},{8,9},{9,8},{10,11... | collective-permute-start | bytes 165896 | tf_op jit(solution)/shard_map/ppermute | solution.py:440
  169.5 13.0 %collective-permute-start.13 = (bf16[64,128]{1,0:T(8,128)(2,1)S(1)}, bf16[64,128]{1,0:T(8,128)(2,1)S(1)}, u32[]{:S(2)}, u32[]{:S(2)}) collective-permute-start(bf16[64,128]{1,0:T(8,128)(2,1)S(1)} %add_convert_fusion.7), channel_id=1, source_target_pairs={{0,128},{16,144},{32,160},{48,176},{64,192},{80,208},{96,224},{112... | collective-permute-start | bytes 49160 | tf_op jit(solution)/shard_map/ppermute | solution.py:440
  173.5 6.2 %collective-permute-start.19 = (bf16[216,128]{1,0:T(8,128)(2,1)S(1)}, bf16[216,128]{1,0:T(8,128)(2,1)S(1)}, u32[]{:S(2)}, u32[]{:S(2)}) collective-permute-start(bf16[216,128]{1,0:T(8,128)(2,1)S(1)} %add_convert_fusion.2), channel_id=1, source_target_pairs={{0,2},{1,3},{2,0},{3,1},{4,6},{5,7},{6,4},{7,5},{8,10},{9,11},{10,... | collective-permute-start | bytes 165896 | tf_op jit(solution)/shard_map/ppermute | solution.py:440
  175.3 13.7 %collective-permute-start.9 = (bf16[64,128]{1,0:T(8,128)(2,1)S(1)}, bf16[64,128]{1,0:T(8,128)(2,1)S(1)}, u32[]{:S(2)}, u32[]{:S(2)}) collective-permute-start(bf16[64,128]{1,0:T(8,128)(2,1)S(1)} %add_convert_fusion.10), channel_id=1, source_target_pairs={{0,8},{1,9},{2,10},{3,11},{4,12},{5,13},{6,14},{7,15},{8,0},{9,1},... | collective-permute-start | bytes 49160 | tf_op jit(solution)/shard_map/ppermute | solution.py:440
  179.7 5.5 %collective-permute-start.20 = (bf16[216,128]{1,0:T(8,128)(2,1)S(1)}, bf16[216,128]{1,0:T(8,128)(2,1)S(1)}, u32[]{:S(2)}, u32[]{:S(2)}) collective-permute-start(bf16[216,128]{1,0:T(8,128)(2,1)S(1)} %add_convert_fusion.1), channel_id=1, source_target_pairs={{0,4},{1,5},{2,6},{3,7},{4,0},{5,1},{6,2},{7,3},{8,12},{9,13},{10,... | collective-permute-start | bytes 165896 | tf_op jit(solution)/shard_map/ppermute | solution.py:440
  185.2 8.2 %collective-permute-start.21 = (bf16[216,128]{1,0:T(8,128)(2,1)S(1)}, bf16[216,128]{1,0:T(8,128)(2,1)S(1)}, u32[]{:S(2)}, u32[]{:S(2)}) collective-permute-start(bf16[216,128]{1,0:T(8,128)(2,1)S(1)} %add_convert_fusion), channel_id=1, source_target_pairs={{0,8},{1,9},{2,10},{3,11},{4,12},{5,13},{6,14},{7,15},{8,0},{9,1},... | collective-permute-start | bytes 165896 | tf_op jit(solution)/shard_map/ppermute | solution.py:440
  (12 other events, 261.7 us)

commit v2 on v1

--- a/solution.py
+++ b/solution.py
@@ -13,6 +13,7 @@
 HALO = 32
 WIDE = TILE + 2 * HALO
 CH = 32
+ROWS = 16
 VMEM = pl.BlockSpec(memory_space=pltpu.VMEM)
 SMEM = pl.BlockSpec(memory_space=pltpu.SMEM)
 
@@ -81,7 +82,7 @@
             ).astype(BF16)
 
 
-def mixed_kernel(place_ref, feat_ref, w_left_ref, w_right_ref, w_in_ref, mixed_ref, rows_ref, cols_ref):
+def mixed_kernel(place_ref, feat_ref, w_left_ref, w_right_ref, w_in_ref, mixed_ref, rows_ref, cols_ref, picked_ref):
     row = place_ref[0]
     col = place_ref[1]
     row_chunks = [jnp.maximum(2 * row - 1, 0), 2 * row, 2 * row + 1, jnp.minimum(2 * row + 2, 31)]
@@ -90,30 +91,28 @@
         (row_chunks, w_left_ref, rows_ref),
         (col_chunks, w_right_ref, cols_ref),
     ):
-        picked = jnp.concatenate([feat_ref[chunk] for chunk in chunks], axis=0)
-        out_ref[...] = jnp.dot(picked, weight_ref[...], preferred_element_type=F32)
+        for n, chunk in enumerate(chunks):
+            for m in range(8):
+                at = HALO * n + 4 * m
+                picked_ref[at : at + 4, :] = feat_ref[8 * chunk + m].astype(F32)
+        out_ref[...] = jnp.dot(
+            picked_ref[...].astype(BF16), weight_ref[...], preferred_element_type=F32
+        )
     w_in = w_in_ref[...]
 
     def body(step, carry):
-        for k in range(2):
-            pair = []
-            for i in range(2):
-                outer = rows_ref[pl.ds(4 * step + 2 * k + i, 1), :] + cols_ref[...]
-                pair.append(gelu(outer).astype(BF16))
+        cols = cols_ref[...]
+        rows = rows_ref[pl.ds(ROWS * step, ROWS), :]
+        for k in range(0, ROWS, 2):
+            pair = [gelu(rows[k + i : k + i + 1, :] + cols).astype(BF16) for i in range(2)]
             out = lax.dot_general(
                 w_in, jnp.concatenate(pair, 0), (((1,), (1,)), ((), ())), preferred_element_type=F32
             )
             for i in range(2):
-                mixed_ref[4 * step + 2 * k + i] = out[:, WIDE * i : WIDE * i + WIDE]
+                mixed_ref[ROWS * step + k + i] = out[:, WIDE * i : WIDE * i + WIDE]
         return carry
 
-    lax.fori_loop(0, WIDE // 4, body, 0)
-
-
-def shifted(value, rate):
-    return jnp.concatenate(
-        [pltpu.roll(value, rate, 1), value, pltpu.roll(value, WIDE - rate, 1)], axis=0
-    ).astype(BF16)
+    lax.fori_loop(0, WIDE // ROWS, body, 0)
 
 
 def lane_mask(col):
@@ -122,24 +121,45 @@
     return jnp.where((bin_at >= 0) & (bin_at < 1024), 1.0, 0.0).astype(F32)
 
 
-def row_valid(row, i):
-    at = TILE * row - HALO + i
-    return jnp.where((at >= 0) & (at < 1024), 1.0, 0.0).astype(F32)
-
-
-def gather_taps(z_ref, i, rate):
-    return z_ref[i - rate, 0:CH, :] + z_ref[i, CH : 2 * CH, :] + z_ref[i + rate, 2 * CH : 3 * CH, :]
-
-
-def rows_loop(first, last, one, many):
+def many_taps(z_ref, base, rows, rate):
+    return (
+        z_ref[pl.ds(base - rate, rows), 0:CH, :]
+        + z_ref[pl.ds(base, rows), CH : 2 * CH, :]
+        + z_ref[pl.ds(base + rate, rows), 2 * CH : 3 * CH, :]
+    )
+
+
+def shifted_rows(value, rate):
+    return jnp.concatenate(
+        [pltpu.roll(value, rate, 2), value, pltpu.roll(value, WIDE - rate, 2)], axis=1
+    ).astype(BF16)
+
+
+def rows_mask(inside, row, base, rows):
+    at = TILE * row - HALO + base + lax.broadcasted_iota(jnp.int32, (rows, 1, 1), 0)
+    return jnp.where((at >= 0) & (at < 1024), 1.0, 0.0).astype(F32) * inside[None]
+
+
+def multiply(weight, patch_ref, z_ref, base, rows):
+    for k in range(rows // 2):
+        i = base + 2 * k
+        pair = jnp.concatenate([patch_ref[i], patch_ref[i + 1]], axis=1)
+        z = jnp.dot(weight, pair, preferred_element_type=F32)
+        z_ref[i] = z[:, :WIDE]
+        z_ref[i + 1] = z[:, WIDE:]
+
+
+def pipelined(first, last, rows, make, use):
+    make(first)
+
     def body(step, carry):
-        base = first + 4 * step
-        for k in range(2):
-            i = base + 2 * k
-            many(i, jnp.concatenate([one(i), one(i + 1)], axis=1))
+        base = first + rows * step
+        use(base - rows)
+        make(base)
         return carry
 
-    lax.fori_loop(0, (last - first) // 4, body, 0)
+    lax.fori_loop(1, (last - first) // rows, body, 0)
+    use(last - rows)
 
 
 def main_kernel(
@@ -167,6 +187,7 @@
     patch1_ref,
     patch2_ref,
     masked_ref,
+    patchb_ref,
     upstream_ref,
     grad2_ref,
 ):
@@ -188,44 +209,36 @@
 
         lax.fori_loop(0, HALO, start, 0, unroll=4)
 
-    def activate(layer, i, state):
-        act, slope = gelu_pair(state)
-        if layer == 0:
-            slope0_ref[i] = slope
-        else:
-            (slope1_ref, slope2_ref)[layer - 1][i] = slope
-        return shifted(act * (inside * row_valid(row, i)), rates[layer])
-
     for layer in range(3):
         z_now = z_refs[layer % 2]
         z_last = z_refs[(layer + 1) % 2]
-
-        def one(i, layer=layer, z_last=z_last):
-            if layer == 0:
-                state = state_ref[i].astype(F32)
-            else:
-                new = state_ref[i].astype(F32) + gather_taps(z_last, i, rates[layer - 1])
-                new = new.astype(BF16)
-                state_ref[i] = new
+        slope_ref = (slope0_ref, slope1_ref, slope2_ref)[layer]
+
+        def make(base, layer=layer, z_last=z_last, slope_ref=slope_ref):
+            block = pl.ds(base, ROWS)
+            state = state_ref[block].astype(F32)
+            if layer > 0:
+                new = (state + many_taps(z_last, base, ROWS, rates[layer - 1])).astype(BF16)
+                state_ref[block] = new
                 state = new.astype(F32)
-            out = activate(layer, i, state)
-            patch_refs[layer][i] = out
-            return out
-
-        def many(i, pair, layer=layer, z_now=z_now):
-            z = jnp.dot(forward_ref[layer], pair, preferred_element_type=F32)
-            z_now[i] = z[:, :WIDE]
-            z_now[i + 1] = z[:, WIDE:]
-
-        rows_loop(8 * layer, WIDE - 8 * layer, one, many)
-
-    def finish(i, carry):
-        new = state_ref[i].astype(F32) + gather_taps(za_ref, i, rates[2])
+            act, slope = gelu_pair(state)
+            slope_ref[block] = slope
+            act = act * rows_mask(inside, row, base, ROWS)
+            patch_refs[layer][block] = shifted_rows(act, rates[layer])
+
+        def use(base, layer=layer, z_now=z_now):
+            multiply(forward_ref[layer], patch_refs[layer], z_now, base, ROWS)
+
+        pipelined(8 * layer, WIDE - 8 * layer, ROWS, make, use)
+
+    def finish(step, carry):
+        base = HALO + ROWS * step
+        new = state_ref[pl.ds(base, ROWS)].astype(F32) + many_taps(za_ref, base, ROWS, rates[2])
         new = new.astype(BF16).astype(F32)
-        direct_ref[pl.ds(i - HALO, 1), :] = jnp.sum(new * w_out, axis=0, keepdims=True)[:, :TILE]
+        direct_ref[pl.ds(base - HALO, ROWS), :] = jnp.sum(new * w_out[None], axis=1)[:, :TILE]
         return carry
 
-    lax.fori_loop(HALO, HALO + TILE, finish, 0, unroll=4)
+    lax.fori_loop(0, TILE // ROWS, finish, 0)
 
     other = mirror_ref[...].T
     other = jnp.concatenate([other[96:128], other[0:96]], axis=0)
@@ -240,63 +253,68 @@
     masked_ref[...] = jnp.zeros_like(masked_ref)
 
     def weight_terms(layer):
-        def keep(i, carry):
-            masked_ref[i] = (round_ref[i].astype(F32) * tile_lanes).astype(BF16)
+        def keep(step, carry):
+            block = pl.ds(HALO + 8 * step, 8)
+            masked_ref[block] = (round_ref[block].astype(F32) * tile_lanes[None]).astype(BF16)
             return carry
 
-        lax.fori_loop(HALO, HALO + TILE, keep, 0, unroll=4)
+        lax.fori_loop(0, TILE // 8, keep, 0)
         rate = rates[layer]
 
         def body(step, total):
-            base = 24 + 4 * step
-            left = jnp.concatenate(
-                [
-                    jnp.concatenate([masked_ref[base + k + off] for k in range(4)], axis=1)
-                    for off in (rate, 0, -rate)
-                ],
-                axis=0,
-            )
-            right = jnp.concatenate([patch_refs[layer][base + k] for k in range(4)], axis=1)
-            return total + lax.dot_general(
-                left, right, (((1,), (1,)), ((), ())), preferred_element_type=F32
-            )
-
-        terms_ref[layer] = lax.fori_loop(0, 20, body, jnp.zeros((96, 96), F32))
+            base = 24 + 8 * step
+            for part in range(2):
+                at = base + 4 * part
+                left = jnp.concatenate(
+                    [
+                        jnp.concatenate([masked_ref[at + k + off] for k in range(4)], axis=1)
+                        for off in (rate, 0, -rate)
+                    ],
+                    axis=0,
+                )
+                right = jnp.concatenate([patch_refs[layer][at + k] for k in range(4)], axis=1)
+                total = total + lax.dot_general(
+                    left, right, (((1,), (1,)), ((), ())), preferred_element_type=F32
+                )
+            return total
+
+        terms_ref[layer] = lax.fori_loop(0, 10, body, jnp.zeros((96, 96), F32))
 
     def back(layer, first, last, one_grad, z_now):
-        def one(i):
-            rounded = one_grad(i).astype(BF16)
-            round_ref[i] = rounded
-            return shifted(rounded.astype(F32), rates[layer])
-
-        def many(i, pair):
-            z = jnp.dot(backward_ref[layer], pair, preferred_element_type=F32)
-            z_now[i] = z[:, :WIDE]
-            z_now[i + 1] = z[:, WIDE:]
-
-        rows_loop(first, last, one, many)
+        def make(base):
+            rounded = one_grad(base).astype(BF16)
+            round_ref[pl.ds(base, ROWS)] = rounded
+            patchb_ref[pl.ds(base, ROWS)] = shifted_rows(rounded.astype(F32), rates[layer])
+
+        def use(base):
+            multiply(backward_ref[layer], patchb_ref, z_now, base, ROWS)
+
+        pipelined(first, last, ROWS, make, use)
         weight_terms(layer)
 
-    def first_grad(i):
-        return upstream_ref[pl.ds(i, 1), :] * w_out
-
-    def second_grad(i):
-        new = first_grad(i) + gather_taps(zb_ref, i, rates[2]) * slope2_ref[i]
-        new = new * (inside * row_valid(row, i))
-        grad2_ref[i] = new
+    def first_grad(base):
+        return upstream_ref[pl.ds(base, ROWS), :][:, None, :] * w_out[None]
+
+    def second_grad(base):
+        block = pl.ds(base, ROWS)
+        new = first_grad(base) + many_taps(zb_ref, base, ROWS, rates[2]) * slope2_ref[block]
+        new = new * rows_mask(inside, row, base, ROWS)
+        grad2_ref[block] = new
         return new
 
     back(2, 8, 120, first_grad, zb_ref)
     back(1, 16, 112, second_grad, za_ref)
 
-    def third_grad(i, carry):
-        new = grad2_ref[i] + gather_taps(za_ref, i, rates[1]) * slope1_ref[i]
-        new = new * (inside * row_valid(row, i))
-        grad_ref[i] = new
-        round_ref[i] = new.astype(BF16)
+    def third_grad(step, carry):
+        base = 24 + ROWS * step
+        block = pl.ds(base, ROWS)
+        new = grad2_ref[block] + many_taps(za_ref, base, ROWS, rates[1]) * slope1_ref[block]
+        new = new * rows_mask(inside, row, base, ROWS)
+        grad_ref[block] = new
+        round_ref[block] = new.astype(BF16)
         return carry
 
-    lax.fori_loop(24, 104, third_grad, 0, unroll=4)
+    lax.fori_loop(0, 80 // ROWS, third_grad, 0)
     weight_terms(0)
 
 
@@ -312,49 +330,56 @@
     row_ref,
     col_ref,
     z_ref,
+    patch_ref,
 ):
     rate = place_ref[2]
 
-    def one(i):
-        return shifted(round_ref[i].astype(F32), rate)
-
-    def many(i, pair):
-        z = jnp.dot(backward_ref[0], pair, preferred_element_type=F32)
-        z_ref[i] = z[:, :WIDE]
-        z_ref[i + 1] = z[:, WIDE:]
-
-    rows_loop(24, 104, one, many)
+    def make(base):
+        patch_ref[pl.ds(base, ROWS)] = shifted_rows(round_ref[pl.ds(base, ROWS)].astype(F32), rate)
+
+    def use(base):
+        multiply(backward_ref[0], patch_ref, z_ref, base, ROWS)
+
+    pipelined(24, 104, ROWS, make, use)
     w_in = w_in_ref[...]
     cols = cols_ref[0:TILE, :]
 
     def body(step, total):
-        for k in range(2):
-            i = HALO + 2 * step + k
-            start = grad_ref[i] + gather_taps(z_ref, i, rate) * slope0_ref[i]
+        base = HALO + ROWS * step
+        block = pl.ds(base, ROWS)
+        start = grad_ref[block] + many_taps(z_ref, base, ROWS, rate) * slope0_ref[block]
+        start = start[:, :, :TILE].astype(BF16)
+        rows = rows_ref[block, :]
+        sums = []
+        for k in range(ROWS):
             hidden = lax.dot_general(
-                start[:, :TILE].astype(BF16), w_in, (((0,), (0,)), ((), ())), preferred_element_type=F32
+                start[k], w_in, (((0,), (0,)), ((), ())), preferred_element_type=F32
             )
-            slope = gelu_pair(rows_ref[pl.ds(i, 1), :] + cols)[1]
-            outer = hidden * slope
-            row_ref[pl.ds(i - HALO, 1), :] = jnp.sum(outer, axis=0, keepdims=True)
+            outer = hidden * gelu_pair(rows[k : k + 1, :] + cols)[1]
+            sums.append(jnp.sum(outer, axis=0, keepdims=True))
             total = total + outer
+        row_ref[pl.ds(base - HALO, ROWS), :] = jnp.concatenate(sums, axis=0).astype(BF16)
         return total
 
-    col_ref[...] = lax.fori_loop(0, TILE // 2, body, jnp.zeros((TILE, 128), F32))
+    total = lax.fori_loop(0, TILE // ROWS, body, jnp.zeros((TILE, 128), F32))
+    col_ref[...] = total.astype(BF16)
 
 
 def shape(*dims, dtype=F32):
     return jax.ShapeDtypeStruct(dims, dtype)
 
 
-def call(kernel, outs, specs, scratch=()):
+def call(kernel, outs, specs, scratch=(), mib=8, cost=1):
     return pl.pallas_call(
         kernel,
         out_shape=outs,
         in_specs=specs,
         out_specs=[VMEM] * len(outs),
         scratch_shapes=list(scratch),
-        compiler_params=pltpu.CompilerParams(vmem_limit_bytes=56 * 2**20),
+        compiler_params=pltpu.CompilerParams(vmem_limit_bytes=mib * 2**20),
+        cost_estimate=pl.CostEstimate(
+            flops=cost * 10**9, bytes_accessed=cost * 3 * 10**6, transcendentals=0
+        ),
     )
 
 
@@ -380,8 +405,9 @@
     from_left = lax.ppermute(right_edge, "col", up)
     from_right = lax.ppermute(left_edge, "col", down)
 
-    sent = jnp.broadcast_to(features.reshape(1, 1, 512), (n_row * n_col, 1, 512))
-    gathered = lax.all_to_all(sent, ("row", "col"), 0, 0).reshape(32, 32, 128)
+    sent = jnp.broadcast_to(features[None], (n_row * n_col,) + features.shape)
+    gathered = lax.all_to_all(sent, ("row", "col"), 0, 0)
+    from_left, from_right, gathered = lax.optimization_barrier((from_left, from_right, gathered))
 
     upper, lower = call(
         widen_kernel, [shape(HALO + 2, CH, WIDE, dtype=BF16)] * 2, [VMEM] * 4
@@ -393,6 +419,9 @@
         mixed_kernel,
         [shape(WIDE, CH, WIDE), shape(WIDE, 128), shape(WIDE, 128)],
         [SMEM] + [VMEM] * 4,
+        [pltpu.VMEM((WIDE, 128), F32)],
+        16,
+        6,
     )(place, gathered, w_left, w_right, w_in)
 
     wide_cot = jnp.concatenate(
@@ -420,35 +449,50 @@
             pltpu.VMEM((WIDE, 96, WIDE), BF16),
             pltpu.VMEM((WIDE, 96, WIDE), BF16),
             pltpu.VMEM(big, BF16),
+            pltpu.VMEM((WIDE, 96, WIDE), BF16),
             pltpu.VMEM((WIDE, WIDE), F32),
             pltpu.VMEM(big, F32),
         ],
+        40,
+        24,
     )(place, mixed, above, upper, lower, below, mirrored, forward_w, backward_w, w_out_wide)
+
+    def summed(value, axis, bit):
+        other = lax.ppermute(value, axis, flips(axis, bit))
+        return (value.astype(F32) + other.astype(F32)).astype(BF16)
+
+    direct_other = lax.ppermute(direct, ("row", "col"), swap)
+    packed = summed(terms.astype(BF16).reshape(216, 128), "row", 1)
+    grad, packed = lax.optimization_barrier((grad, packed))
+    packed = summed(packed, "row", 2)
 
     row_part, col_part = call(
         last_kernel,
-        [shape(TILE, 128), shape(TILE, 128)],
+        [shape(TILE, 128, dtype=BF16), shape(TILE, 128, dtype=BF16)],
         [SMEM] + [VMEM] * 7,
-        [pltpu.VMEM((WIDE, 96, WIDE), F32)],
+        [pltpu.VMEM((WIDE, 96, WIDE), F32), pltpu.VMEM((WIDE, 96, WIDE), BF16)],
+        24,
+        7,
     )(place, grad, rounded, slope0, row_project, col_project, backward_w, w_in)
 
-    other = lax.ppermute(direct, ("row", "col"), swap)
-    logits = 0.5 * (direct + other.T)
-
-    def summed(value, axis, bit):
-        value = value.astype(BF16)
-        return value.astype(F32) + lax.ppermute(value, axis, flips(axis, bit)).astype(F32)
-
-    packed = terms.reshape(216, 128)
-    for bit in (1, 2, 4, 8):
+    logits = 0.5 * (direct + direct_other.T)
+    packed = jnp.concatenate([col_part, packed], axis=0)
+    for bit in (4, 8):
         packed = summed(packed, "row", bit)
-        row_part = summed(row_part, "col", bit)
+    col_part = packed[:TILE]
+    packed = jnp.concatenate([row_part, packed[TILE:]], axis=0)
+    for bit in (1, 2):
+        packed = summed(packed, "col", bit)
         col_part = summed(col_part, "row", bit)
-    for bit in (1, 2, 4, 8):
+    for bit in (4, 8):
         packed = summed(packed, "col", bit)
+    row_part = packed[:TILE]
     conv_grads = (
-        packed.reshape(3, 3, CH, 96).transpose(0, 2, 1, 3).reshape(3, CH, 288) / (TILE * n_row)
+        packed[TILE:].reshape(3, 3, CH, 96).transpose(0, 2, 1, 3).reshape(3, CH, 288).astype(F32)
+        / (TILE * n_row)
     )
+    row_part = row_part.astype(F32)
+    col_part = col_part.astype(F32)
     grad_rows = jnp.dot(row_part, w_left.astype(F32).T, precision=lax.Precision.HIGHEST)
     grad_cols = jnp.dot(col_part, w_right.astype(F32).T, precision=lax.Precision.HIGHEST)
     return (logits, grad_rows, grad_cols, conv_grads)

time: 198 us -> 140 us (0.71)
  the two profiles are of different devices: /device:TPU:40 before, /device:TPU:4 now
where the time goes in v2:
time: 140 us; the launch traced here: 139 us
  starting transfers between devices  69.1 us (49%)
  Pallas kernels  29.8 us (21%)
  waiting for transfers between devices  25.7 us (18%)
  local copies, waits for them, and re-layouts  11.1 us (8%)
  matrix products  1.53 us (1%)
    ppermute x10, starting transfers between devices, summed(): other = lax.ppermute(value, axis, flips(axis, bit))  36.3 us
    pallas_call x1, Pallas kernels, on_device(): call(main_kernel, [shape(TILE, TILE), shape(3, 96, 96), shape(*big), shap...  20.6 us
    ppermute x10, waiting for transfers between devices, summed(): other = lax.ppermute(value, axis, flips(axis, bit))  15.2 us
    all_to_all x1, starting transfers between devices, on_device(): gathered = lax.all_to_all(sent, ('row', 'col'), 0, 0)  14.7 us
    unnamed x26, local copies, waits for them, and re-layouts  6.97 us
    ppermute x1, starting transfers between devices, on_device(): mirrored = lax.ppermute(wide_cot, ('row', 'col'), swap)  5.99 us
    pallas_call x1, Pallas kernels, on_device(): call(mixed_kernel, [shape(WIDE, CH, WIDE), shape(WIDE, 128), shape(WIDE,...  4.44 us
    ppermute x1, waiting for transfers between devices, on_device(): below = lax.ppermute(upper, 'row', down)  4.42 us
  transfers between devices with their start and end apart: 17, of which 11 were waited for; matrix products, arithmetic and copies ran while one was open for 2% of the time, Pallas kernels for 6%

profile of v2, /device:TPU:4, one launch (start us, length us, event | category | flops | bytes accessed | tf_op | source)
XLA Modules:
  0.0 139.2 jit_solution(8462468803589197274)
XLA Ops:
  2.1 14.7 %all-to-all-start = ((bf16[256,4,128]{2,1,0:T(4,128)(2,1)}), bf16[256,4,128]{2,1,0:T(4,128)(2,1)S(1)}, u32[]{:S(2)}, u32[]{:S(2)}) async-start(bf16[256,4,128]{2,1,0:T(4,128)(2,1)} %broadcast_in_dim.4), calls=%async_computation | async-start | bytes 524288 | tf_op jit(solution)/shard_map/all_to_all | solution.py:409
  19.1 3.6 %collective-permute-start = (bf16[17,32,128]{2,1,0:T(8,128)(2,1)S(1)}, bf16[17,32,128]{2,1,0:T(8,128)(2,1)S(1)}, u32[]{:S(2)}, u32[]{:S(2)}) collective-permute-start(bf16[17,32,128]{2,1,0:T(8,128)(2,1)S(1)} %get-tuple-element.24), channel_id=1, source_target_pairs={{0,1},{1,2},{2,3},{3,4},{4,5},{5,6},{6,7},{7,8},{8,9},{9,10},{10,1... | collective-permute-start | bytes 417800 | tf_op jit(solution)/shard_map/ppermute | solution.py:405
  22.7 3.9 %collective-permute-start.1 = (bf16[17,32,128]{2,1,0:T(8,128)(2,1)S(1)}, bf16[17,32,128]{2,1,0:T(8,128)(2,1)S(1)}, u32[]{:S(2)}, u32[]{:S(2)}) collective-permute-start(bf16[17,32,128]{2,1,0:T(8,128)(2,1)S(1)} %get-tuple-element.25), channel_id=1, source_target_pairs={{1,0},{2,1},{3,2},{4,3},{5,4},{6,5},{7,6},{8,7},{9,8},{10,9},{11,1... | collective-permute-start | bytes 417800 | tf_op jit(solution)/shard_map/ppermute | solution.py:406
  26.6 2.1 %collective-permute-done.from_left_ref = bf16[17,32,128]{2,1,0:T(8,128)(2,1)S(1)} collective-permute-done((bf16[17,32,128]{2,1,0:T(8,128)(2,1)S(1)}, bf16[17,32,128]{2,1,0:T(8,128)(2,1)S(1)}, u32[]{:S(2)}, u32[]{:S(2)}) %collective-permute-start) | collective-permute-done | bytes 139296 | tf_op jit(solution)/shard_map/ppermute | solution.py:405
  28.7 3.8 %collective-permute-done.1.from_right_ref = bf16[17,32,128]{2,1,0:T(8,128)(2,1)S(1)} collective-permute-done((bf16[17,32,128]{2,1,0:T(8,128)(2,1)S(1)}, bf16[17,32,128]{2,1,0:T(8,128)(2,1)S(1)}, u32[]{:S(2)}, u32[]{:S(2)}) %collective-permute-start.1) | collective-permute-done | bytes 139296 | tf_op jit(solution)/shard_map/ppermute | solution.py:406
  37.1 4.4 %collective-permute-done.3.part3_ref = bf16[34,32,128]{2,1,0:T(8,128)(2,1)S(1)} collective-permute-done((bf16[34,32,128]{2,1,0:T(8,128)(2,1)S(1)}, bf16[34,32,128]{2,1,0:T(8,128)(2,1)S(1)}, u32[]{:S(2)}, u32[]{:S(2)}) %collective-permute-start.3) | collective-permute-done | bytes 278560 | tf_op jit(solution)/shard_map/ppermute | solution.py:416
  41.6 6.0 %collective-permute-start.4 = (f32[128,128]{1,0:T(8,128)S(1)}, f32[128,128]{1,0:T(8,128)S(1)}, u32[]{:S(2)}, u32[]{:S(2)}) collective-permute-start(f32[128,128]{1,0:T(8,128)S(1)} %pad_maximum_fusion.2), channel_id=1, source_target_pairs={{0,0},{1,16},{2,32},{3,48},{4,64},{5,80},{6,96},{7,112},{8,128},{9... | collective-permute-start | bytes 196616 | tf_op jit(solution)/shard_map/ppermute | solution.py:430
  47.6 4.4 %shard_map.121 = (f32[128,32,128]{2,1,0:T(8,128)S(1)}, f32[128,128]{1,0:T(8,128)S(1)}, f32[128,128]{1,0:T(8,128)S(1)}) custom-call(s32[8]{0:T(128)S(1)} %pad_add_fusion.place_ref, bf16[256,4,128]{2,1,0:T(4,128)(2,1)S(1)} %all-to-all-done.feat_ref, bf16[128,128]{1,0:T(8,128)(2,1)S(1)} %copy-done.1, bf16[128,128]{1,0:T(8,128)(2,1)S(1)} %copy-done, ...), custom_call_target="tpu_custom_call" | custom-call | flops 6000000000 | bytes 18000000 | tf_op jit(solution)/shard_map/pallas_call | solution.py:418
  52.1 20.6 %shard_map.123 = (f32[64,64]{1,0:T(8,128)S(1)}, f32[3,96,96]{2,1,0:T(8,128)S(1)}, f32[128,32,128]{2,1,0:T(8,128)S(1)}, bf16[128,32,128]{2,1,0:T(8,128)(2,1)S(1)}, f32[128,32,128]{2,1,0:T(8,128)S(1)}) custom-call(s32[8]{0:T(128)S(1)} %pad_add_fusion.place_ref, f32[128,32,128]{2,1,0:T(8,128)S(1)} %get-tuple-element.27.mixed_ref, ...), custom_call_target="tpu_custom_call" | custom-call | flops 24000000000 | bytes 72000000 | tf_op jit(solution)/shard_map/pallas_call | solution.py:438
  76.6 3.8 %collective-permute-start.7 = (bf16[216,128]{1,0:T(8,128)(2,1)S(1)}, bf16[216,128]{1,0:T(8,128)(2,1)S(1)}, u32[]{:S(2)}, u32[]{:S(2)}) collective-permute-start(bf16[216,128]{1,0:T(8,128)(2,1)S(1)} %add_convert_fusion.7), channel_id=1, source_target_pairs={{0,32},{16,48},{32,0},{48,16},{64,96},{80,112},{96,64},{112,80},{1... | collective-permute-start | bytes 165896 | tf_op jit(solution)/shard_map/ppermute | solution.py:461
  83.2 3.9 %shard_map.124 = (bf16[64,128]{1,0:T(8,128)(2,1)S(1)}, bf16[64,128]{1,0:T(8,128)(2,1)S(1)}) custom-call(s32[8]{0:T(128)S(1)} %pad_add_fusion.place_ref, f32[128,32,128]{2,1,0:T(8,128)S(1)} %get-tuple-element.36.grad_ref, bf16[128,32,128]{2,1,0:T(8,128)(2,1)S(1)} %copy-done.9, f32[128,32,128]{2,1,0:T(8,128)S(1)} %copy-done.7, ...), custom_call_target="tpu_custom_call" | custom-call | flops 7000000000 | bytes 21000000 | tf_op jit(solution)/shard_map/pallas_call | solution.py:469
  87.3 6.0 %collective-permute-start.8 = (bf16[280,128]{1,0:T(8,128)(2,1)S(1)}, bf16[280,128]{1,0:T(8,128)(2,1)S(1)}, u32[]{:S(2)}, u32[]{:S(2)}) collective-permute-start(bf16[280,128]{1,0:T(8,128)(2,1)S(1)} %pad_maximum_fusion), channel_id=1, source_target_pairs={{0,64},{16,80},{32,96},{48,112},{64,0},{80,16},{96,32},{112,48},{1... | collective-permute-start | bytes 215048 | tf_op jit(solution)/shard_map/ppermute | solution.py:461
  93.2 2.5 %collective-permute-done.8 = bf16[280,128]{1,0:T(8,128)(2,1)S(1)} collective-permute-done((bf16[280,128]{1,0:T(8,128)(2,1)S(1)}, bf16[280,128]{1,0:T(8,128)(2,1)S(1)}, u32[]{:S(2)}, u32[]{:S(2)}) %collective-permute-start.8) | collective-permute-done | bytes 71712 | tf_op jit(solution)/shard_map/ppermute | solution.py:461
  95.7 3.9 %collective-permute-start.9 = (bf16[280,128]{1,0:T(8,128)(2,1)S(1)}, bf16[280,128]{1,0:T(8,128)(2,1)S(1)}, u32[]{:S(2)}, u32[]{:S(2)}) collective-permute-start(bf16[280,128]{1,0:T(8,128)(2,1)S(1)} %add_convert_fusion.5), channel_id=1, source_target_pairs={{0,128},{16,144},{32,160},{48,176},{64,192},{80,208},{96,224},{112... | collective-permute-start | bytes 215048 | tf_op jit(solution)/shard_map/ppermute | solution.py:461
  99.6 2.3 %collective-permute-done.9 = bf16[280,128]{1,0:T(8,128)(2,1)S(1)} collective-permute-done((bf16[280,128]{1,0:T(8,128)(2,1)S(1)}, bf16[280,128]{1,0:T(8,128)(2,1)S(1)}, u32[]{:S(2)}, u32[]{:S(2)}) %collective-permute-start.9) | collective-permute-done | bytes 71712 | tf_op jit(solution)/shard_map/ppermute | solution.py:461
  102.0 1.7 %collective-permute-start.10 = (bf16[280,128]{1,0:T(8,128)(2,1)S(1)}, bf16[280,128]{1,0:T(8,128)(2,1)S(1)}, u32[]{:S(2)}, u32[]{:S(2)}) collective-permute-start(bf16[280,128]{1,0:T(8,128)(2,1)S(1)} %pad_maximum_fusion.1), channel_id=1, source_target_pairs={{0,1},{1,0},{2,3},{3,2},{4,5},{5,4},{6,7},{7,6},{8,9},{9,8},{10,11... | collective-permute-start | bytes 215048 | tf_op jit(solution)/shard_map/ppermute | solution.py:461
  103.8 1.9 %collective-permute-start.5 = (f32[64,64]{0,1:T(8,128)S(1)}, f32[64,64]{0,1:T(8,128)S(1)}, u32[]{:S(2)}, u32[]{:S(2)}) collective-permute-start(f32[64,64]{0,1:T(8,128)S(1)} %copy.22), channel_id=1, source_target_pairs={{0,0},{1,16},{2,32},{3,48},{4,64},{5,80},{6,96},{7,112},{8,128},{9... | collective-permute-start | bytes 49160 | tf_op jit(solution)/shard_map/ppermute | solution.py:464
  105.7 2.4 %collective-permute-done.10 = bf16[280,128]{1,0:T(8,128)(2,1)S(1)} collective-permute-done((bf16[280,128]{1,0:T(8,128)(2,1)S(1)}, bf16[280,128]{1,0:T(8,128)(2,1)S(1)}, u32[]{:S(2)}, u32[]{:S(2)}) %collective-permute-start.10) | collective-permute-done | bytes 71712 | tf_op jit(solution)/shard_map/ppermute | solution.py:461
  108.1 2.2 %collective-permute-start.11 = (bf16[280,128]{1,0:T(8,128)(2,1)S(1)}, bf16[280,128]{1,0:T(8,128)(2,1)S(1)}, u32[]{:S(2)}, u32[]{:S(2)}) collective-permute-start(bf16[280,128]{1,0:T(8,128)(2,1)S(1)} %add_convert_fusion.3), channel_id=1, source_target_pairs={{0,2},{1,3},{2,0},{3,1},{4,6},{5,7},{6,4},{7,5},{8,10},{9,11},{10,... | collective-permute-start | bytes 215048 | tf_op jit(solution)/shard_map/ppermute | solution.py:461
  112.6 4.2 %collective-permute-start.12 = (bf16[280,128]{1,0:T(8,128)(2,1)S(1)}, bf16[280,128]{1,0:T(8,128)(2,1)S(1)}, u32[]{:S(2)}, u32[]{:S(2)}) collective-permute-start(bf16[280,128]{1,0:T(8,128)(2,1)S(1)} %add_convert_fusion.2), channel_id=1, source_target_pairs={{0,4},{1,5},{2,6},{3,7},{4,0},{5,1},{6,2},{7,3},{8,12},{9,13},{10,... | collective-permute-start | bytes 215048 | tf_op jit(solution)/shard_map/ppermute | solution.py:461
  116.9 1.7 %collective-permute-start.15 = (bf16[64,128]{1,0:T(8,128)(2,1)S(1)}, bf16[64,128]{1,0:T(8,128)(2,1)S(1)}, u32[]{:S(2)}, u32[]{:S(2)}) collective-permute-start(bf16[64,128]{1,0:T(8,128)(2,1)S(1)} %add_convert_fusion.9), channel_id=1, source_target_pairs={{0,32},{16,48},{32,0},{48,16},{64,96},{80,112},{96,64},{112,80},{1... | collective-permute-start | bytes 49160 | tf_op jit(solution)/shard_map/ppermute | solution.py:461
  118.6 2.1 %collective-permute-done.12 = bf16[280,128]{1,0:T(8,128)(2,1)S(1)} collective-permute-done((bf16[280,128]{1,0:T(8,128)(2,1)S(1)}, bf16[280,128]{1,0:T(8,128)(2,1)S(1)}, u32[]{:S(2)}, u32[]{:S(2)}) %collective-permute-start.12) | collective-permute-done | bytes 71712 | tf_op jit(solution)/shard_map/ppermute | solution.py:461
  120.7 12.8 %collective-permute-start.13 = (bf16[280,128]{1,0:T(8,128)(2,1)S(1)}, bf16[280,128]{1,0:T(8,128)(2,1)S(1)}, u32[]{:S(2)}, u32[]{:S(2)}) collective-permute-start(bf16[280,128]{1,0:T(8,128)(2,1)S(1)} %add_convert_fusion.1), channel_id=1, source_target_pairs={{0,8},{1,9},{2,10},{3,11},{4,12},{5,13},{6,14},{7,15},{8,0},{9,1},... | collective-permute-start | bytes 215048 | tf_op jit(solution)/shard_map/ppermute | solution.py:461
  134.3 3.2 %collective-permute-done.13 = bf16[280,128]{1,0:T(8,128)(2,1)S(1)} collective-permute-done((bf16[280,128]{1,0:T(8,128)(2,1)S(1)}, bf16[280,128]{1,0:T(8,128)(2,1)S(1)}, u32[]{:S(2)}, u32[]{:S(2)}) %collective-permute-start.13) | collective-permute-done | bytes 71712 | tf_op jit(solution)/shard_map/ppermute | solution.py:461
  (78 shorter events, 20.2 us)
Async XLA Ops:
  2.1 30.4 %copy-start.4 = (f32[64,64]{1,0:T(8,128)S(1)}, f32[64,64]{1,0:T(8,128)}, u32[]{:S(2)}) copy-start(f32[64,64]{1,0:T(8,128)} %cot_ref.3) | copy-start | bytes 49156
  2.1 30.4 %all-to-all-start = ((bf16[256,4,128]{2,1,0:T(4,128)(2,1)}), bf16[256,4,128]{2,1,0:T(4,128)(2,1)S(1)}, u32[]{:S(2)}, u32[]{:S(2)}) async-start(bf16[256,4,128]{2,1,0:T(4,128)(2,1)} %broadcast_in_dim.4), calls=%async_computation | async-start | bytes 524288 | tf_op jit(solution)/shard_map/all_to_all | solution.py:409
  19.0 15.2 %copy-start.11 = (s32[3]{0:T(128)S(1)}, s32[3]{0:T(128)}, u32[]{:S(2)}) copy-start(s32[3]{0:T(128)} %param.16) | copy-start | bytes 40
  19.1 15.3 %copy-start.10 = (bf16[3,32,288]{2,1,0:T(8,128)(2,1)S(1)}, bf16[3,32,288]{2,1,0:T(8,128)(2,1)}, u32[]{:S(2)}) copy-start(bf16[3,32,288]{2,1,0:T(8,128)(2,1)} %param.14) | copy-start | bytes 165892
  19.1 9.6 %collective-permute-start = (bf16[17,32,128]{2,1,0:T(8,128)(2,1)S(1)}, bf16[17,32,128]{2,1,0:T(8,128)(2,1)S(1)}, u32[]{:S(2)}, u32[]{:S(2)}) collective-permute-start(bf16[17,32,128]{2,1,0:T(8,128)(2,1)S(1)} %get-tuple-element.24), channel_id=1, source_target_pairs={{0,1},{1,2},{2,3},{3,4},{4,5},{5,6},{6,7},{7,8},{8,9},{9,10},{10,1... | collective-permute-start | bytes 417800 | tf_op jit(solution)/shard_map/ppermute | solution.py:405
  22.7 9.7 %collective-permute-start.1 = (bf16[17,32,128]{2,1,0:T(8,128)(2,1)S(1)}, bf16[17,32,128]{2,1,0:T(8,128)(2,1)S(1)}, u32[]{:S(2)}, u32[]{:S(2)}) collective-permute-start(bf16[17,32,128]{2,1,0:T(8,128)(2,1)S(1)} %get-tuple-element.25), channel_id=1, source_target_pairs={{1,0},{2,1},{3,2},{4,3},{5,4},{6,5},{7,6},{8,7},{9,8},{10,9},{11,1... | collective-permute-start | bytes 417800 | tf_op jit(solution)/shard_map/ppermute | solution.py:406
  32.8 14.8 %copy-start = (bf16[128,128]{1,0:T(8,128)(2,1)S(1)}, bf16[128,128]{1,0:T(8,128)(2,1)}, u32[]{:S(2)}) copy-start(bf16[128,128]{1,0:T(8,128)(2,1)} %w_right_ref.1) | copy-start | bytes 98308
  32.8 14.8 %copy-start.1 = (bf16[128,128]{1,0:T(8,128)(2,1)S(1)}, bf16[128,128]{1,0:T(8,128)(2,1)}, u32[]{:S(2)}) copy-start(bf16[128,128]{1,0:T(8,128)(2,1)} %w_left_ref.1) | copy-start | bytes 98308
  32.8 14.8 %copy-start.5 = (bf16[32,128]{1,0:T(8,128)(2,1)S(1)}, bf16[32,128]{1,0:T(8,128)(2,1)}, u32[]{:S(2)}) copy-start(bf16[32,128]{1,0:T(8,128)(2,1)} %w_in_ref.3) | copy-start | bytes 24580
  32.8 4.3 %collective-permute-start.2 = (bf16[34,32,128]{2,1,0:T(8,128)(2,1)S(1)}, bf16[34,32,128]{2,1,0:T(8,128)(2,1)S(1)}, u32[]{:S(2)}, u32[]{:S(2)}) collective-permute-start(bf16[34,32,128]{2,1,0:T(8,128)(2,1)S(1)} %get-tuple-element.31.part2_ref), channel_id=1, source_target_pairs={{0,16},{16,32},{32,48},{48,64},{64,80},{80,96},{96,112},{112,128},... | collective-permute-start | bytes 835592 | tf_op jit(solution)/shard_map/ppermute | solution.py:415
  35.8 5.8 %collective-permute-start.3 = (bf16[34,32,128]{2,1,0:T(8,128)(2,1)S(1)}, bf16[34,32,128]{2,1,0:T(8,128)(2,1)S(1)}, u32[]{:S(2)}, u32[]{:S(2)}) collective-permute-start(bf16[34,32,128]{2,1,0:T(8,128)(2,1)S(1)} %get-tuple-element.32.part1_ref), channel_id=1, source_target_pairs={{16,0},{32,16},{48,32},{64,48},{80,64},{96,80},{112,96},{128,112},... | collective-permute-start | bytes 835592 | tf_op jit(solution)/shard_map/ppermute | solution.py:416
  41.6 10.5 %copy-start.12 = (bf16[32]{0:T(256)(128)(2,1)S(1)}, bf16[32]{0:T(256)(128)(2,1)}, u32[]{:S(2)}) copy-start(bf16[32]{0:T(256)(128)(2,1)} %param.15) | copy-start | bytes 196
  41.6 10.5 %collective-permute-start.4 = (f32[128,128]{1,0:T(8,128)S(1)}, f32[128,128]{1,0:T(8,128)S(1)}, u32[]{:S(2)}, u32[]{:S(2)}) collective-permute-start(f32[128,128]{1,0:T(8,128)S(1)} %pad_maximum_fusion.2), channel_id=1, source_target_pairs={{0,0},{1,16},{2,32},{3,48},{4,64},{5,80},{6,96},{7,112},{8,128},{9... | collective-permute-start | bytes 196616 | tf_op jit(solution)/shard_map/ppermute | solution.py:430
  75.2 1.3 collective-permute-start.6
  76.6 10.6 %collective-permute-start.7 = (bf16[216,128]{1,0:T(8,128)(2,1)S(1)}, bf16[216,128]{1,0:T(8,128)(2,1)S(1)}, u32[]{:S(2)}, u32[]{:S(2)}) collective-permute-start(bf16[216,128]{1,0:T(8,128)(2,1)S(1)} %add_convert_fusion.7), channel_id=1, source_target_pairs={{0,32},{16,48},{32,0},{48,16},{64,96},{80,112},{96,64},{112,80},{1... | collective-permute-start | bytes 165896 | tf_op jit(solution)/shard_map/ppermute | solution.py:461
  87.3 8.4 %collective-permute-start.8 = (bf16[280,128]{1,0:T(8,128)(2,1)S(1)}, bf16[280,128]{1,0:T(8,128)(2,1)S(1)}, u32[]{:S(2)}, u32[]{:S(2)}) collective-permute-start(bf16[280,128]{1,0:T(8,128)(2,1)S(1)} %pad_maximum_fusion), channel_id=1, source_target_pairs={{0,64},{16,80},{32,96},{48,112},{64,0},{80,16},{96,32},{112,48},{1... | collective-permute-start | bytes 215048 | tf_op jit(solution)/shard_map/ppermute | solution.py:461
  95.7 6.2 %collective-permute-start.9 = (bf16[280,128]{1,0:T(8,128)(2,1)S(1)}, bf16[280,128]{1,0:T(8,128)(2,1)S(1)}, u32[]{:S(2)}, u32[]{:S(2)}) collective-permute-start(bf16[280,128]{1,0:T(8,128)(2,1)S(1)} %add_convert_fusion.5), channel_id=1, source_target_pairs={{0,128},{16,144},{32,160},{48,176},{64,192},{80,208},{96,224},{112... | collective-permute-start | bytes 215048 | tf_op jit(solution)/shard_map/ppermute | solution.py:461
  102.0 6.1 %collective-permute-start.10 = (bf16[280,128]{1,0:T(8,128)(2,1)S(1)}, bf16[280,128]{1,0:T(8,128)(2,1)S(1)}, u32[]{:S(2)}, u32[]{:S(2)}) collective-permute-start(bf16[280,128]{1,0:T(8,128)(2,1)S(1)} %pad_maximum_fusion.1), channel_id=1, source_target_pairs={{0,1},{1,0},{2,3},{3,2},{4,5},{5,4},{6,7},{7,6},{8,9},{9,8},{10,11... | collective-permute-start | bytes 215048 | tf_op jit(solution)/shard_map/ppermute | solution.py:461
  103.8 6.7 %collective-permute-start.5 = (f32[64,64]{0,1:T(8,128)S(1)}, f32[64,64]{0,1:T(8,128)S(1)}, u32[]{:S(2)}, u32[]{:S(2)}) collective-permute-start(f32[64,64]{0,1:T(8,128)S(1)} %copy.22), channel_id=1, source_target_pairs={{0,0},{1,16},{2,32},{3,48},{4,64},{5,80},{6,96},{7,112},{8,128},{9... | collective-permute-start | bytes 49160 | tf_op jit(solution)/shard_map/ppermute | solution.py:464
  108.1 4.5 %collective-permute-start.11 = (bf16[280,128]{1,0:T(8,128)(2,1)S(1)}, bf16[280,128]{1,0:T(8,128)(2,1)S(1)}, u32[]{:S(2)}, u32[]{:S(2)}) collective-permute-start(bf16[280,128]{1,0:T(8,128)(2,1)S(1)} %add_convert_fusion.3), channel_id=1, source_target_pairs={{0,2},{1,3},{2,0},{3,1},{4,6},{5,7},{6,4},{7,5},{8,10},{9,11},{10,... | collective-permute-start | bytes 215048 | tf_op jit(solution)/shard_map/ppermute | solution.py:461
  111.1 5.7 %collective-permute-start.14 = (bf16[64,128]{1,0:T(8,128)(2,1)S(1)}, bf16[64,128]{1,0:T(8,128)(2,1)S(1)}, u32[]{:S(2)}, u32[]{:S(2)}) collective-permute-start(bf16[64,128]{1,0:T(8,128)(2,1)S(1)} %slice.54), channel_id=1, source_target_pairs={{0,16},{16,0},{32,48},{48,32},{64,80},{80,64},{96,112},{112,96},{1... | collective-permute-start | bytes 49160 | tf_op jit(solution)/shard_map/ppermute | solution.py:461
  112.6 8.1 %collective-permute-start.12 = (bf16[280,128]{1,0:T(8,128)(2,1)S(1)}, bf16[280,128]{1,0:T(8,128)(2,1)S(1)}, u32[]{:S(2)}, u32[]{:S(2)}) collective-permute-start(bf16[280,128]{1,0:T(8,128)(2,1)S(1)} %add_convert_fusion.2), channel_id=1, source_target_pairs={{0,4},{1,5},{2,6},{3,7},{4,0},{5,1},{6,2},{7,3},{8,12},{9,13},{10,... | collective-permute-start | bytes 215048 | tf_op jit(solution)/shard_map/ppermute | solution.py:461
  116.9 16.6 %collective-permute-start.15 = (bf16[64,128]{1,0:T(8,128)(2,1)S(1)}, bf16[64,128]{1,0:T(8,128)(2,1)S(1)}, u32[]{:S(2)}, u32[]{:S(2)}) collective-permute-start(bf16[64,128]{1,0:T(8,128)(2,1)S(1)} %add_convert_fusion.9), channel_id=1, source_target_pairs={{0,32},{16,48},{32,0},{48,16},{64,96},{80,112},{96,64},{112,80},{1... | collective-permute-start | bytes 49160 | tf_op jit(solution)/shard_map/ppermute | solution.py:461
  120.7 16.7 %collective-permute-start.13 = (bf16[280,128]{1,0:T(8,128)(2,1)S(1)}, bf16[280,128]{1,0:T(8,128)(2,1)S(1)}, u32[]{:S(2)}, u32[]{:S(2)}) collective-permute-start(bf16[280,128]{1,0:T(8,128)(2,1)S(1)} %add_convert_fusion.1), channel_id=1, source_target_pairs={{0,8},{1,9},{2,10},{3,11},{4,12},{5,13},{6,14},{7,15},{8,0},{9,1},... | collective-permute-start | bytes 215048 | tf_op jit(solution)/shard_map/ppermute | solution.py:461
  (6 other events, 6.9 us)

commit v3 on v2

--- a/solution.py
+++ b/solution.py
@@ -39,7 +39,8 @@
     return high, (value - high.astype(F32)).astype(BF16)
 
 
-def edges_kernel(pair_ref, cot_ref, own_ref, left_ref, right_ref):
+def edges_kernel(pair_ref, cot_ref, feat_ref, own_ref, left_ref, right_ref, sent_ref):
+    sent_ref[...] = jnp.broadcast_to(feat_ref[...][None], sent_ref.shape)
     own = jnp.swapaxes(pair_ref[...].astype(F32), 0, 1)
     own_ref[...] = own.astype(BF16)
     cot = cot_ref[...]
@@ -176,6 +177,7 @@
     direct_ref,
     terms_ref,
     grad_ref,
+    last_ref,
     round_ref,
     slope0_ref,
     state_ref,
@@ -249,7 +251,6 @@
         upstream_ref[rows, :] = 0.5 * (mine + other[rows, :])
 
     tile_lanes = jnp.where(lax.broadcasted_iota(jnp.int32, (1, WIDE), 1) < TILE, 1.0, 0.0).astype(F32)
-    terms_ref[...] = jnp.zeros_like(terms_ref)
     masked_ref[...] = jnp.zeros_like(masked_ref)
 
     def weight_terms(layer):
@@ -278,7 +279,7 @@
                 )
             return total
 
-        terms_ref[layer] = lax.fori_loop(0, 10, body, jnp.zeros((96, 96), F32))
+        return lax.fori_loop(0, 10, body, jnp.zeros((96, 96), F32))
 
     def back(layer, first, last, one_grad, z_now):
         def make(base):
@@ -290,7 +291,7 @@
             multiply(backward_ref[layer], patchb_ref, z_now, base, ROWS)
 
         pipelined(first, last, ROWS, make, use)
-        weight_terms(layer)
+        return weight_terms(layer)
 
     def first_grad(base):
         return upstream_ref[pl.ds(base, ROWS), :][:, None, :] * w_out[None]
@@ -302,27 +303,33 @@
         grad2_ref[block] = new
         return new
 
-    back(2, 8, 120, first_grad, zb_ref)
-    back(1, 16, 112, second_grad, za_ref)
+    terms2 = back(2, 8, 120, first_grad, zb_ref)
+    terms1 = back(1, 16, 112, second_grad, za_ref)
 
     def third_grad(step, carry):
         base = 24 + ROWS * step
         block = pl.ds(base, ROWS)
         new = grad2_ref[block] + many_taps(za_ref, base, ROWS, rates[1]) * slope1_ref[block]
         new = new * rows_mask(inside, row, base, ROWS)
-        grad_ref[block] = new
-        round_ref[block] = new.astype(BF16)
+        rounded = new.astype(BF16)
+        last_ref[pl.ds(base - 24, ROWS)] = rounded
+        round_ref[block] = rounded
+        slope = pltpu.roll(slope0_ref[block], TILE, 2)
+        grad_ref[pl.ds(base - 24, ROWS)] = jnp.where(first_half, new, slope)
         return carry
 
+    first_half = lax.broadcasted_iota(jnp.int32, (1, 1, WIDE), 2) < TILE
     lax.fori_loop(0, 80 // ROWS, third_grad, 0)
-    weight_terms(0)
+    terms0 = weight_terms(0)
+    terms = jnp.concatenate([terms0, terms1, terms2], axis=0)
+    spare = jnp.concatenate([terms[216:288, 32 * k : 32 * k + 32] for k in range(3)], axis=0)
+    terms_ref[...] = jnp.concatenate([terms[0:216], spare], axis=1).astype(BF16)
 
 
 def last_kernel(
     place_ref,
     grad_ref,
     round_ref,
-    slope0_ref,
     rows_ref,
     cols_ref,
     backward_ref,
@@ -340,16 +347,17 @@
     def use(base):
         multiply(backward_ref[0], patch_ref, z_ref, base, ROWS)
 
-    pipelined(24, 104, ROWS, make, use)
+    pipelined(0, 80, ROWS, make, use)
     w_in = w_in_ref[...]
     cols = cols_ref[0:TILE, :]
 
     def body(step, total):
-        base = HALO + ROWS * step
-        block = pl.ds(base, ROWS)
-        start = grad_ref[block] + many_taps(z_ref, base, ROWS, rate) * slope0_ref[block]
+        base = ROWS * step
+        both = grad_ref[pl.ds(base + 8, ROWS)]
+        slope = pltpu.roll(both, TILE, 2)
+        start = both + many_taps(z_ref, base + 8, ROWS, rate) * slope
         start = start[:, :, :TILE].astype(BF16)
-        rows = rows_ref[block, :]
+        rows = rows_ref[pl.ds(base + HALO, ROWS), :]
         sums = []
         for k in range(ROWS):
             hidden = lax.dot_general(
@@ -358,11 +366,47 @@
             outer = hidden * gelu_pair(rows[k : k + 1, :] + cols)[1]
             sums.append(jnp.sum(outer, axis=0, keepdims=True))
             total = total + outer
-        row_ref[pl.ds(base - HALO, ROWS), :] = jnp.concatenate(sums, axis=0).astype(BF16)
+        row_ref[pl.ds(base, ROWS), :] = jnp.concatenate(sums, axis=0).astype(BF16)
         return total
 
     total = lax.fori_loop(0, TILE // ROWS, body, jnp.zeros((TILE, 128), F32))
     col_ref[...] = total.astype(BF16)
+
+
+def finish_kernel(
+    mine_ref,
+    got_ref,
+    col_ref,
+    w_left_ref,
+    w_right_ref,
+    direct_ref,
+    other_ref,
+    logits_ref,
+    grad_rows_ref,
+    grad_cols_ref,
+    conv_ref,
+):
+    logits_ref[...] = 0.5 * (direct_ref[...] + other_ref[...].T)
+    total = mine_ref[...].astype(F32) + got_ref[...].astype(F32)
+    for value, weight_ref, out_ref in (
+        (total[0:TILE], w_left_ref, grad_rows_ref),
+        (col_ref[...].astype(F32), w_right_ref, grad_cols_ref),
+    ):
+        out_ref[...] = lax.dot_general(
+            value,
+            weight_ref[...].astype(F32),
+            (((1,), (1,)), ((), ())),
+            precision=lax.Precision.HIGHEST,
+            preferred_element_type=F32,
+        )
+    terms = total[TILE:] * (1.0 / 1024.0)
+    spare = jnp.concatenate([terms[72 * k : 72 * k + 72, 96:128] for k in range(3)], axis=1)
+    terms = jnp.concatenate([terms[:, 0:96], spare], axis=0)
+    for layer in range(3):
+        at = 96 * layer
+        conv_ref[layer] = jnp.concatenate(
+            [terms[at + CH * a : at + CH * a + CH] for a in range(3)], axis=1
+        )
 
 
 def shape(*dims, dtype=F32):
@@ -383,10 +427,6 @@
     )
 
 
-def flips(axis, bit):
-    return [(i, i ^ bit) for i in range(lax.axis_size(axis))]
-
-
 def on_device(features, w_left, w_right, w_in, pair_input, conv_w, w_out, dilation, cotangent):
     n_row = lax.axis_size("row")
     n_col = lax.axis_size("col")
@@ -397,15 +437,15 @@
     down = [(i + 1, i) for i in range(n_row - 1)]
     swap = [(r * n_col + c, c * n_col + r) for r in range(n_row) for c in range(n_col)]
 
-    own, left_edge, right_edge = call(
+    own, left_edge, right_edge, sent = call(
         edges_kernel,
-        [shape(TILE, CH, TILE, dtype=BF16)] + [shape(17, CH, WIDE, dtype=BF16)] * 2,
-        [VMEM] * 2,
-    )(pair_input, cotangent)
+        [shape(TILE, CH, TILE, dtype=BF16)]
+        + [shape(17, CH, WIDE, dtype=BF16)] * 2
+        + [shape(n_row * n_col, *features.shape, dtype=BF16)],
+        [VMEM] * 3,
+    )(pair_input, cotangent, features)
     from_left = lax.ppermute(right_edge, "col", up)
     from_right = lax.ppermute(left_edge, "col", down)
-
-    sent = jnp.broadcast_to(features[None], (n_row * n_col,) + features.shape)
     gathered = lax.all_to_all(sent, ("row", "col"), 0, 0)
     from_left, from_right, gathered = lax.optimization_barrier((from_left, from_right, gathered))
 
@@ -435,11 +475,13 @@
     )
     w_out_wide = jnp.broadcast_to(w_out.astype(F32)[:, None], (CH, WIDE))
     big = (WIDE, CH, WIDE)
-    direct, terms, grad, rounded, slope0 = call(
+    direct, terms, grad, rounded = call(
         main_kernel,
-        [shape(TILE, TILE), shape(3, 96, 96), shape(*big), shape(*big, dtype=BF16), shape(*big)],
+        [shape(TILE, TILE), shape(216, 128, dtype=BF16), shape(80, CH, WIDE), shape(80, CH, WIDE, dtype=BF16)],
         [SMEM] + [VMEM] * 9,
         [
+            pltpu.VMEM(big, BF16),
+            pltpu.VMEM(big, F32),
             pltpu.VMEM(big, BF16),
             pltpu.VMEM(big, F32),
             pltpu.VMEM(big, F32),
@@ -453,49 +495,54 @@
             pltpu.VMEM((WIDE, WIDE), F32),
             pltpu.VMEM(big, F32),
         ],
-        40,
+        42,
         24,
     )(place, mixed, above, upper, lower, below, mirrored, forward_w, backward_w, w_out_wide)
 
-    def summed(value, axis, bit):
-        other = lax.ppermute(value, axis, flips(axis, bit))
-        return (value.astype(F32) + other.astype(F32)).astype(BF16)
+    def flipped(value, row_bits, col_bits):
+        pairs = [
+            (r * n_col + c, (r ^ row_bits) * n_col + (c ^ col_bits))
+            for r in range(n_row)
+            for c in range(n_col)
+        ]
+        return lax.ppermute(value, ("row", "col"), pairs)
+
+    def summed(value, row_bits, col_bits):
+        return (value.astype(F32) + flipped(value, row_bits, col_bits).astype(F32)).astype(BF16)
 
     direct_other = lax.ppermute(direct, ("row", "col"), swap)
-    packed = summed(terms.astype(BF16).reshape(216, 128), "row", 1)
-    grad, packed = lax.optimization_barrier((grad, packed))
-    packed = summed(packed, "row", 2)
-
+    terms = summed(terms, 1, 0)
+    grad, rounded, row_project, col_project, terms = lax.optimization_barrier(
+        (grad, rounded, row_project, col_project, terms)
+    )
+    terms = summed(terms, 2, 0)
     row_part, col_part = call(
         last_kernel,
         [shape(TILE, 128, dtype=BF16), shape(TILE, 128, dtype=BF16)],
-        [SMEM] + [VMEM] * 7,
-        [pltpu.VMEM((WIDE, 96, WIDE), F32), pltpu.VMEM((WIDE, 96, WIDE), BF16)],
-        24,
+        [SMEM] + [VMEM] * 6,
+        [pltpu.VMEM((80, 96, WIDE), F32), pltpu.VMEM((80, 96, WIDE), BF16)],
+        16,
         7,
-    )(place, grad, rounded, slope0, row_project, col_project, backward_w, w_in)
-
-    logits = 0.5 * (direct + direct_other.T)
-    packed = jnp.concatenate([col_part, packed], axis=0)
-    for bit in (4, 8):
-        packed = summed(packed, "row", bit)
+    )(place, grad, rounded, row_project, col_project, backward_w, w_in)
+
+    packed = jnp.concatenate([col_part, terms], axis=0)
+    packed = summed(packed, 4, 0)
+    row_part = summed(row_part, 0, 1)
+    packed = summed(packed, 12, 0)
     col_part = packed[:TILE]
-    packed = jnp.concatenate([row_part, packed[TILE:]], axis=0)
-    for bit in (1, 2):
-        packed = summed(packed, "col", bit)
-        col_part = summed(col_part, "row", bit)
-    for bit in (4, 8):
-        packed = summed(packed, "col", bit)
-    row_part = packed[:TILE]
-    conv_grads = (
-        packed[TILE:].reshape(3, 3, CH, 96).transpose(0, 2, 1, 3).reshape(3, CH, 288).astype(F32)
-        / (TILE * n_row)
-    )
-    row_part = row_part.astype(F32)
-    col_part = col_part.astype(F32)
-    grad_rows = jnp.dot(row_part, w_left.astype(F32).T, precision=lax.Precision.HIGHEST)
-    grad_cols = jnp.dot(col_part, w_right.astype(F32).T, precision=lax.Precision.HIGHEST)
-    return (logits, grad_rows, grad_cols, conv_grads)
+    terms = summed(packed[TILE:], 2, 1)
+    col_part = summed(col_part, 1, 0)
+    packed = jnp.concatenate([row_part, terms], axis=0)
+    packed = summed(packed, 0, 2)
+    col_part = summed(col_part, 2, 0)
+    packed = summed(packed, 0, 4)
+    return tuple(
+        call(
+            finish_kernel,
+            [shape(TILE, TILE), shape(TILE, 128), shape(TILE, 128), shape(3, CH, 288)],
+            [VMEM] * 7,
+        )(packed, flipped(packed, 0, 12), col_part, w_left, w_right, direct, direct_other)
+    )
 
 
 def solution(mesh):

time: 140 us -> 129 us (0.921)
  the two profiles are of different devices: /device:TPU:4 before, /device:TPU:40 now
where the time goes in v3:
time: 129 us; the launch traced here: 128 us
  starting transfers between devices  56.5 us (44%)
  waiting for transfers between devices  33.5 us (26%)
  Pallas kernels  32.5 us (25%)
  local copies, waits for them, and re-layouts  3.96 us (3%)
    pallas_call x1, Pallas kernels, on_device(): call(main_kernel, [shape(TILE, TILE), shape(216, 128, dtype=BF16), shape(...  21.1 us
    ppermute x11, starting transfers between devices, flipped(): return lax.ppermute(value, ('row', 'col'), pairs)  20.2 us
    ppermute x11, waiting for transfers between devices, flipped(): return lax.ppermute(value, ('row', 'col'), pairs)  20 us
    all_to_all x1, starting transfers between devices, on_device(): gathered = lax.all_to_all(sent, ('row', 'col'), 0, 0)  14.3 us
    ppermute x1, starting transfers between devices, on_device(): from_left = lax.ppermute(right_edge, 'col', up)  4.91 us
    ppermute x1, starting transfers between devices, on_device(): direct_other = lax.ppermute(direct, ('row', 'col'), swap)  4.9 us
    ppermute x1, starting transfers between devices, on_device(): below = lax.ppermute(upper, 'row', down)  4.51 us
    pallas_call x1, Pallas kernels, on_device(): call(mixed_kernel, [shape(WIDE, CH, WIDE), shape(WIDE, 128), shape(WIDE,...  4.44 us
  transfers between devices with their start and end apart: 18, of which 13 were waited for; matrix products, arithmetic and copies ran while one was open for 1% of the time, Pallas kernels for 7%

profile of v3, /device:TPU:40, one launch (start us, length us, event | category | flops | bytes accessed | tf_op | source)
XLA Modules:
  0.0 127.7 jit_solution(4818442329620155842)
XLA Ops:
  4.3 14.3 %all-to-all-start = ((bf16[256,4,128]{2,1,0:T(4,128)(2,1)}), bf16[256,4,128]{2,1,0:T(4,128)(2,1)S(1)}, u32[]{:S(2)}, u32[]{:S(2)}) async-start(bf16[256,4,128]{2,1,0:T(4,128)(2,1)} %get-tuple-element.29), calls=%async_computation | async-start | bytes 524288 | tf_op jit(solution)/shard_map/all_to_all | solution.py:449
  18.6 4.9 %collective-permute-start = (bf16[17,32,128]{2,1,0:T(8,128)(2,1)S(1)}, bf16[17,32,128]{2,1,0:T(8,128)(2,1)S(1)}, u32[]{:S(2)}, u32[]{:S(2)}) collective-permute-start(bf16[17,32,128]{2,1,0:T(8,128)(2,1)S(1)} %get-tuple-element.27), channel_id=1, source_target_pairs={{0,1},{1,2},{2,3},{3,4},{4,5},{5,6},{6,7},{7,8},{8,9},{9,10},{10,1... | collective-permute-start | bytes 417800 | tf_op jit(solution)/shard_map/ppermute | solution.py:447
  23.6 3.3 %collective-permute-start.1 = (bf16[17,32,128]{2,1,0:T(8,128)(2,1)S(1)}, bf16[17,32,128]{2,1,0:T(8,128)(2,1)S(1)}, u32[]{:S(2)}, u32[]{:S(2)}) collective-permute-start(bf16[17,32,128]{2,1,0:T(8,128)(2,1)S(1)} %get-tuple-element.28), channel_id=1, source_target_pairs={{1,0},{2,1},{3,2},{4,3},{5,4},{6,5},{7,6},{8,7},{9,8},{10,9},{11,1... | collective-permute-start | bytes 417800 | tf_op jit(solution)/shard_map/ppermute | solution.py:448
  26.9 4.0 %collective-permute-done.from_left_ref = bf16[17,32,128]{2,1,0:T(8,128)(2,1)S(1)} collective-permute-done((bf16[17,32,128]{2,1,0:T(8,128)(2,1)S(1)}, bf16[17,32,128]{2,1,0:T(8,128)(2,1)S(1)}, u32[]{:S(2)}, u32[]{:S(2)}) %collective-permute-start) | collective-permute-done | bytes 139296 | tf_op jit(solution)/shard_map/ppermute | solution.py:447
  30.9 3.0 %collective-permute-done.1.from_right_ref = bf16[17,32,128]{2,1,0:T(8,128)(2,1)S(1)} collective-permute-done((bf16[17,32,128]{2,1,0:T(8,128)(2,1)S(1)}, bf16[17,32,128]{2,1,0:T(8,128)(2,1)S(1)}, u32[]{:S(2)}, u32[]{:S(2)}) %collective-permute-start.1) | collective-permute-done | bytes 139296 | tf_op jit(solution)/shard_map/ppermute | solution.py:448
  34.3 2.1 %collective-permute-start.2 = (bf16[34,32,128]{2,1,0:T(8,128)(2,1)S(1)}, bf16[34,32,128]{2,1,0:T(8,128)(2,1)S(1)}, u32[]{:S(2)}, u32[]{:S(2)}) collective-permute-start(bf16[34,32,128]{2,1,0:T(8,128)(2,1)S(1)} %get-tuple-element.35.part2_ref), channel_id=1, source_target_pairs={{0,16},{16,32},{32,48},{48,64},{64,80},{80,96},{96,112},{112,128},... | collective-permute-start | bytes 835592 | tf_op jit(solution)/shard_map/ppermute | solution.py:455
  37.9 4.5 %collective-permute-start.3 = (bf16[34,32,128]{2,1,0:T(8,128)(2,1)S(1)}, bf16[34,32,128]{2,1,0:T(8,128)(2,1)S(1)}, u32[]{:S(2)}, u32[]{:S(2)}) collective-permute-start(bf16[34,32,128]{2,1,0:T(8,128)(2,1)S(1)} %get-tuple-element.36.part1_ref), channel_id=1, source_target_pairs={{16,0},{32,16},{48,32},{64,48},{80,64},{96,80},{112,96},{128,112},... | collective-permute-start | bytes 835592 | tf_op jit(solution)/shard_map/ppermute | solution.py:456
  43.2 3.3 %collective-permute-done.3.part3_ref = bf16[34,32,128]{2,1,0:T(8,128)(2,1)S(1)} collective-permute-done((bf16[34,32,128]{2,1,0:T(8,128)(2,1)S(1)}, bf16[34,32,128]{2,1,0:T(8,128)(2,1)S(1)}, u32[]{:S(2)}, u32[]{:S(2)}) %collective-permute-start.3) | collective-permute-done | bytes 278560 | tf_op jit(solution)/shard_map/ppermute | solution.py:456
  46.5 2.2 %collective-permute-start.4 = (f32[128,128]{1,0:T(8,128)S(1)}, f32[128,128]{1,0:T(8,128)S(1)}, u32[]{:S(2)}, u32[]{:S(2)}) collective-permute-start(f32[128,128]{1,0:T(8,128)S(1)} %pad_maximum_fusion.2), channel_id=1, source_target_pairs={{0,0},{1,16},{2,32},{3,48},{4,64},{5,80},{6,96},{7,112},{8,128},{9... | collective-permute-start | bytes 196616 | tf_op jit(solution)/shard_map/ppermute | solution.py:470
  48.7 4.4 %shard_map.121 = (f32[128,32,128]{2,1,0:T(8,128)S(1)}, f32[128,128]{1,0:T(8,128)S(1)}, f32[128,128]{1,0:T(8,128)S(1)}) custom-call(s32[8]{0:T(128)S(1)} %pad_add_fusion.place_ref, bf16[256,4,128]{2,1,0:T(4,128)(2,1)S(1)} %all-to-all-done.feat_ref, bf16[128,128]{1,0:T(8,128)(2,1)S(1)} %copy-done.3, bf16[128,128]{1,0:T(8,128)(2,1)S(1)} %copy-done.4, ...), custom_call_target="tpu_custom_call" | custom-call | flops 6000000000 | bytes 18000000 | tf_op jit(solution)/shard_map/pallas_call | solution.py:458
  53.2 2.5 %collective-permute-done.4.mirror_ref = f32[128,128]{1,0:T(8,128)S(1)} collective-permute-done((f32[128,128]{1,0:T(8,128)S(1)}, f32[128,128]{1,0:T(8,128)S(1)}, u32[]{:S(2)}, u32[]{:S(2)}) %collective-permute-start.4) | collective-permute-done | bytes 65568 | tf_op jit(solution)/shard_map/ppermute | solution.py:470
  55.8 21.1 %shard_map.123 = (f32[64,64]{1,0:T(8,128)S(1)}, bf16[216,128]{1,0:T(8,128)(2,1)S(1)}, f32[80,32,128]{2,1,0:T(8,128)S(1)}, bf16[80,32,128]{2,1,0:T(8,128)(2,1)S(1)}) custom-call(s32[8]{0:T(128)S(1)} %pad_add_fusion.place_ref, f32[128,32,128]{2,1,0:T(8,128)S(1)} %get-tuple-element.31.mixed_ref, bf16[34,32,128]{2,1,0:T(8,128)(2,1)S(1)} %collective-permute-done.2.part0_ref, ...), custom_call_target="tpu_custom_call" | custom-call | flops 24000000000 | bytes 72000000 | tf_op jit(solution)/shard_map/pallas_call | solution.py:478
  78.2 5.7 %collective-permute-start.7 = (bf16[216,128]{1,0:T(8,128)(2,1)S(1)}, bf16[216,128]{1,0:T(8,128)(2,1)S(1)}, u32[]{:S(2)}, u32[]{:S(2)}) collective-permute-start(bf16[216,128]{1,0:T(8,128)(2,1)S(1)} %add_convert_fusion.6), channel_id=1, source_target_pairs={{0,32},{1,33},{2,34},{3,35},{4,36},{5,37},{6,38},{7,39},{8,40},{9,... | collective-permute-start | bytes 165896 | tf_op jit(solution)/shard_map/ppermute | solution.py:508
  84.0 4.4 %shard_map.124 = (bf16[64,128]{1,0:T(8,128)(2,1)S(1)}, bf16[64,128]{1,0:T(8,128)(2,1)S(1)}) custom-call(s32[8]{0:T(128)S(1)} %pad_add_fusion.place_ref, f32[80,32,128]{2,1,0:T(8,128)S(1)} %get-tuple-element.42.grad_ref, bf16[80,32,128]{2,1,0:T(8,128)(2,1)S(1)} %get-tuple-element.43.round_ref, f32[128,128]{1,0:T(8,128)S(1)} %get-tuple-element.44.rows_ref, ...), custom_call_target="tpu_custom_call" | custom-call | flops 7000000000 | bytes 21000000 | tf_op jit(solution)/shard_map/pallas_call | solution.py:519
  88.5 4.3 %collective-permute-done.8 = bf16[280,128]{1,0:T(8,128)(2,1)S(1)} collective-permute-done((bf16[280,128]{1,0:T(8,128)(2,1)S(1)}, bf16[280,128]{1,0:T(8,128)(2,1)S(1)}, u32[]{:S(2)}, u32[]{:S(2)}) %collective-permute-start.8) | collective-permute-done | bytes 71712 | tf_op jit(solution)/shard_map/ppermute | solution.py:508
  92.9 3.6 %collective-permute-start.9 = (bf16[280,128]{1,0:T(8,128)(2,1)S(1)}, bf16[280,128]{1,0:T(8,128)(2,1)S(1)}, u32[]{:S(2)}, u32[]{:S(2)}) collective-permute-start(bf16[280,128]{1,0:T(8,128)(2,1)S(1)} %add_convert_fusion.3), channel_id=1, source_target_pairs={{0,192},{1,193},{2,194},{3,195},{4,196},{5,197},{6,198},{7,199},{8... | collective-permute-start | bytes 215048 | tf_op jit(solution)/shard_map/ppermute | solution.py:508
  97.0 1.8 %collective-permute-done.9 = bf16[280,128]{1,0:T(8,128)(2,1)S(1)} collective-permute-done((bf16[280,128]{1,0:T(8,128)(2,1)S(1)}, bf16[280,128]{1,0:T(8,128)(2,1)S(1)}, u32[]{:S(2)}, u32[]{:S(2)}) %collective-permute-start.9) | collective-permute-done | bytes 71712 | tf_op jit(solution)/shard_map/ppermute | solution.py:508
  99.5 2.3 %collective-permute-done.6 = bf16[64,128]{1,0:T(8,128)(2,1)S(1)} collective-permute-done((bf16[64,128]{1,0:T(8,128)(2,1)S(1)}, bf16[64,128]{1,0:T(8,128)(2,1)S(1)}, u32[]{:S(2)}, u32[]{:S(2)}) %collective-permute-start.6) | collective-permute-done | bytes 16416 | tf_op jit(solution)/shard_map/ppermute | solution.py:508
  101.8 2.5 %collective-permute-done.10 = bf16[216,128]{1,0:T(8,128)(2,1)S(1)} collective-permute-done((bf16[216,128]{1,0:T(8,128)(2,1)S(1)}, bf16[216,128]{1,0:T(8,128)(2,1)S(1)}, u32[]{:S(2)}, u32[]{:S(2)}) %collective-permute-start.10) | collective-permute-done | bytes 55328 | tf_op jit(solution)/shard_map/ppermute | solution.py:508
  104.5 4.9 %collective-permute-start.16 = (f32[64,64]{1,0:T(8,128)S(1)}, f32[64,64]{1,0:T(8,128)S(1)}, u32[]{:S(2)}, u32[]{:S(2)}) collective-permute-start(f32[64,64]{1,0:T(8,128)S(1)} %get-tuple-element.49.direct_ref), channel_id=1, source_target_pairs={{0,0},{1,16},{2,32},{3,48},{4,64},{5,80},{6,96},{7,112},{8,128},{9... | collective-permute-start | bytes 49160 | tf_op jit(solution)/shard_map/ppermute | solution.py:513
  109.4 2.0 %collective-permute-start.14 = (bf16[64,128]{1,0:T(8,128)(2,1)S(1)}, bf16[64,128]{1,0:T(8,128)(2,1)S(1)}, u32[]{:S(2)}, u32[]{:S(2)}) collective-permute-start(bf16[64,128]{1,0:T(8,128)(2,1)S(1)} %slice.45), channel_id=1, source_target_pairs={{0,16},{1,17},{2,18},{3,19},{4,20},{5,21},{6,22},{7,23},{8,24},{9,... | collective-permute-start | bytes 49160 | tf_op jit(solution)/shard_map/ppermute | solution.py:508
  112.7 4.7 %collective-permute-done.12 = bf16[280,128]{1,0:T(8,128)(2,1)S(1)} collective-permute-done((bf16[280,128]{1,0:T(8,128)(2,1)S(1)}, bf16[280,128]{1,0:T(8,128)(2,1)S(1)}, u32[]{:S(2)}, u32[]{:S(2)}) %collective-permute-start.12) | collective-permute-done | bytes 71712 | tf_op jit(solution)/shard_map/ppermute | solution.py:508
  117.4 6.7 %collective-permute-start.13 = (bf16[280,128]{1,0:T(8,128)(2,1)S(1)}, bf16[280,128]{1,0:T(8,128)(2,1)S(1)}, u32[]{:S(2)}, u32[]{:S(2)}) collective-permute-start(bf16[280,128]{1,0:T(8,128)(2,1)S(1)} %add_convert_fusion.mine_ref), channel_id=1, source_target_pairs={{0,12},{1,13},{2,14},{3,15},{4,8},{5,9},{6,10},{7,11},{8,4},{9,5},... | collective-permute-start | bytes 215048 | tf_op jit(solution)/shard_map/ppermute | solution.py:508
  124.1 2.7 %collective-permute-done.13.got_ref = bf16[280,128]{1,0:T(8,128)(2,1)S(1)} collective-permute-done((bf16[280,128]{1,0:T(8,128)(2,1)S(1)}, bf16[280,128]{1,0:T(8,128)(2,1)S(1)}, u32[]{:S(2)}, u32[]{:S(2)}) %collective-permute-start.13) | collective-permute-done | bytes 71712 | tf_op jit(solution)/shard_map/ppermute | solution.py:508
  (65 shorter events, 11.3 us)
Async XLA Ops:
  3.1 30.8 %copy-start.2 = (f32[64,64]{1,0:T(8,128)S(1)}, f32[64,64]{1,0:T(8,128)}, u32[]{:S(2)}) copy-start(f32[64,64]{1,0:T(8,128)} %cot_ref.3) | copy-start | bytes 49156
  4.3 32.1 %copy-start.8 = (s32[3]{0:T(128)S(1)}, s32[3]{0:T(128)}, u32[]{:S(2)}) copy-start(s32[3]{0:T(128)} %param.16) | copy-start | bytes 40
  4.3 32.1 %copy-start.7 = (bf16[3,32,288]{2,1,0:T(8,128)(2,1)S(1)}, bf16[3,32,288]{2,1,0:T(8,128)(2,1)}, u32[]{:S(2)}) copy-start(bf16[3,32,288]{2,1,0:T(8,128)(2,1)} %param.14) | copy-start | bytes 165892
  4.3 29.6 %all-to-all-start = ((bf16[256,4,128]{2,1,0:T(4,128)(2,1)}), bf16[256,4,128]{2,1,0:T(4,128)(2,1)S(1)}, u32[]{:S(2)}, u32[]{:S(2)}) async-start(bf16[256,4,128]{2,1,0:T(4,128)(2,1)} %get-tuple-element.29), calls=%async_computation | async-start | bytes 524288 | tf_op jit(solution)/shard_map/all_to_all | solution.py:449
  18.6 12.3 %collective-permute-start = (bf16[17,32,128]{2,1,0:T(8,128)(2,1)S(1)}, bf16[17,32,128]{2,1,0:T(8,128)(2,1)S(1)}, u32[]{:S(2)}, u32[]{:S(2)}) collective-permute-start(bf16[17,32,128]{2,1,0:T(8,128)(2,1)S(1)} %get-tuple-element.27), channel_id=1, source_target_pairs={{0,1},{1,2},{2,3},{3,4},{4,5},{5,6},{6,7},{7,8},{8,9},{9,10},{10,1... | collective-permute-start | bytes 417800 | tf_op jit(solution)/shard_map/ppermute | solution.py:447
  23.6 10.3 %collective-permute-start.1 = (bf16[17,32,128]{2,1,0:T(8,128)(2,1)S(1)}, bf16[17,32,128]{2,1,0:T(8,128)(2,1)S(1)}, u32[]{:S(2)}, u32[]{:S(2)}) collective-permute-start(bf16[17,32,128]{2,1,0:T(8,128)(2,1)S(1)} %get-tuple-element.28), channel_id=1, source_target_pairs={{1,0},{2,1},{3,2},{4,3},{5,4},{6,5},{7,6},{8,7},{9,8},{10,9},{11,1... | collective-permute-start | bytes 417800 | tf_op jit(solution)/shard_map/ppermute | solution.py:448
  34.2 14.5 %copy-start.3 = (bf16[128,128]{1,0:T(8,128)(2,1)S(1)}, bf16[128,128]{1,0:T(8,128)(2,1)}, u32[]{:S(2)}) copy-start(bf16[128,128]{1,0:T(8,128)(2,1)} %w_left_ref.3) | copy-start | bytes 98308
  34.2 14.5 %copy-start.4 = (bf16[128,128]{1,0:T(8,128)(2,1)S(1)}, bf16[128,128]{1,0:T(8,128)(2,1)}, u32[]{:S(2)}) copy-start(bf16[128,128]{1,0:T(8,128)(2,1)} %w_right_ref.3) | copy-start | bytes 98308
  34.2 14.5 %copy-start.5 = (bf16[32,128]{1,0:T(8,128)(2,1)S(1)}, bf16[32,128]{1,0:T(8,128)(2,1)}, u32[]{:S(2)}) copy-start(bf16[32,128]{1,0:T(8,128)(2,1)} %w_in_ref.3) | copy-start | bytes 24580
  34.3 8.9 %collective-permute-start.2 = (bf16[34,32,128]{2,1,0:T(8,128)(2,1)S(1)}, bf16[34,32,128]{2,1,0:T(8,128)(2,1)S(1)}, u32[]{:S(2)}, u32[]{:S(2)}) collective-permute-start(bf16[34,32,128]{2,1,0:T(8,128)(2,1)S(1)} %get-tuple-element.35.part2_ref), channel_id=1, source_target_pairs={{0,16},{16,32},{32,48},{48,64},{64,80},{80,96},{96,112},{112,128},... | collective-permute-start | bytes 835592 | tf_op jit(solution)/shard_map/ppermute | solution.py:455
  37.9 8.6 %collective-permute-start.3 = (bf16[34,32,128]{2,1,0:T(8,128)(2,1)S(1)}, bf16[34,32,128]{2,1,0:T(8,128)(2,1)S(1)}, u32[]{:S(2)}, u32[]{:S(2)}) collective-permute-start(bf16[34,32,128]{2,1,0:T(8,128)(2,1)S(1)} %get-tuple-element.36.part1_ref), channel_id=1, source_target_pairs={{16,0},{32,16},{48,32},{64,48},{80,64},{96,80},{112,96},{128,112},... | collective-permute-start | bytes 835592 | tf_op jit(solution)/shard_map/ppermute | solution.py:456
  46.5 9.2 %collective-permute-start.4 = (f32[128,128]{1,0:T(8,128)S(1)}, f32[128,128]{1,0:T(8,128)S(1)}, u32[]{:S(2)}, u32[]{:S(2)}) collective-permute-start(f32[128,128]{1,0:T(8,128)S(1)} %pad_maximum_fusion.2), channel_id=1, source_target_pairs={{0,0},{1,16},{2,32},{3,48},{4,64},{5,80},{6,96},{7,112},{8,128},{9... | collective-permute-start | bytes 196616 | tf_op jit(solution)/shard_map/ppermute | solution.py:470
  76.9 1.3 %collective-permute-start.5 = (bf16[216,128]{1,0:T(8,128)(2,1)S(1)}, bf16[216,128]{1,0:T(8,128)(2,1)S(1)}, u32[]{:S(2)}, u32[]{:S(2)}) collective-permute-start(bf16[216,128]{1,0:T(8,128)(2,1)S(1)} %get-tuple-element.41), channel_id=1, source_target_pairs={{0,16},{1,17},{2,18},{3,19},{4,20},{5,21},{6,22},{7,23},{8,24},{9,... | collective-permute-start | bytes 165896 | tf_op jit(solution)/shard_map/ppermute | solution.py:508
  78.2 10.2 %collective-permute-start.7 = (bf16[216,128]{1,0:T(8,128)(2,1)S(1)}, bf16[216,128]{1,0:T(8,128)(2,1)S(1)}, u32[]{:S(2)}, u32[]{:S(2)}) collective-permute-start(bf16[216,128]{1,0:T(8,128)(2,1)S(1)} %add_convert_fusion.6), channel_id=1, source_target_pairs={{0,32},{1,33},{2,34},{3,35},{4,36},{5,37},{6,38},{7,39},{8,40},{9,... | collective-permute-start | bytes 165896 | tf_op jit(solution)/shard_map/ppermute | solution.py:508
  88.4 4.4 %collective-permute-start.8 = (bf16[280,128]{1,0:T(8,128)(2,1)S(1)}, bf16[280,128]{1,0:T(8,128)(2,1)S(1)}, u32[]{:S(2)}, u32[]{:S(2)}) collective-permute-start(bf16[280,128]{1,0:T(8,128)(2,1)S(1)} %pad_maximum_fusion), channel_id=1, source_target_pairs={{0,64},{1,65},{2,66},{3,67},{4,68},{5,69},{6,70},{7,71},{8,72},{9,... | collective-permute-start | bytes 215048 | tf_op jit(solution)/shard_map/ppermute | solution.py:508
  92.9 6.0 %collective-permute-start.9 = (bf16[280,128]{1,0:T(8,128)(2,1)S(1)}, bf16[280,128]{1,0:T(8,128)(2,1)S(1)}, u32[]{:S(2)}, u32[]{:S(2)}) collective-permute-start(bf16[280,128]{1,0:T(8,128)(2,1)S(1)} %add_convert_fusion.3), channel_id=1, source_target_pairs={{0,192},{1,193},{2,194},{3,195},{4,196},{5,197},{6,198},{7,199},{8... | collective-permute-start | bytes 215048 | tf_op jit(solution)/shard_map/ppermute | solution.py:508
  96.5 5.2 %collective-permute-start.6 = (bf16[64,128]{1,0:T(8,128)(2,1)S(1)}, bf16[64,128]{1,0:T(8,128)(2,1)S(1)}, u32[]{:S(2)}, u32[]{:S(2)}) collective-permute-start(bf16[64,128]{1,0:T(8,128)(2,1)S(1)} %get-tuple-element.46), channel_id=1, source_target_pairs={{0,1},{1,0},{2,3},{3,2},{4,5},{5,4},{6,7},{7,6},{8,9},{9,8},{10,11... | collective-permute-start | bytes 49160 | tf_op jit(solution)/shard_map/ppermute | solution.py:508
  98.9 5.5 %collective-permute-start.10 = (bf16[216,128]{1,0:T(8,128)(2,1)S(1)}, bf16[216,128]{1,0:T(8,128)(2,1)S(1)}, u32[]{:S(2)}, u32[]{:S(2)}) collective-permute-start(bf16[216,128]{1,0:T(8,128)(2,1)S(1)} %slice.44), channel_id=1, source_target_pairs={{0,33},{1,32},{2,35},{3,34},{4,37},{5,36},{6,39},{7,38},{8,41},{9,... | collective-permute-start | bytes 165896 | tf_op jit(solution)/shard_map/ppermute | solution.py:508
  104.4 7.1 %collective-permute-start.11 = (bf16[280,128]{1,0:T(8,128)(2,1)S(1)}, bf16[280,128]{1,0:T(8,128)(2,1)S(1)}, u32[]{:S(2)}, u32[]{:S(2)}) collective-permute-start(bf16[280,128]{1,0:T(8,128)(2,1)S(1)} %pad_maximum_fusion.1), channel_id=1, source_target_pairs={{0,2},{1,3},{2,0},{3,1},{4,6},{5,7},{6,4},{7,5},{8,10},{9,11},{10,... | collective-permute-start | bytes 215048 | tf_op jit(solution)/shard_map/ppermute | solution.py:508
  104.5 19.6 %collective-permute-start.16 = (f32[64,64]{1,0:T(8,128)S(1)}, f32[64,64]{1,0:T(8,128)S(1)}, u32[]{:S(2)}, u32[]{:S(2)}) collective-permute-start(f32[64,64]{1,0:T(8,128)S(1)} %get-tuple-element.49.direct_ref), channel_id=1, source_target_pairs={{0,0},{1,16},{2,32},{3,48},{4,64},{5,80},{6,96},{7,112},{8,128},{9... | collective-permute-start | bytes 49160 | tf_op jit(solution)/shard_map/ppermute | solution.py:513
  109.4 2.9 %collective-permute-start.14 = (bf16[64,128]{1,0:T(8,128)(2,1)S(1)}, bf16[64,128]{1,0:T(8,128)(2,1)S(1)}, u32[]{:S(2)}, u32[]{:S(2)}) collective-permute-start(bf16[64,128]{1,0:T(8,128)(2,1)S(1)} %slice.45), channel_id=1, source_target_pairs={{0,16},{1,17},{2,18},{3,19},{4,20},{5,21},{6,22},{7,23},{8,24},{9,... | collective-permute-start | bytes 49160 | tf_op jit(solution)/shard_map/ppermute | solution.py:508
  111.5 5.9 %collective-permute-start.12 = (bf16[280,128]{1,0:T(8,128)(2,1)S(1)}, bf16[280,128]{1,0:T(8,128)(2,1)S(1)}, u32[]{:S(2)}, u32[]{:S(2)}) collective-permute-start(bf16[280,128]{1,0:T(8,128)(2,1)S(1)} %add_convert_fusion.1), channel_id=1, source_target_pairs={{0,4},{1,5},{2,6},{3,7},{4,0},{5,1},{6,2},{7,3},{8,12},{9,13},{10,... | collective-permute-start | bytes 215048 | tf_op jit(solution)/shard_map/ppermute | solution.py:508
  112.3 11.8 %collective-permute-start.15 = (bf16[64,128]{1,0:T(8,128)(2,1)S(1)}, bf16[64,128]{1,0:T(8,128)(2,1)S(1)}, u32[]{:S(2)}, u32[]{:S(2)}) collective-permute-start(bf16[64,128]{1,0:T(8,128)(2,1)S(1)} %add_convert_fusion.8), channel_id=1, source_target_pairs={{0,32},{1,33},{2,34},{3,35},{4,36},{5,37},{6,38},{7,39},{8,40},{9,... | collective-permute-start | bytes 49160 | tf_op jit(solution)/shard_map/ppermute | solution.py:508
  117.4 9.4 %collective-permute-start.13 = (bf16[280,128]{1,0:T(8,128)(2,1)S(1)}, bf16[280,128]{1,0:T(8,128)(2,1)S(1)}, u32[]{:S(2)}, u32[]{:S(2)}) collective-permute-start(bf16[280,128]{1,0:T(8,128)(2,1)S(1)} %add_convert_fusion.mine_ref), channel_id=1, source_target_pairs={{0,12},{1,13},{2,14},{3,15},{4,8},{5,9},{6,10},{7,11},{8,4},{9,5},... | collective-permute-start | bytes 215048 | tf_op jit(solution)/shard_map/ppermute | solution.py:508
  (4 other events, 11.7 us)

commit v4 on v3

--- a/solution.py
+++ b/solution.py
@@ -39,11 +39,17 @@
     return high, (value - high.astype(F32)).astype(BF16)
 
 
-def edges_kernel(pair_ref, cot_ref, feat_ref, own_ref, left_ref, right_ref, sent_ref):
+def spread_kernel(feat_ref, sent_ref):
     sent_ref[...] = jnp.broadcast_to(feat_ref[...][None], sent_ref.shape)
+
+
+def edges_kernel(
+    pair_ref, cot_ref, mirror_ref, own_ref, left_ref, right_ref, upstream_ref
+):
     own = jnp.swapaxes(pair_ref[...].astype(F32), 0, 1)
     own_ref[...] = own.astype(BF16)
-    cot = cot_ref[...]
+    cot = 0.5 * (cot_ref[...] + mirror_ref[...].T)
+    upstream_ref[...] = cot
     for out_ref, first in ((left_ref, 0), (right_ref, TILE - HALO)):
         last = first + HALO
         for q in range(16):
@@ -56,8 +62,8 @@
         out_ref[16, 16:32, :] = low
 
 
-def widen_kernel(own_ref, cot_ref, from_left_ref, from_right_ref, upper_ref, lower_ref):
-    cot = cot_ref[...]
+def widen_kernel(own_ref, upstream_ref, from_left_ref, from_right_ref, upper_ref, lower_ref):
+    cot = upstream_ref[...]
     for m in range(4):
         out_ref = (upper_ref, lower_ref)[m // 2]
         lanes = slice(HALO * m, HALO * m + HALO)
@@ -83,7 +89,10 @@
             ).astype(BF16)
 
 
-def mixed_kernel(place_ref, feat_ref, w_left_ref, w_right_ref, w_in_ref, mixed_ref, rows_ref, cols_ref, picked_ref):
+def mixed_kernel(
+    place_ref, feat_ref, w_left_ref, w_right_ref, w_in_ref, conv_ref,
+    mixed_ref, rows_ref, cols_ref, forward_ref, backward_ref, picked_ref,
+):
     row = place_ref[0]
     col = place_ref[1]
     row_chunks = [jnp.maximum(2 * row - 1, 0), 2 * row, 2 * row + 1, jnp.minimum(2 * row + 2, 31)]
@@ -99,6 +108,16 @@
         out_ref[...] = jnp.dot(
             picked_ref[...].astype(BF16), weight_ref[...], preferred_element_type=F32
         )
+    for layer in range(3):
+        weight = conv_ref[layer].astype(F32)
+        turned = jnp.concatenate([weight, jnp.zeros((CH, 96), F32)], axis=1)
+        turned = jnp.concatenate([turned[:, 128 * k : 128 * k + 128].T for k in range(3)], axis=0)
+        for a in range(3):
+            forward_ref[layer, CH * a : CH * a + CH, :] = weight[:, 96 * a : 96 * a + 96].astype(BF16)
+            taps = [8 - 3 * a - b for b in range(3)]
+            backward_ref[layer, CH * a : CH * a + CH, :] = jnp.concatenate(
+                [turned[CH * tap : CH * tap + CH] for tap in taps], axis=1
+            ).astype(BF16)
     w_in = w_in_ref[...]
 
     def body(step, carry):
@@ -170,7 +189,6 @@
     part1_ref,
     part2_ref,
     part3_ref,
-    mirror_ref,
     forward_ref,
     backward_ref,
     w_out_ref,
@@ -242,13 +260,8 @@
 
     lax.fori_loop(0, TILE // ROWS, finish, 0)
 
-    other = mirror_ref[...].T
-    other = jnp.concatenate([other[96:128], other[0:96]], axis=0)
-    other = jnp.concatenate([other[:, 32:128], other[:, 0:32]], axis=1)
     for n in range(4):
-        mine = parts[n][32].astype(F32) + parts[n][33].astype(F32)
-        rows = slice(HALO * n, HALO * n + HALO)
-        upstream_ref[rows, :] = 0.5 * (mine + other[rows, :])
+        upstream_ref[HALO * n : HALO * n + HALO, :] = parts[n][32].astype(F32) + parts[n][33].astype(F32)
 
     tile_lanes = jnp.where(lax.broadcasted_iota(jnp.int32, (1, WIDE), 1) < TILE, 1.0, 0.0).astype(F32)
     masked_ref[...] = jnp.zeros_like(masked_ref)
@@ -437,48 +450,47 @@
     down = [(i + 1, i) for i in range(n_row - 1)]
     swap = [(r * n_col + c, c * n_col + r) for r in range(n_row) for c in range(n_col)]
 
-    own, left_edge, right_edge, sent = call(
+    mirrored = lax.ppermute(cotangent, ("row", "col"), swap)
+    (sent,) = call(
+        spread_kernel, [shape(n_row * n_col, *features.shape, dtype=BF16)], [VMEM]
+    )(features)
+    gathered = lax.all_to_all(sent, ("row", "col"), 0, 0)
+    own, left_edge, right_edge, upstream = call(
         edges_kernel,
         [shape(TILE, CH, TILE, dtype=BF16)]
         + [shape(17, CH, WIDE, dtype=BF16)] * 2
-        + [shape(n_row * n_col, *features.shape, dtype=BF16)],
+        + [shape(TILE, TILE)],
         [VMEM] * 3,
-    )(pair_input, cotangent, features)
+        (),
+        8,
+        12,
+    )(pair_input, cotangent, mirrored)
     from_left = lax.ppermute(right_edge, "col", up)
     from_right = lax.ppermute(left_edge, "col", down)
-    gathered = lax.all_to_all(sent, ("row", "col"), 0, 0)
-    from_left, from_right, gathered = lax.optimization_barrier((from_left, from_right, gathered))
-
-    upper, lower = call(
-        widen_kernel, [shape(HALO + 2, CH, WIDE, dtype=BF16)] * 2, [VMEM] * 4
-    )(own, cotangent, from_left, from_right)
-    above = lax.ppermute(lower, "row", up)
-    below = lax.ppermute(upper, "row", down)
-
-    mixed, row_project, col_project = call(
+
+    mixed, row_project, col_project, forward_w, backward_w = call(
         mixed_kernel,
-        [shape(WIDE, CH, WIDE), shape(WIDE, 128), shape(WIDE, 128)],
-        [SMEM] + [VMEM] * 4,
+        [shape(WIDE, CH, WIDE), shape(WIDE, 128), shape(WIDE, 128)]
+        + [shape(3, 96, 96, dtype=BF16)] * 2,
+        [SMEM] + [VMEM] * 5,
         [pltpu.VMEM((WIDE, 128), F32)],
         16,
         6,
-    )(place, gathered, w_left, w_right, w_in)
-
-    wide_cot = jnp.concatenate(
-        [part[32].astype(F32) + part[33].astype(F32) for part in (above, upper, lower, below)], axis=0
-    )
-    mirrored = lax.ppermute(wide_cot, ("row", "col"), swap)
-
-    forward_w = conv_w.reshape(3, CH, 3, 3 * CH).transpose(0, 2, 1, 3).reshape(3, 96, 96)
-    backward_w = (
-        conv_w.reshape(3, CH, 3, 3, CH)[:, :, ::-1, ::-1, :].transpose(0, 2, 4, 3, 1).reshape(3, 96, 96)
-    )
+    )(place, gathered, w_left, w_right, w_in, conv_w)
+    from_left, from_right, mixed = lax.optimization_barrier((from_left, from_right, mixed))
+
+    upper, lower = call(
+        widen_kernel, [shape(HALO + 2, CH, WIDE, dtype=BF16)] * 2, [VMEM] * 4
+    )(own, upstream, from_left, from_right)
+    above = lax.ppermute(lower, "row", up)
+    below = lax.ppermute(upper, "row", down)
+
     w_out_wide = jnp.broadcast_to(w_out.astype(F32)[:, None], (CH, WIDE))
     big = (WIDE, CH, WIDE)
     direct, terms, grad, rounded = call(
         main_kernel,
         [shape(TILE, TILE), shape(216, 128, dtype=BF16), shape(80, CH, WIDE), shape(80, CH, WIDE, dtype=BF16)],
-        [SMEM] + [VMEM] * 9,
+        [SMEM] + [VMEM] * 8,
         [
             pltpu.VMEM(big, BF16),
             pltpu.VMEM(big, F32),
@@ -497,7 +509,7 @@
         ],
         42,
         24,
-    )(place, mixed, above, upper, lower, below, mirrored, forward_w, backward_w, w_out_wide)
+    )(place, mixed, above, upper, lower, below, forward_w, backward_w, w_out_wide)
 
     def flipped(value, row_bits, col_bits):
         pairs = [

time: 129 us -> 117 us (0.907); the launches traced: 128 us -> 117 us
  waiting for transfers between devices: 33.5 us -> 28.8 us
  local copies, waits for them, and re-layouts: 3.96 us -> 0.79 us
  starting transfers between devices: 56.5 us -> 53.6 us
    all_to_all x1, waiting for transfers between devices: 0.01 us -> 5.59 us  [on_device(): gathered = lax.all_to_all(sent, ('row', 'col'), 0, 0)]
    ppermute x1, waiting for transfers between devices: 4.01 us -> 0.01 us  [on_device(): from_left = lax.ppermute(right_edge, 'col', up)]
    ppermute x11, starting transfers between devices: 20.2 us -> 17 us  [flipped(): return lax.ppermute(value, ('row', 'col'), pairs)]
    ppermute x1, waiting for transfers between devices: 2.96 us -> 0.01 us  [on_device(): from_right = lax.ppermute(left_edge, 'col', down)]
    ppermute x1, starting transfers between devices: 2.25 us -> 4.77 us  [on_device(): mirrored = lax.ppermute(cotangent, ('row', 'col'), swap)]
    ppermute x1, waiting for transfers between devices: 2.51 us -> 0.01 us  [on_device(): mirrored = lax.ppermute(cotangent, ('row', 'col'), swap)]
    unnamed x20 -> x18, local copies, waits for them, and re-layouts: 2.51 us -> 0.71 us
    ppermute x1, starting transfers between devices: 4.9 us -> 3.13 us  [on_device(): direct_other = lax.ppermute(direct, ('row', 'col'), swap)]
  transfers between devices with their start and end apart: 18 -> 18, of which waited for: 13 -> 11; matrix products, arithmetic and copies ran while one was open for 1% -> 0% of each run, Pallas kernels for 7% -> 9%
where the time goes in v4:
time: 117 us
  starting transfers between devices  53.6 us (46%)
  Pallas kernels  32.6 us (28%)
  waiting for transfers between devices  28.8 us (25%)
    pallas_call x1, Pallas kernels, on_device(): call(main_kernel, [shape(TILE, TILE), shape(216, 128, dtype=BF16), shape(...  21.1 us
    ppermute x11, waiting for transfers between devices, flipped(): return lax.ppermute(value, ('row', 'col'), pairs)  19.2 us
    ppermute x11, starting transfers between devices, flipped(): return lax.ppermute(value, ('row', 'col'), pairs)  17 us
    all_to_all x1, starting transfers between devices, on_device(): gathered = lax.all_to_all(sent, ('row', 'col'), 0, 0)  14 us
    all_to_all x1, waiting for transfers between devices, on_device(): gathered = lax.all_to_all(sent, ('row', 'col'), 0, 0)  5.59 us
    ppermute x1, starting transfers between devices, on_device(): from_left = lax.ppermute(right_edge, 'col', up)  4.91 us
    ppermute x1, starting transfers between devices, on_device(): mirrored = lax.ppermute(cotangent, ('row', 'col'), swap)  4.77 us
    ppermute x1, starting transfers between devices, on_device(): below = lax.ppermute(upper, 'row', down)  4.54 us
  transfers between devices with their start and end apart: 18, of which 11 were waited for; matrix products, arithmetic and copies ran while one was open for 0% of the time, Pallas kernels for 9%

profile of v4, /device:TPU:40, one launch (start us, length us, event | category | flops | bytes accessed | tf_op | source)
XLA Modules:
  0.0 117.0 jit_solution(16373766237809493148)
XLA Ops:
  0.7 4.8 %collective-permute-start = (f32[64,64]{1,0:T(8,128)}, f32[64,64]{1,0:T(8,128)S(1)}, u32[]{:S(2)}, u32[]{:S(2)}) collective-permute-start(f32[64,64]{1,0:T(8,128)} %cot_ref.1), channel_id=1, source_target_pairs={{0,0},{1,16},{2,32},{3,48},{4,64},{5,80},{6,96},{7,112},{8,128},{9... | collective-permute-start | bytes 49160 | tf_op jit(solution)/shard_map/ppermute | solution.py:453
  6.9 14.0 %all-to-all-start = ((bf16[256,4,128]{2,1,0:T(4,128)(2,1)}), bf16[256,4,128]{2,1,0:T(4,128)(2,1)S(1)}, u32[]{:S(2)}, u32[]{:S(2)}) async-start(bf16[256,4,128]{2,1,0:T(4,128)(2,1)} %shard_map.121), calls=%async_computation | async-start | bytes 524288 | tf_op jit(solution)/shard_map/all_to_all | solution.py:457
  21.6 4.9 %collective-permute-start.1 = (bf16[17,32,128]{2,1,0:T(8,128)(2,1)S(1)}, bf16[17,32,128]{2,1,0:T(8,128)(2,1)S(1)}, u32[]{:S(2)}, u32[]{:S(2)}) collective-permute-start(bf16[17,32,128]{2,1,0:T(8,128)(2,1)S(1)} %get-tuple-element.29), channel_id=1, source_target_pairs={{0,1},{1,2},{2,3},{3,4},{4,5},{5,6},{6,7},{7,8},{8,9},{9,10},{10,1... | collective-permute-start | bytes 417800 | tf_op jit(solution)/shard_map/ppermute | solution.py:468
  26.5 3.3 %collective-permute-start.2 = (bf16[17,32,128]{2,1,0:T(8,128)(2,1)S(1)}, bf16[17,32,128]{2,1,0:T(8,128)(2,1)S(1)}, u32[]{:S(2)}, u32[]{:S(2)}) collective-permute-start(bf16[17,32,128]{2,1,0:T(8,128)(2,1)S(1)} %get-tuple-element.30), channel_id=1, source_target_pairs={{1,0},{2,1},{3,2},{4,3},{5,4},{6,5},{7,6},{8,7},{9,8},{10,9},{11,1... | collective-permute-start | bytes 417800 | tf_op jit(solution)/shard_map/ppermute | solution.py:469
  29.9 5.6 %all-to-all-done.feat_ref = bf16[256,4,128]{2,1,0:T(4,128)(2,1)S(1)} async-done(((bf16[256,4,128]{2,1,0:T(4,128)(2,1)}), bf16[256,4,128]{2,1,0:T(4,128)(2,1)S(1)}, u32[]{:S(2)}, u32[]{:S(2)}) %all-to-all-start) | async-done | bytes 262176 | tf_op jit(solution)/shard_map/all_to_all | solution.py:457
  35.5 4.5 %shard_map.122 = (f32[128,32,128]{2,1,0:T(8,128)S(1)}, f32[128,128]{1,0:T(8,128)S(1)}, f32[128,128]{1,0:T(8,128)S(1)}, bf16[3,96,96]{2,1,0:T(8,128)(2,1)S(1)}, bf16[3,96,96]{2,1,0:T(8,128)(2,1)S(1)}) custom-call(s32[8]{0:T(128)S(1)} %pad_add_fusion.place_ref, bf16[256,4,128]{2,1,0:T(4,128)(2,1)S(1)} %all-to-all-done.feat_ref, ...), custom_call_target="tpu_custom_call" | custom-call | flops 6000000000 | bytes 18000000 | tf_op jit(solution)/shard_map/pallas_call | solution.py:471
  40.4 1.9 %collective-permute-start.3 = (bf16[34,32,128]{2,1,0:T(8,128)(2,1)S(1)}, bf16[34,32,128]{2,1,0:T(8,128)(2,1)S(1)}, u32[]{:S(2)}, u32[]{:S(2)}) collective-permute-start(bf16[34,32,128]{2,1,0:T(8,128)(2,1)S(1)} %get-tuple-element.37.part2_ref), channel_id=1, source_target_pairs={{0,16},{16,32},{32,48},{48,64},{64,80},{80,96},{96,112},{112,128},... | collective-permute-start | bytes 835592 | tf_op jit(solution)/shard_map/ppermute | solution.py:485
  42.3 4.5 %collective-permute-start.4 = (bf16[34,32,128]{2,1,0:T(8,128)(2,1)S(1)}, bf16[34,32,128]{2,1,0:T(8,128)(2,1)S(1)}, u32[]{:S(2)}, u32[]{:S(2)}) collective-permute-start(bf16[34,32,128]{2,1,0:T(8,128)(2,1)S(1)} %get-tuple-element.38.part1_ref), channel_id=1, source_target_pairs={{16,0},{32,16},{48,32},{64,48},{80,64},{96,80},{112,96},{128,112},... | collective-permute-start | bytes 835592 | tf_op jit(solution)/shard_map/ppermute | solution.py:486
  46.9 2.4 %collective-permute-done.3.part0_ref = bf16[34,32,128]{2,1,0:T(8,128)(2,1)S(1)} collective-permute-done((bf16[34,32,128]{2,1,0:T(8,128)(2,1)S(1)}, bf16[34,32,128]{2,1,0:T(8,128)(2,1)S(1)}, u32[]{:S(2)}, u32[]{:S(2)}) %collective-permute-start.3) | collective-permute-done | bytes 278560 | tf_op jit(solution)/shard_map/ppermute | solution.py:485
  49.2 1.7 %collective-permute-done.4.part3_ref = bf16[34,32,128]{2,1,0:T(8,128)(2,1)S(1)} collective-permute-done((bf16[34,32,128]{2,1,0:T(8,128)(2,1)S(1)}, bf16[34,32,128]{2,1,0:T(8,128)(2,1)S(1)}, u32[]{:S(2)}, u32[]{:S(2)}) %collective-permute-start.4) | collective-permute-done | bytes 278560 | tf_op jit(solution)/shard_map/ppermute | solution.py:486
  51.0 21.1 %shard_map.124 = (f32[64,64]{1,0:T(8,128)S(1)}, bf16[216,128]{1,0:T(8,128)(2,1)S(1)}, f32[80,32,128]{2,1,0:T(8,128)S(1)}, bf16[80,32,128]{2,1,0:T(8,128)(2,1)S(1)}) custom-call(s32[8]{0:T(128)S(1)} %pad_add_fusion.place_ref, f32[128,32,128]{2,1,0:T(8,128)S(1)} %get-tuple-element.32.mixed_ref, bf16[34,32,128]{2,1,0:T(8,128)(2,1)S(1)} %collective-permute-done.3.part0_ref, ...), custom_call_target="tpu_custom_call" | custom-call | flops 24000000000 | bytes 72000000 | tf_op jit(solution)/shard_map/pallas_call | solution.py:490
  73.4 1.7 %collective-permute-start.7 = (bf16[216,128]{1,0:T(8,128)(2,1)S(1)}, bf16[216,128]{1,0:T(8,128)(2,1)S(1)}, u32[]{:S(2)}, u32[]{:S(2)}) collective-permute-start(bf16[216,128]{1,0:T(8,128)(2,1)S(1)} %add_convert_fusion.6), channel_id=1, source_target_pairs={{0,32},{1,33},{2,34},{3,35},{4,36},{5,37},{6,38},{7,39},{8,40},{9,... | collective-permute-start | bytes 165896 | tf_op jit(solution)/shard_map/ppermute | solution.py:520
  75.1 4.4 %shard_map.125 = (bf16[64,128]{1,0:T(8,128)(2,1)S(1)}, bf16[64,128]{1,0:T(8,128)(2,1)S(1)}) custom-call(s32[8]{0:T(128)S(1)} %pad_add_fusion.place_ref, f32[80,32,128]{2,1,0:T(8,128)S(1)} %get-tuple-element.46.grad_ref, bf16[80,32,128]{2,1,0:T(8,128)(2,1)S(1)} %get-tuple-element.47.round_ref, f32[128,128]{1,0:T(8,128)S(1)} %get-tuple-element.48.rows_ref, ...), custom_call_target="tpu_custom_call" | custom-call | flops 7000000000 | bytes 21000000 | tf_op jit(solution)/shard_map/pallas_call | solution.py:531
  79.6 1.8 %collective-permute-start.8 = (bf16[280,128]{1,0:T(8,128)(2,1)S(1)}, bf16[280,128]{1,0:T(8,128)(2,1)S(1)}, u32[]{:S(2)}, u32[]{:S(2)}) collective-permute-start(bf16[280,128]{1,0:T(8,128)(2,1)S(1)} %pad_maximum_fusion), channel_id=1, source_target_pairs={{0,64},{1,65},{2,66},{3,67},{4,68},{5,69},{6,70},{7,71},{8,72},{9,... | collective-permute-start | bytes 215048 | tf_op jit(solution)/shard_map/ppermute | solution.py:520
  81.4 2.6 %collective-permute-done.8 = bf16[280,128]{1,0:T(8,128)(2,1)S(1)} collective-permute-done((bf16[280,128]{1,0:T(8,128)(2,1)S(1)}, bf16[280,128]{1,0:T(8,128)(2,1)S(1)}, u32[]{:S(2)}, u32[]{:S(2)}) %collective-permute-start.8) | collective-permute-done | bytes 71712 | tf_op jit(solution)/shard_map/ppermute | solution.py:520
  84.1 1.7 %collective-permute-start.9 = (bf16[280,128]{1,0:T(8,128)(2,1)S(1)}, bf16[280,128]{1,0:T(8,128)(2,1)S(1)}, u32[]{:S(2)}, u32[]{:S(2)}) collective-permute-start(bf16[280,128]{1,0:T(8,128)(2,1)S(1)} %add_convert_fusion.3), channel_id=1, source_target_pairs={{0,192},{1,193},{2,194},{3,195},{4,196},{5,197},{6,198},{7,199},{8... | collective-permute-start | bytes 215048 | tf_op jit(solution)/shard_map/ppermute | solution.py:520
  86.9 1.6 %collective-permute-done.9 = bf16[280,128]{1,0:T(8,128)(2,1)S(1)} collective-permute-done((bf16[280,128]{1,0:T(8,128)(2,1)S(1)}, bf16[280,128]{1,0:T(8,128)(2,1)S(1)}, u32[]{:S(2)}, u32[]{:S(2)}) %collective-permute-start.9) | collective-permute-done | bytes 71712 | tf_op jit(solution)/shard_map/ppermute | solution.py:520
  88.7 2.3 %collective-permute-done.6 = bf16[64,128]{1,0:T(8,128)(2,1)S(1)} collective-permute-done((bf16[64,128]{1,0:T(8,128)(2,1)S(1)}, bf16[64,128]{1,0:T(8,128)(2,1)S(1)}, u32[]{:S(2)}, u32[]{:S(2)}) %collective-permute-start.6) | collective-permute-done | bytes 16416 | tf_op jit(solution)/shard_map/ppermute | solution.py:520
  91.0 3.0 %collective-permute-done.10 = bf16[216,128]{1,0:T(8,128)(2,1)S(1)} collective-permute-done((bf16[216,128]{1,0:T(8,128)(2,1)S(1)}, bf16[216,128]{1,0:T(8,128)(2,1)S(1)}, u32[]{:S(2)}, u32[]{:S(2)}) %collective-permute-start.10) | collective-permute-done | bytes 55328 | tf_op jit(solution)/shard_map/ppermute | solution.py:520
  95.4 3.1 %collective-permute-start.16 = (f32[64,64]{1,0:T(8,128)S(1)}, f32[64,64]{1,0:T(8,128)S(1)}, u32[]{:S(2)}, u32[]{:S(2)}) collective-permute-start(f32[64,64]{1,0:T(8,128)S(1)} %get-tuple-element.53.direct_ref), channel_id=1, source_target_pairs={{0,0},{1,16},{2,32},{3,48},{4,64},{5,80},{6,96},{7,112},{8,128},{9... | collective-permute-start | bytes 49160 | tf_op jit(solution)/shard_map/ppermute | solution.py:525
  98.6 2.2 %collective-permute-start.14 = (bf16[64,128]{1,0:T(8,128)(2,1)S(1)}, bf16[64,128]{1,0:T(8,128)(2,1)S(1)}, u32[]{:S(2)}, u32[]{:S(2)}) collective-permute-start(bf16[64,128]{1,0:T(8,128)(2,1)S(1)} %slice.9), channel_id=1, source_target_pairs={{0,16},{1,17},{2,18},{3,19},{4,20},{5,21},{6,22},{7,23},{8,24},{9,... | collective-permute-start | bytes 49160 | tf_op jit(solution)/shard_map/ppermute | solution.py:520
  102.0 4.6 %collective-permute-done.12 = bf16[280,128]{1,0:T(8,128)(2,1)S(1)} collective-permute-done((bf16[280,128]{1,0:T(8,128)(2,1)S(1)}, bf16[280,128]{1,0:T(8,128)(2,1)S(1)}, u32[]{:S(2)}, u32[]{:S(2)}) %collective-permute-start.12) | collective-permute-done | bytes 71712 | tf_op jit(solution)/shard_map/ppermute | solution.py:520
  106.7 5.8 %collective-permute-start.13 = (bf16[280,128]{1,0:T(8,128)(2,1)S(1)}, bf16[280,128]{1,0:T(8,128)(2,1)S(1)}, u32[]{:S(2)}, u32[]{:S(2)}) collective-permute-start(bf16[280,128]{1,0:T(8,128)(2,1)S(1)} %add_convert_fusion.mine_ref), channel_id=1, source_target_pairs={{0,12},{1,13},{2,14},{3,15},{4,8},{5,9},{6,10},{7,11},{8,4},{9,5},... | collective-permute-start | bytes 215048 | tf_op jit(solution)/shard_map/ppermute | solution.py:520
  112.5 3.6 %collective-permute-done.13.got_ref = bf16[280,128]{1,0:T(8,128)(2,1)S(1)} collective-permute-done((bf16[280,128]{1,0:T(8,128)(2,1)S(1)}, bf16[280,128]{1,0:T(8,128)(2,1)S(1)}, u32[]{:S(2)}, u32[]{:S(2)}) %collective-permute-start.13) | collective-permute-done | bytes 71712 | tf_op jit(solution)/shard_map/ppermute | solution.py:520
  (54 shorter events, 9.0 us)
Async XLA Ops:
  0.6 20.4 %copy-start.2 = (f32[64,64]{1,0:T(8,128)S(1)}, f32[64,64]{1,0:T(8,128)}, u32[]{:S(2)}) copy-start(f32[64,64]{1,0:T(8,128)} %cot_ref.1) | copy-start | bytes 49156
  0.6 20.4 %copy-start = (bf16[32,64,64]{2,1,0:T(8,128)(2,1)S(1)}, bf16[32,64,64]{2,1,0:T(8,128)(2,1)}, u32[]{:S(2)}) copy-start(bf16[32,64,64]{2,1,0:T(8,128)(2,1)} %pair_ref.1) | copy-start | bytes 786436
  0.7 20.4 %collective-permute-start = (f32[64,64]{1,0:T(8,128)}, f32[64,64]{1,0:T(8,128)S(1)}, u32[]{:S(2)}, u32[]{:S(2)}) collective-permute-start(f32[64,64]{1,0:T(8,128)} %cot_ref.1), channel_id=1, source_target_pairs={{0,0},{1,16},{2,32},{3,48},{4,64},{5,80},{6,96},{7,112},{8,128},{9... | collective-permute-start | bytes 49160 | tf_op jit(solution)/shard_map/ppermute | solution.py:453
  6.1 14.8 %copy-start.7 = (s32[3]{0:T(128)S(1)}, s32[3]{0:T(128)}, u32[]{:S(2)}) copy-start(s32[3]{0:T(128)} %param.16) | copy-start | bytes 40
  6.9 28.6 %all-to-all-start = ((bf16[256,4,128]{2,1,0:T(4,128)(2,1)}), bf16[256,4,128]{2,1,0:T(4,128)(2,1)S(1)}, u32[]{:S(2)}, u32[]{:S(2)}) async-start(bf16[256,4,128]{2,1,0:T(4,128)(2,1)} %shard_map.121), calls=%async_computation | async-start | bytes 524288 | tf_op jit(solution)/shard_map/all_to_all | solution.py:457
  21.0 14.4 %copy-start.3 = (bf16[128,128]{1,0:T(8,128)(2,1)S(1)}, bf16[128,128]{1,0:T(8,128)(2,1)}, u32[]{:S(2)}) copy-start(bf16[128,128]{1,0:T(8,128)(2,1)} %w_left_ref.3) | copy-start | bytes 98308
  21.0 14.4 %copy-start.4 = (bf16[128,128]{1,0:T(8,128)(2,1)S(1)}, bf16[128,128]{1,0:T(8,128)(2,1)}, u32[]{:S(2)}) copy-start(bf16[128,128]{1,0:T(8,128)(2,1)} %w_right_ref.3) | copy-start | bytes 98308
  21.0 14.4 %copy-start.5 = (bf16[32,128]{1,0:T(8,128)(2,1)S(1)}, bf16[32,128]{1,0:T(8,128)(2,1)}, u32[]{:S(2)}) copy-start(bf16[32,128]{1,0:T(8,128)(2,1)} %w_in_ref.3) | copy-start | bytes 24580
  21.6 18.4 %collective-permute-start.1 = (bf16[17,32,128]{2,1,0:T(8,128)(2,1)S(1)}, bf16[17,32,128]{2,1,0:T(8,128)(2,1)S(1)}, u32[]{:S(2)}, u32[]{:S(2)}) collective-permute-start(bf16[17,32,128]{2,1,0:T(8,128)(2,1)S(1)} %get-tuple-element.29), channel_id=1, source_target_pairs={{0,1},{1,2},{2,3},{3,4},{4,5},{5,6},{6,7},{7,8},{8,9},{9,10},{10,1... | collective-permute-start | bytes 417800 | tf_op jit(solution)/shard_map/ppermute | solution.py:468
  26.5 13.5 %collective-permute-start.2 = (bf16[17,32,128]{2,1,0:T(8,128)(2,1)S(1)}, bf16[17,32,128]{2,1,0:T(8,128)(2,1)S(1)}, u32[]{:S(2)}, u32[]{:S(2)}) collective-permute-start(bf16[17,32,128]{2,1,0:T(8,128)(2,1)S(1)} %get-tuple-element.30), channel_id=1, source_target_pairs={{1,0},{2,1},{3,2},{4,3},{5,4},{6,5},{7,6},{8,7},{9,8},{10,9},{11,1... | collective-permute-start | bytes 417800 | tf_op jit(solution)/shard_map/ppermute | solution.py:469
  40.4 8.8 %collective-permute-start.3 = (bf16[34,32,128]{2,1,0:T(8,128)(2,1)S(1)}, bf16[34,32,128]{2,1,0:T(8,128)(2,1)S(1)}, u32[]{:S(2)}, u32[]{:S(2)}) collective-permute-start(bf16[34,32,128]{2,1,0:T(8,128)(2,1)S(1)} %get-tuple-element.37.part2_ref), channel_id=1, source_target_pairs={{0,16},{16,32},{32,48},{48,64},{64,80},{80,96},{96,112},{112,128},... | collective-permute-start | bytes 835592 | tf_op jit(solution)/shard_map/ppermute | solution.py:485
  42.3 8.6 %collective-permute-start.4 = (bf16[34,32,128]{2,1,0:T(8,128)(2,1)S(1)}, bf16[34,32,128]{2,1,0:T(8,128)(2,1)S(1)}, u32[]{:S(2)}, u32[]{:S(2)}) collective-permute-start(bf16[34,32,128]{2,1,0:T(8,128)(2,1)S(1)} %get-tuple-element.38.part1_ref), channel_id=1, source_target_pairs={{16,0},{32,16},{48,32},{64,48},{80,64},{96,80},{112,96},{128,112},... | collective-permute-start | bytes 835592 | tf_op jit(solution)/shard_map/ppermute | solution.py:486
  72.0 1.3 %collective-permute-start.5 = (bf16[216,128]{1,0:T(8,128)(2,1)S(1)}, bf16[216,128]{1,0:T(8,128)(2,1)S(1)}, u32[]{:S(2)}, u32[]{:S(2)}) collective-permute-start(bf16[216,128]{1,0:T(8,128)(2,1)S(1)} %get-tuple-element.45), channel_id=1, source_target_pairs={{0,16},{1,17},{2,18},{3,19},{4,20},{5,21},{6,22},{7,23},{8,24},{9,... | collective-permute-start | bytes 165896 | tf_op jit(solution)/shard_map/ppermute | solution.py:520
  73.4 6.2 %collective-permute-start.7 = (bf16[216,128]{1,0:T(8,128)(2,1)S(1)}, bf16[216,128]{1,0:T(8,128)(2,1)S(1)}, u32[]{:S(2)}, u32[]{:S(2)}) collective-permute-start(bf16[216,128]{1,0:T(8,128)(2,1)S(1)} %add_convert_fusion.6), channel_id=1, source_target_pairs={{0,32},{1,33},{2,34},{3,35},{4,36},{5,37},{6,38},{7,39},{8,40},{9,... | collective-permute-start | bytes 165896 | tf_op jit(solution)/shard_map/ppermute | solution.py:520
  79.6 4.4 %collective-permute-start.8 = (bf16[280,128]{1,0:T(8,128)(2,1)S(1)}, bf16[280,128]{1,0:T(8,128)(2,1)S(1)}, u32[]{:S(2)}, u32[]{:S(2)}) collective-permute-start(bf16[280,128]{1,0:T(8,128)(2,1)S(1)} %pad_maximum_fusion), channel_id=1, source_target_pairs={{0,64},{1,65},{2,66},{3,67},{4,68},{5,69},{6,70},{7,71},{8,72},{9,... | collective-permute-start | bytes 215048 | tf_op jit(solution)/shard_map/ppermute | solution.py:520
  84.1 4.4 %collective-permute-start.9 = (bf16[280,128]{1,0:T(8,128)(2,1)S(1)}, bf16[280,128]{1,0:T(8,128)(2,1)S(1)}, u32[]{:S(2)}, u32[]{:S(2)}) collective-permute-start(bf16[280,128]{1,0:T(8,128)(2,1)S(1)} %add_convert_fusion.3), channel_id=1, source_target_pairs={{0,192},{1,193},{2,194},{3,195},{4,196},{5,197},{6,198},{7,199},{8... | collective-permute-start | bytes 215048 | tf_op jit(solution)/shard_map/ppermute | solution.py:520
  85.8 5.2 %collective-permute-start.6 = (bf16[64,128]{1,0:T(8,128)(2,1)S(1)}, bf16[64,128]{1,0:T(8,128)(2,1)S(1)}, u32[]{:S(2)}, u32[]{:S(2)}) collective-permute-start(bf16[64,128]{1,0:T(8,128)(2,1)S(1)} %get-tuple-element.50), channel_id=1, source_target_pairs={{0,1},{1,0},{2,3},{3,2},{4,5},{5,4},{6,7},{7,6},{8,9},{9,8},{10,11... | collective-permute-start | bytes 49160 | tf_op jit(solution)/shard_map/ppermute | solution.py:520
  88.5 5.5 %collective-permute-start.10 = (bf16[216,128]{1,0:T(8,128)(2,1)S(1)}, bf16[216,128]{1,0:T(8,128)(2,1)S(1)}, u32[]{:S(2)}, u32[]{:S(2)}) collective-permute-start(bf16[216,128]{1,0:T(8,128)(2,1)S(1)} %slice.8), channel_id=1, source_target_pairs={{0,33},{1,32},{2,35},{3,34},{4,37},{5,36},{6,39},{7,38},{8,41},{9,... | collective-permute-start | bytes 165896 | tf_op jit(solution)/shard_map/ppermute | solution.py:520
  94.0 6.8 %collective-permute-start.11 = (bf16[280,128]{1,0:T(8,128)(2,1)S(1)}, bf16[280,128]{1,0:T(8,128)(2,1)S(1)}, u32[]{:S(2)}, u32[]{:S(2)}) collective-permute-start(bf16[280,128]{1,0:T(8,128)(2,1)S(1)} %pad_maximum_fusion.1), channel_id=1, source_target_pairs={{0,2},{1,3},{2,0},{3,1},{4,6},{5,7},{6,4},{7,5},{8,10},{9,11},{10,... | collective-permute-start | bytes 215048 | tf_op jit(solution)/shard_map/ppermute | solution.py:520
  95.4 17.1 %collective-permute-start.16 = (f32[64,64]{1,0:T(8,128)S(1)}, f32[64,64]{1,0:T(8,128)S(1)}, u32[]{:S(2)}, u32[]{:S(2)}) collective-permute-start(f32[64,64]{1,0:T(8,128)S(1)} %get-tuple-element.53.direct_ref), channel_id=1, source_target_pairs={{0,0},{1,16},{2,32},{3,48},{4,64},{5,80},{6,96},{7,112},{8,128},{9... | collective-permute-start | bytes 49160 | tf_op jit(solution)/shard_map/ppermute | solution.py:525
  98.6 3.1 %collective-permute-start.14 = (bf16[64,128]{1,0:T(8,128)(2,1)S(1)}, bf16[64,128]{1,0:T(8,128)(2,1)S(1)}, u32[]{:S(2)}, u32[]{:S(2)}) collective-permute-start(bf16[64,128]{1,0:T(8,128)(2,1)S(1)} %slice.9), channel_id=1, source_target_pairs={{0,16},{1,17},{2,18},{3,19},{4,20},{5,21},{6,22},{7,23},{8,24},{9,... | collective-permute-start | bytes 49160 | tf_op jit(solution)/shard_map/ppermute | solution.py:520
  100.8 5.8 %collective-permute-start.12 = (bf16[280,128]{1,0:T(8,128)(2,1)S(1)}, bf16[280,128]{1,0:T(8,128)(2,1)S(1)}, u32[]{:S(2)}, u32[]{:S(2)}) collective-permute-start(bf16[280,128]{1,0:T(8,128)(2,1)S(1)} %add_convert_fusion.1), channel_id=1, source_target_pairs={{0,4},{1,5},{2,6},{3,7},{4,0},{5,1},{6,2},{7,3},{8,12},{9,13},{10,... | collective-permute-start | bytes 215048 | tf_op jit(solution)/shard_map/ppermute | solution.py:520
  101.6 10.8 %collective-permute-start.15 = (bf16[64,128]{1,0:T(8,128)(2,1)S(1)}, bf16[64,128]{1,0:T(8,128)(2,1)S(1)}, u32[]{:S(2)}, u32[]{:S(2)}) collective-permute-start(bf16[64,128]{1,0:T(8,128)(2,1)S(1)} %add_convert_fusion.8), channel_id=1, source_target_pairs={{0,32},{1,33},{2,34},{3,35},{4,36},{5,37},{6,38},{7,39},{8,40},{9,... | collective-permute-start | bytes 49160 | tf_op jit(solution)/shard_map/ppermute | solution.py:520
  106.7 9.4 %collective-permute-start.13 = (bf16[280,128]{1,0:T(8,128)(2,1)S(1)}, bf16[280,128]{1,0:T(8,128)(2,1)S(1)}, u32[]{:S(2)}, u32[]{:S(2)}) collective-permute-start(bf16[280,128]{1,0:T(8,128)(2,1)S(1)} %add_convert_fusion.mine_ref), channel_id=1, source_target_pairs={{0,12},{1,13},{2,14},{3,15},{4,8},{5,9},{6,10},{7,11},{8,4},{9,5},... | collective-permute-start | bytes 215048 | tf_op jit(solution)/shard_map/ppermute | solution.py:520
  (3 other events, 26.0 us)

commit v5 on v4

--- a/solution.py
+++ b/solution.py
@@ -91,7 +91,7 @@
 
 def mixed_kernel(
     place_ref, feat_ref, w_left_ref, w_right_ref, w_in_ref, conv_ref,
-    mixed_ref, rows_ref, cols_ref, forward_ref, backward_ref, picked_ref,
+    mixed_ref, rows_ref, cols_ref, backward_ref, picked_ref,
 ):
     row = place_ref[0]
     col = place_ref[1]
@@ -109,15 +109,11 @@
             picked_ref[...].astype(BF16), weight_ref[...], preferred_element_type=F32
         )
     for layer in range(3):
-        weight = conv_ref[layer].astype(F32)
-        turned = jnp.concatenate([weight, jnp.zeros((CH, 96), F32)], axis=1)
+        turned = jnp.concatenate([conv_ref[layer].astype(F32), jnp.zeros((CH, 96), F32)], axis=1)
         turned = jnp.concatenate([turned[:, 128 * k : 128 * k + 128].T for k in range(3)], axis=0)
-        for a in range(3):
-            forward_ref[layer, CH * a : CH * a + CH, :] = weight[:, 96 * a : 96 * a + 96].astype(BF16)
-            taps = [8 - 3 * a - b for b in range(3)]
-            backward_ref[layer, CH * a : CH * a + CH, :] = jnp.concatenate(
-                [turned[CH * tap : CH * tap + CH] for tap in taps], axis=1
-            ).astype(BF16)
+        backward_ref[layer] = jnp.concatenate(
+            [turned[CH * tap : CH * tap + CH] for tap in range(8, -1, -1)], axis=1
+        ).astype(BF16)
     w_in = w_in_ref[...]
 
     def body(step, carry):
@@ -141,14 +137,6 @@
     return jnp.where((bin_at >= 0) & (bin_at < 1024), 1.0, 0.0).astype(F32)
 
 
-def many_taps(z_ref, base, rows, rate):
-    return (
-        z_ref[pl.ds(base - rate, rows), 0:CH, :]
-        + z_ref[pl.ds(base, rows), CH : 2 * CH, :]
-        + z_ref[pl.ds(base + rate, rows), 2 * CH : 3 * CH, :]
-    )
-
-
 def shifted_rows(value, rate):
     return jnp.concatenate(
         [pltpu.roll(value, rate, 2), value, pltpu.roll(value, WIDE - rate, 2)], axis=1
@@ -160,26 +148,33 @@
     return jnp.where((at >= 0) & (at < 1024), 1.0, 0.0).astype(F32) * inside[None]
 
 
-def multiply(weight, patch_ref, z_ref, base, rows):
+def convolve(weight, patch_ref, out_ref, base, rows, rate):
     for k in range(rows // 2):
         i = base + 2 * k
-        pair = jnp.concatenate([patch_ref[i], patch_ref[i + 1]], axis=1)
-        z = jnp.dot(weight, pair, preferred_element_type=F32)
-        z_ref[i] = z[:, :WIDE]
-        z_ref[i + 1] = z[:, WIDE:]
-
-
-def pipelined(first, last, rows, make, use):
+        taps = [
+            jnp.concatenate([patch_ref[i + off], patch_ref[i + off + 1]], axis=1)
+            for off in (-rate, 0, rate)
+        ]
+        z = jnp.dot(weight, jnp.concatenate(taps, axis=0), preferred_element_type=F32)
+        out_ref[i] = z[:, :WIDE]
+        out_ref[i + 1] = z[:, WIDE:]
+
+
+def pipelined(first, last, rows, make, use, beside=None):
     make(first)
 
     def body(step, carry):
         base = first + rows * step
         use(base - rows)
         make(base)
+        if beside is not None:
+            beside(step - 1)
         return carry
 
-    lax.fori_loop(1, (last - first) // rows, body, 0)
+    blocks = (last - first) // rows
+    lax.fori_loop(1, blocks, body, 0)
     use(last - rows)
+    return blocks - 1
 
 
 def main_kernel(
@@ -196,145 +191,149 @@
     terms_ref,
     grad_ref,
     last_ref,
-    round_ref,
     slope0_ref,
-    state_ref,
     slope1_ref,
     slope2_ref,
-    za_ref,
-    zb_ref,
+    state_ref,
+    z_ref,
     patch0_ref,
     patch1_ref,
     patch2_ref,
-    masked_ref,
-    patchb_ref,
+    patch3_ref,
+    patch4_ref,
+    masked0_ref,
+    masked1_ref,
     upstream_ref,
     grad2_ref,
+    total_ref,
 ):
     row = place_ref[0]
     col = place_ref[1]
     rates = [place_ref[2], place_ref[3], place_ref[4]]
     inside = lane_mask(col)
     patch_refs = (patch0_ref, patch1_ref, patch2_ref)
+    slope_refs = (slope0_ref, slope1_ref, slope2_ref)
     parts = (part0_ref, part1_ref, part2_ref, part3_ref)
     w_out = w_out_ref[...]
-    z_refs = (za_ref, zb_ref)
+
+    def activate(layer, base, state):
+        block = pl.ds(base, ROWS)
+        state_ref[block] = state
+        act, slope = gelu_pair(state.astype(F32))
+        slope_refs[layer][block] = slope.astype(BF16)
+        act = act * rows_mask(inside, row, base, ROWS)
+        patch_refs[layer][block] = shifted_rows(act, rates[layer])
 
     for n in range(4):
 
-        def start(q, carry, n=n):
-            given = parts[n][q].astype(F32)
-            state_ref[HALO * n + q] = (mixed_ref[HALO * n + q] + given).astype(BF16)
+        def start(step, carry, n=n):
+            at = ROWS * step
+            given = parts[n][pl.ds(at, ROWS)].astype(F32)
+            base = HALO * n + at
+            activate(0, base, (mixed_ref[pl.ds(base, ROWS)] + given).astype(BF16))
             return carry
 
-        lax.fori_loop(0, HALO, start, 0, unroll=4)
-
-    for layer in range(3):
-        z_now = z_refs[layer % 2]
-        z_last = z_refs[(layer + 1) % 2]
-        slope_ref = (slope0_ref, slope1_ref, slope2_ref)[layer]
-
-        def make(base, layer=layer, z_last=z_last, slope_ref=slope_ref):
-            block = pl.ds(base, ROWS)
-            state = state_ref[block].astype(F32)
-            if layer > 0:
-                new = (state + many_taps(z_last, base, ROWS, rates[layer - 1])).astype(BF16)
-                state_ref[block] = new
-                state = new.astype(F32)
-            act, slope = gelu_pair(state)
-            slope_ref[block] = slope
-            act = act * rows_mask(inside, row, base, ROWS)
-            patch_refs[layer][block] = shifted_rows(act, rates[layer])
-
-        def use(base, layer=layer, z_now=z_now):
-            multiply(forward_ref[layer], patch_refs[layer], z_now, base, ROWS)
+        lax.fori_loop(0, HALO // ROWS, start, 0)
+
+    def next_state(base):
+        block = pl.ds(base, ROWS)
+        return (state_ref[block].astype(F32) + z_ref[block]).astype(BF16)
+
+    for layer in (1, 2):
+
+        def make(base, layer=layer):
+            convolve(
+                forward_ref[layer - 1], patch_refs[layer - 1], z_ref, base, ROWS, rates[layer - 1]
+            )
+
+        def use(base, layer=layer):
+            activate(layer, base, next_state(base))
 
         pipelined(8 * layer, WIDE - 8 * layer, ROWS, make, use)
-
-    def finish(step, carry):
-        base = HALO + ROWS * step
-        new = state_ref[pl.ds(base, ROWS)].astype(F32) + many_taps(za_ref, base, ROWS, rates[2])
-        new = new.astype(BF16).astype(F32)
-        direct_ref[pl.ds(base - HALO, ROWS), :] = jnp.sum(new * w_out[None], axis=1)[:, :TILE]
-        return carry
-
-    lax.fori_loop(0, TILE // ROWS, finish, 0)
 
     for n in range(4):
         upstream_ref[HALO * n : HALO * n + HALO, :] = parts[n][32].astype(F32) + parts[n][33].astype(F32)
-
     tile_lanes = jnp.where(lax.broadcasted_iota(jnp.int32, (1, WIDE), 1) < TILE, 1.0, 0.0).astype(F32)
-    masked_ref[...] = jnp.zeros_like(masked_ref)
-
-    def weight_terms(layer):
-        def keep(step, carry):
-            block = pl.ds(HALO + 8 * step, 8)
-            masked_ref[block] = (round_ref[block].astype(F32) * tile_lanes[None]).astype(BF16)
-            return carry
-
-        lax.fori_loop(0, TILE // 8, keep, 0)
-        rate = rates[layer]
-
-        def body(step, total):
-            base = 24 + 8 * step
-            for part in range(2):
-                at = base + 4 * part
-                left = jnp.concatenate(
-                    [
-                        jnp.concatenate([masked_ref[at + k + off] for k in range(4)], axis=1)
-                        for off in (rate, 0, -rate)
-                    ],
-                    axis=0,
-                )
-                right = jnp.concatenate([patch_refs[layer][at + k] for k in range(4)], axis=1)
-                total = total + lax.dot_general(
-                    left, right, (((1,), (1,)), ((), ())), preferred_element_type=F32
-                )
-            return total
-
-        return lax.fori_loop(0, 10, body, jnp.zeros((96, 96), F32))
-
-    def back(layer, first, last, one_grad, z_now):
-        def make(base):
-            rounded = one_grad(base).astype(BF16)
-            round_ref[pl.ds(base, ROWS)] = rounded
-            patchb_ref[pl.ds(base, ROWS)] = shifted_rows(rounded.astype(F32), rates[layer])
-
-        def use(base):
-            multiply(backward_ref[layer], patchb_ref, z_now, base, ROWS)
-
-        pipelined(first, last, ROWS, make, use)
-        return weight_terms(layer)
+
+    def keep(ref, base, rounded):
+        at = base + lax.broadcasted_iota(jnp.int32, (ROWS, 1, 1), 0)
+        own = jnp.where((at >= HALO) & (at < HALO + TILE), 1.0, 0.0).astype(F32) * tile_lanes[None]
+        ref[pl.ds(base, ROWS)] = (rounded.astype(F32) * own).astype(BF16)
 
     def first_grad(base):
         return upstream_ref[pl.ds(base, ROWS), :][:, None, :] * w_out[None]
 
-    def second_grad(base):
+    def last_make(base):
+        convolve(forward_ref[2], patch2_ref, z_ref, base, ROWS, rates[2])
+
+    def last_use(base):
+        new = next_state(base).astype(F32)
+        direct_ref[pl.ds(base - HALO, ROWS), :] = jnp.sum(new * w_out[None], axis=1)[:, :TILE]
+
+    def begin(step):
+        base = 8 + ROWS * step
+        rounded = first_grad(base).astype(BF16)
+        keep(masked0_ref, base, rounded)
+        patch3_ref[pl.ds(base, ROWS)] = shifted_rows(rounded.astype(F32), rates[2])
+
+    pipelined(HALO, HALO + TILE, ROWS, last_make, last_use, begin)
+    for step in (3, 4, 5, 6):
+        begin(step)
+
+    total_ref[...] = jnp.zeros_like(total_ref)
+
+    def weight_terms(layer, masked_ref, step):
+        rate = rates[layer]
+        total = total_ref[layer]
+        for part in range(4):
+            at = 24 + ROWS * step + 4 * part
+            left = jnp.concatenate(
+                [
+                    jnp.concatenate([masked_ref[at + k + off] for k in range(4)], axis=1)
+                    for off in (rate, 0, -rate)
+                ],
+                axis=0,
+            )
+            right = jnp.concatenate([patch_refs[layer][at + k] for k in range(4)], axis=1)
+            total = total + lax.dot_general(
+                left, right, (((1,), (1,)), ((), ())), preferred_element_type=F32
+            )
+        total_ref[layer] = total
+
+    def second_make(base):
+        convolve(backward_ref[2], patch3_ref, z_ref, base, ROWS, rates[2])
+
+    def second_use(base):
         block = pl.ds(base, ROWS)
-        new = first_grad(base) + many_taps(zb_ref, base, ROWS, rates[2]) * slope2_ref[block]
+        new = first_grad(base) + z_ref[block] * slope2_ref[block].astype(F32)
         new = new * rows_mask(inside, row, base, ROWS)
         grad2_ref[block] = new
-        return new
-
-    terms2 = back(2, 8, 120, first_grad, zb_ref)
-    terms1 = back(1, 16, 112, second_grad, za_ref)
-
-    def third_grad(step, carry):
-        base = 24 + ROWS * step
+        rounded = new.astype(BF16)
+        keep(masked1_ref, base, rounded)
+        patch4_ref[block] = shifted_rows(rounded.astype(F32), rates[1])
+
+    pipelined(16, 112, ROWS, second_make, second_use, lambda step: weight_terms(2, masked0_ref, step))
+
+    first_half = lax.broadcasted_iota(jnp.int32, (1, 1, WIDE), 2) < TILE
+
+    def third_make(base):
+        convolve(backward_ref[1], patch4_ref, z_ref, base, ROWS, rates[1])
+
+    def third_use(base):
         block = pl.ds(base, ROWS)
-        new = grad2_ref[block] + many_taps(za_ref, base, ROWS, rates[1]) * slope1_ref[block]
+        new = grad2_ref[block] + z_ref[block] * slope1_ref[block].astype(F32)
         new = new * rows_mask(inside, row, base, ROWS)
         rounded = new.astype(BF16)
+        keep(masked0_ref, base, rounded)
         last_ref[pl.ds(base - 24, ROWS)] = rounded
-        round_ref[block] = rounded
-        slope = pltpu.roll(slope0_ref[block], TILE, 2)
+        slope = pltpu.roll(slope0_ref[block].astype(F32), TILE, 2)
         grad_ref[pl.ds(base - 24, ROWS)] = jnp.where(first_half, new, slope)
-        return carry
-
-    first_half = lax.broadcasted_iota(jnp.int32, (1, 1, WIDE), 2) < TILE
-    lax.fori_loop(0, 80 // ROWS, third_grad, 0)
-    terms0 = weight_terms(0)
-    terms = jnp.concatenate([terms0, terms1, terms2], axis=0)
+
+    done = pipelined(24, 104, ROWS, third_make, third_use, lambda step: weight_terms(1, masked1_ref, step))
+    weight_terms(1, masked1_ref, done)
+    for step in range(5):
+        weight_terms(0, masked0_ref, step)
+    terms = jnp.concatenate([total_ref[layer] for layer in range(3)], axis=0)
     spare = jnp.concatenate([terms[216:288, 32 * k : 32 * k + 32] for k in range(3)], axis=0)
     terms_ref[...] = jnp.concatenate([terms[0:216], spare], axis=1).astype(BF16)
 
@@ -351,27 +350,30 @@
     col_ref,
     z_ref,
     patch_ref,
+    total_ref,
 ):
     rate = place_ref[2]
 
-    def make(base):
-        patch_ref[pl.ds(base, ROWS)] = shifted_rows(round_ref[pl.ds(base, ROWS)].astype(F32), rate)
-
-    def use(base):
-        multiply(backward_ref[0], patch_ref, z_ref, base, ROWS)
-
-    pipelined(0, 80, ROWS, make, use)
+    def spread(step, carry):
+        block = pl.ds(ROWS * step, ROWS)
+        patch_ref[block] = shifted_rows(round_ref[block].astype(F32), rate)
+        return carry
+
+    lax.fori_loop(0, 80 // ROWS, spread, 0)
     w_in = w_in_ref[...]
     cols = cols_ref[0:TILE, :]
 
-    def body(step, total):
-        base = ROWS * step
-        both = grad_ref[pl.ds(base + 8, ROWS)]
+    def make(base):
+        convolve(backward_ref[0], patch_ref, z_ref, base, ROWS, rate)
+
+    def use(base):
+        block = pl.ds(base, ROWS)
+        both = grad_ref[block]
         slope = pltpu.roll(both, TILE, 2)
-        start = both + many_taps(z_ref, base + 8, ROWS, rate) * slope
-        start = start[:, :, :TILE].astype(BF16)
-        rows = rows_ref[pl.ds(base + HALO, ROWS), :]
+        start = (both + z_ref[block] * slope)[:, :, :TILE].astype(BF16)
+        rows = rows_ref[pl.ds(base + 24, ROWS), :]
         sums = []
+        total = total_ref[...]
         for k in range(ROWS):
             hidden = lax.dot_general(
                 start[k], w_in, (((0,), (0,)), ((), ())), preferred_element_type=F32
@@ -379,11 +381,12 @@
             outer = hidden * gelu_pair(rows[k : k + 1, :] + cols)[1]
             sums.append(jnp.sum(outer, axis=0, keepdims=True))
             total = total + outer
-        row_ref[pl.ds(base, ROWS), :] = jnp.concatenate(sums, axis=0).astype(BF16)
-        return total
-
-    total = lax.fori_loop(0, TILE // ROWS, body, jnp.zeros((TILE, 128), F32))
-    col_ref[...] = total.astype(BF16)
+        total_ref[...] = total
+        row_ref[pl.ds(base - 8, ROWS), :] = jnp.concatenate(sums, axis=0).astype(BF16)
+
+    total_ref[...] = jnp.zeros_like(total_ref)
+    pipelined(8, 8 + TILE, ROWS, make, use)
+    col_ref[...] = total_ref[...].astype(BF16)
 
 
 def finish_kernel(
@@ -468,48 +471,35 @@
     from_left = lax.ppermute(right_edge, "col", up)
     from_right = lax.ppermute(left_edge, "col", down)
 
-    mixed, row_project, col_project, forward_w, backward_w = call(
+    upper, lower = call(
+        widen_kernel, [shape(HALO + 2, CH, WIDE, dtype=BF16)] * 2, [VMEM] * 4
+    )(own, upstream, from_left, from_right)
+    above = lax.ppermute(lower, "row", up)
+    below = lax.ppermute(upper, "row", down)
+
+    mixed, row_project, col_project, backward_w = call(
         mixed_kernel,
         [shape(WIDE, CH, WIDE), shape(WIDE, 128), shape(WIDE, 128)]
-        + [shape(3, 96, 96, dtype=BF16)] * 2,
+        + [shape(3, CH, 288, dtype=BF16)],
         [SMEM] + [VMEM] * 5,
         [pltpu.VMEM((WIDE, 128), F32)],
         16,
         6,
     )(place, gathered, w_left, w_right, w_in, conv_w)
-    from_left, from_right, mixed = lax.optimization_barrier((from_left, from_right, mixed))
-
-    upper, lower = call(
-        widen_kernel, [shape(HALO + 2, CH, WIDE, dtype=BF16)] * 2, [VMEM] * 4
-    )(own, upstream, from_left, from_right)
-    above = lax.ppermute(lower, "row", up)
-    below = lax.ppermute(upper, "row", down)
-
     w_out_wide = jnp.broadcast_to(w_out.astype(F32)[:, None], (CH, WIDE))
     big = (WIDE, CH, WIDE)
     direct, terms, grad, rounded = call(
         main_kernel,
         [shape(TILE, TILE), shape(216, 128, dtype=BF16), shape(80, CH, WIDE), shape(80, CH, WIDE, dtype=BF16)],
         [SMEM] + [VMEM] * 8,
-        [
-            pltpu.VMEM(big, BF16),
-            pltpu.VMEM(big, F32),
-            pltpu.VMEM(big, BF16),
-            pltpu.VMEM(big, F32),
-            pltpu.VMEM(big, F32),
-            pltpu.VMEM((WIDE, 96, WIDE), F32),
-            pltpu.VMEM((WIDE, 96, WIDE), F32),
-            pltpu.VMEM((WIDE, 96, WIDE), BF16),
-            pltpu.VMEM((WIDE, 96, WIDE), BF16),
-            pltpu.VMEM((WIDE, 96, WIDE), BF16),
-            pltpu.VMEM(big, BF16),
-            pltpu.VMEM((WIDE, 96, WIDE), BF16),
-            pltpu.VMEM((WIDE, WIDE), F32),
-            pltpu.VMEM(big, F32),
-        ],
-        42,
+        [pltpu.VMEM(big, BF16)] * 4
+        + [pltpu.VMEM(big, F32)]
+        + [pltpu.VMEM((WIDE, 96, WIDE), BF16)] * 5
+        + [pltpu.VMEM(big, BF16)] * 2
+        + [pltpu.VMEM((WIDE, WIDE), F32), pltpu.VMEM(big, F32), pltpu.VMEM((3, 96, 96), F32)],
+        36,
         24,
-    )(place, mixed, above, upper, lower, below, forward_w, backward_w, w_out_wide)
+    )(place, mixed, above, upper, lower, below, conv_w, backward_w, w_out_wide)
 
     def flipped(value, row_bits, col_bits):
         pairs = [
@@ -532,7 +522,11 @@
         last_kernel,
         [shape(TILE, 128, dtype=BF16), shape(TILE, 128, dtype=BF16)],
         [SMEM] + [VMEM] * 6,
-        [pltpu.VMEM((80, 96, WIDE), F32), pltpu.VMEM((80, 96, WIDE), BF16)],
+        [
+            pltpu.VMEM((80, CH, WIDE), F32),
+            pltpu.VMEM((80, 96, WIDE), BF16),
+            pltpu.VMEM((TILE, 128), F32),
+        ],
         16,
         7,
     )(place, grad, rounded, row_project, col_project, backward_w, w_in)

time: 117 us -> 114 us (0.974)
  Pallas kernels: 32.6 us -> 29.1 us
  starting transfers between devices: 53.6 us -> 55.9 us
  waiting for transfers between devices: 28.8 us -> 26.6 us
    all_to_all x1, waiting for transfers between devices: 5.59 us -> 0.01 us  [on_device(): gathered = lax.all_to_all(sent, ('row', 'col'), 0, 0)]
    ppermute x1, waiting for transfers between devices: 0.01 us -> 3.65 us  [on_device(): from_left = lax.ppermute(right_edge, 'col', up)]
    pallas_call x1, Pallas kernels: 21.1 us -> 17.5 us  [on_device(): call(main_kernel, [shape(TILE, TILE), shape(216, 128, dtype=BF16), shape(...]
    ppermute x1, starting transfers between devices: 3.13 us -> 6.49 us  [on_device(): direct_other = lax.ppermute(direct, ('row', 'col'), swap)]
    ppermute x1, waiting for transfers between devices: 0.01 us -> 2.94 us  [on_device(): from_right = lax.ppermute(left_edge, 'col', down)]
    ppermute x1, waiting for transfers between devices: 2.37 us -> 0.01 us  [on_device(): above = lax.ppermute(lower, 'row', up)]
    ppermute x1, waiting for transfers between devices: 1.67 us -> 0.01 us  [on_device(): below = lax.ppermute(upper, 'row', down)]
    ppermute x11, starting transfers between devices: 17 us -> 15.7 us  [flipped(): return lax.ppermute(value, ('row', 'col'), pairs)]
  transfers between devices with their start and end apart: 18 -> 18, of which waited for: 11 -> 10; matrix products, arithmetic and copies ran while one was open for 0% -> 0% of each run, Pallas kernels for 9% -> 9%
where the time goes in v5:
time: 114 us
  starting transfers between devices  55.9 us (49%)
  Pallas kernels  29.1 us (26%)
  waiting for transfers between devices  26.6 us (23%)
    ppermute x11, waiting for transfers between devices, flipped(): return lax.ppermute(value, ('row', 'col'), pairs)  20 us
    pallas_call x1, Pallas kernels, on_device(): call(main_kernel, [shape(TILE, TILE), shape(216, 128, dtype=BF16), shape(...  17.5 us
    ppermute x11, starting transfers between devices, flipped(): return lax.ppermute(value, ('row', 'col'), pairs)  15.7 us
    all_to_all x1, starting transfers between devices, on_device(): gathered = lax.all_to_all(sent, ('row', 'col'), 0, 0)  14 us
    ppermute x1, starting transfers between devices, on_device(): direct_other = lax.ppermute(direct, ('row', 'col'), swap)  6.49 us
    ppermute x1, starting transfers between devices, on_device(): from_left = lax.ppermute(right_edge, 'col', up)  5.04 us
    ppermute x1, starting transfers between devices, on_device(): mirrored = lax.ppermute(cotangent, ('row', 'col'), swap)  4.77 us
    pallas_call x1, Pallas kernels, on_device(): call(mixed_kernel, [shape(WIDE, CH, WIDE), shape(WIDE, 128), shape(WIDE,...  4.52 us
  transfers between devices with their start and end apart: 18, of which 10 were waited for; matrix products, arithmetic and copies ran while one was open for 0% of the time, Pallas kernels for 9%

profile of v5, /device:TPU:40, one launch (start us, length us, event | category | flops | bytes accessed | tf_op | source)
XLA Modules:
  0.0 113.6 jit_solution(2894743387617907452)
XLA Ops:
  0.7 4.8 %collective-permute-start = (f32[64,64]{1,0:T(8,128)}, f32[64,64]{1,0:T(8,128)S(1)}, u32[]{:S(2)}, u32[]{:S(2)}) collective-permute-start(f32[64,64]{1,0:T(8,128)} %cot_ref.1), channel_id=1, source_target_pairs={{0,0},{1,16},{2,32},{3,48},{4,64},{5,80},{6,96},{7,112},{8,128},{9... | collective-permute-start | bytes 49160 | tf_op jit(solution)/shard_map/ppermute | solution.py:456
  6.9 14.0 %all-to-all-start = ((bf16[256,4,128]{2,1,0:T(4,128)(2,1)}), bf16[256,4,128]{2,1,0:T(4,128)(2,1)S(1)}, u32[]{:S(2)}, u32[]{:S(2)}) async-start(bf16[256,4,128]{2,1,0:T(4,128)(2,1)} %shard_map.120), calls=%async_computation | async-start | bytes 524288 | tf_op jit(solution)/shard_map/all_to_all | solution.py:460
  21.5 5.0 %collective-permute-start.1 = (bf16[17,32,128]{2,1,0:T(8,128)(2,1)S(1)}, bf16[17,32,128]{2,1,0:T(8,128)(2,1)S(1)}, u32[]{:S(2)}, u32[]{:S(2)}) collective-permute-start(bf16[17,32,128]{2,1,0:T(8,128)(2,1)S(1)} %get-tuple-element.28), channel_id=1, source_target_pairs={{0,1},{1,2},{2,3},{3,4},{4,5},{5,6},{6,7},{7,8},{8,9},{9,10},{10,1... | collective-permute-start | bytes 417800 | tf_op jit(solution)/shard_map/ppermute | solution.py:471
  26.6 3.3 %collective-permute-start.2 = (bf16[17,32,128]{2,1,0:T(8,128)(2,1)S(1)}, bf16[17,32,128]{2,1,0:T(8,128)(2,1)S(1)}, u32[]{:S(2)}, u32[]{:S(2)}) collective-permute-start(bf16[17,32,128]{2,1,0:T(8,128)(2,1)S(1)} %get-tuple-element.29), channel_id=1, source_target_pairs={{1,0},{2,1},{3,2},{4,3},{5,4},{6,5},{7,6},{8,7},{9,8},{10,9},{11,1... | collective-permute-start | bytes 417800 | tf_op jit(solution)/shard_map/ppermute | solution.py:472
  30.0 3.7 %collective-permute-done.1.from_left_ref = bf16[17,32,128]{2,1,0:T(8,128)(2,1)S(1)} collective-permute-done((bf16[17,32,128]{2,1,0:T(8,128)(2,1)S(1)}, bf16[17,32,128]{2,1,0:T(8,128)(2,1)S(1)}, u32[]{:S(2)}, u32[]{:S(2)}) %collective-permute-start.1) | collective-permute-done | bytes 139296 | tf_op jit(solution)/shard_map/ppermute | solution.py:471
  33.7 2.9 %collective-permute-done.2.from_right_ref = bf16[17,32,128]{2,1,0:T(8,128)(2,1)S(1)} collective-permute-done((bf16[17,32,128]{2,1,0:T(8,128)(2,1)S(1)}, bf16[17,32,128]{2,1,0:T(8,128)(2,1)S(1)}, u32[]{:S(2)}, u32[]{:S(2)}) %collective-permute-start.2) | collective-permute-done | bytes 139296 | tf_op jit(solution)/shard_map/ppermute | solution.py:472
  37.0 2.0 %collective-permute-start.3 = (bf16[34,32,128]{2,1,0:T(8,128)(2,1)S(1)}, bf16[34,32,128]{2,1,0:T(8,128)(2,1)S(1)}, u32[]{:S(2)}, u32[]{:S(2)}) collective-permute-start(bf16[34,32,128]{2,1,0:T(8,128)(2,1)S(1)} %get-tuple-element.30.part2_ref), channel_id=1, source_target_pairs={{0,16},{16,32},{32,48},{48,64},{64,80},{80,96},{96,112},{112,128},... | collective-permute-start | bytes 835592 | tf_op jit(solution)/shard_map/ppermute | solution.py:477
  38.9 4.5 %collective-permute-start.4 = (bf16[34,32,128]{2,1,0:T(8,128)(2,1)S(1)}, bf16[34,32,128]{2,1,0:T(8,128)(2,1)S(1)}, u32[]{:S(2)}, u32[]{:S(2)}) collective-permute-start(bf16[34,32,128]{2,1,0:T(8,128)(2,1)S(1)} %get-tuple-element.31.part1_ref), channel_id=1, source_target_pairs={{16,0},{32,16},{48,32},{64,48},{80,64},{96,80},{112,96},{128,112},... | collective-permute-start | bytes 835592 | tf_op jit(solution)/shard_map/ppermute | solution.py:478
  43.5 4.5 %shard_map.121 = (f32[128,32,128]{2,1,0:T(8,128)S(1)}, f32[128,128]{1,0:T(8,128)S(1)}, f32[128,128]{1,0:T(8,128)S(1)}, bf16[3,32,288]{2,1,0:T(8,128)(2,1)S(1)}) custom-call(s32[8]{0:T(128)S(1)} %pad_add_fusion.place_ref, bf16[256,4,128]{2,1,0:T(4,128)(2,1)S(1)} %all-to-all-done.feat_ref, bf16[128,128]{1,0:T(8,128)(2,1)S(1)} %copy-done.3, ...), custom_call_target="tpu_custom_call" | custom-call | flops 6000000000 | bytes 18000000 | tf_op jit(solution)/shard_map/pallas_call | solution.py:480
  48.1 17.5 %shard_map.124 = (f32[64,64]{1,0:T(8,128)S(1)}, bf16[216,128]{1,0:T(8,128)(2,1)S(1)}, f32[80,32,128]{2,1,0:T(8,128)S(1)}, bf16[80,32,128]{2,1,0:T(8,128)(2,1)S(1)}) custom-call(s32[8]{0:T(128)S(1)} %pad_add_fusion.place_ref, f32[128,32,128]{2,1,0:T(8,128)S(1)} %get-tuple-element.25.mixed_ref, bf16[34,32,128]{2,1,0:T(8,128)(2,1)S(1)} %collective-permute-done.3.part0_ref, ...), custom_call_target="tpu_custom_call" | custom-call | flops 24000000000 | bytes 72000000 | tf_op jit(solution)/shard_map/pallas_call | solution.py:491
  67.2 2.2 %collective-permute-start.7 = (bf16[216,128]{1,0:T(8,128)(2,1)S(1)}, bf16[216,128]{1,0:T(8,128)(2,1)S(1)}, u32[]{:S(2)}, u32[]{:S(2)}) collective-permute-start(bf16[216,128]{1,0:T(8,128)(2,1)S(1)} %add_convert_fusion.6), channel_id=1, source_target_pairs={{0,32},{1,33},{2,34},{3,35},{4,36},{5,37},{6,38},{7,39},{8,40},{9,... | collective-permute-start | bytes 165896 | tf_op jit(solution)/shard_map/ppermute | solution.py:510
  69.4 4.4 %shard_map.125 = (bf16[64,128]{1,0:T(8,128)(2,1)S(1)}, bf16[64,128]{1,0:T(8,128)(2,1)S(1)}) custom-call(s32[8]{0:T(128)S(1)} %pad_add_fusion.place_ref, f32[80,32,128]{2,1,0:T(8,128)S(1)} %get-tuple-element.38.grad_ref, bf16[80,32,128]{2,1,0:T(8,128)(2,1)S(1)} %get-tuple-element.39.round_ref, f32[128,128]{1,0:T(8,128)S(1)} %get-tuple-element.40.rows_ref, ...), custom_call_target="tpu_custom_call" | custom-call | flops 7000000000 | bytes 21000000 | tf_op jit(solution)/shard_map/pallas_call | solution.py:521
  74.7 3.8 %collective-permute-done.8 = bf16[280,128]{1,0:T(8,128)(2,1)S(1)} collective-permute-done((bf16[280,128]{1,0:T(8,128)(2,1)S(1)}, bf16[280,128]{1,0:T(8,128)(2,1)S(1)}, u32[]{:S(2)}, u32[]{:S(2)}) %collective-permute-start.8) | collective-permute-done | bytes 71712 | tf_op jit(solution)/shard_map/ppermute | solution.py:510
  78.6 1.3 %collective-permute-start.9 = (bf16[280,128]{1,0:T(8,128)(2,1)S(1)}, bf16[280,128]{1,0:T(8,128)(2,1)S(1)}, u32[]{:S(2)}, u32[]{:S(2)}) collective-permute-start(bf16[280,128]{1,0:T(8,128)(2,1)S(1)} %add_convert_fusion.3), channel_id=1, source_target_pairs={{0,192},{1,193},{2,194},{3,195},{4,196},{5,197},{6,198},{7,199},{8... | collective-permute-start | bytes 215048 | tf_op jit(solution)/shard_map/ppermute | solution.py:510
  79.9 1.4 %collective-permute-start.6 = (bf16[64,128]{1,0:T(8,128)(2,1)S(1)}, bf16[64,128]{1,0:T(8,128)(2,1)S(1)}, u32[]{:S(2)}, u32[]{:S(2)}) collective-permute-start(bf16[64,128]{1,0:T(8,128)(2,1)S(1)} %get-tuple-element.42), channel_id=1, source_target_pairs={{0,1},{1,0},{2,3},{3,2},{4,5},{5,4},{6,7},{7,6},{8,9},{9,8},{10,11... | collective-permute-start | bytes 49160 | tf_op jit(solution)/shard_map/ppermute | solution.py:510
  81.3 1.7 %collective-permute-done.9 = bf16[280,128]{1,0:T(8,128)(2,1)S(1)} collective-permute-done((bf16[280,128]{1,0:T(8,128)(2,1)S(1)}, bf16[280,128]{1,0:T(8,128)(2,1)S(1)}, u32[]{:S(2)}, u32[]{:S(2)}) %collective-permute-start.9) | collective-permute-done | bytes 71712 | tf_op jit(solution)/shard_map/ppermute | solution.py:510
  83.3 2.0 %collective-permute-done.6 = bf16[64,128]{1,0:T(8,128)(2,1)S(1)} collective-permute-done((bf16[64,128]{1,0:T(8,128)(2,1)S(1)}, bf16[64,128]{1,0:T(8,128)(2,1)S(1)}, u32[]{:S(2)}, u32[]{:S(2)}) %collective-permute-start.6) | collective-permute-done | bytes 16416 | tf_op jit(solution)/shard_map/ppermute | solution.py:510
  85.3 3.2 %collective-permute-done.10 = bf16[216,128]{1,0:T(8,128)(2,1)S(1)} collective-permute-done((bf16[216,128]{1,0:T(8,128)(2,1)S(1)}, bf16[216,128]{1,0:T(8,128)(2,1)S(1)}, u32[]{:S(2)}, u32[]{:S(2)}) %collective-permute-start.10) | collective-permute-done | bytes 55328 | tf_op jit(solution)/shard_map/ppermute | solution.py:510
  88.6 6.5 %collective-permute-start.16 = (f32[64,64]{1,0:T(8,128)S(1)}, f32[64,64]{1,0:T(8,128)S(1)}, u32[]{:S(2)}, u32[]{:S(2)}) collective-permute-start(f32[64,64]{1,0:T(8,128)S(1)} %get-tuple-element.45.direct_ref), channel_id=1, source_target_pairs={{0,0},{1,16},{2,32},{3,48},{4,64},{5,80},{6,96},{7,112},{8,128},{9... | collective-permute-start | bytes 49160 | tf_op jit(solution)/shard_map/ppermute | solution.py:515
  95.1 2.2 %collective-permute-start.14 = (bf16[64,128]{1,0:T(8,128)(2,1)S(1)}, bf16[64,128]{1,0:T(8,128)(2,1)S(1)}, u32[]{:S(2)}, u32[]{:S(2)}) collective-permute-start(bf16[64,128]{1,0:T(8,128)(2,1)S(1)} %slice.9), channel_id=1, source_target_pairs={{0,16},{1,17},{2,18},{3,19},{4,20},{5,21},{6,22},{7,23},{8,24},{9,... | collective-permute-start | bytes 49160 | tf_op jit(solution)/shard_map/ppermute | solution.py:510
  98.6 4.6 %collective-permute-done.12 = bf16[280,128]{1,0:T(8,128)(2,1)S(1)} collective-permute-done((bf16[280,128]{1,0:T(8,128)(2,1)S(1)}, bf16[280,128]{1,0:T(8,128)(2,1)S(1)}, u32[]{:S(2)}, u32[]{:S(2)}) %collective-permute-start.12) | collective-permute-done | bytes 71712 | tf_op jit(solution)/shard_map/ppermute | solution.py:510
  103.2 6.0 %collective-permute-start.13 = (bf16[280,128]{1,0:T(8,128)(2,1)S(1)}, bf16[280,128]{1,0:T(8,128)(2,1)S(1)}, u32[]{:S(2)}, u32[]{:S(2)}) collective-permute-start(bf16[280,128]{1,0:T(8,128)(2,1)S(1)} %add_convert_fusion.mine_ref), channel_id=1, source_target_pairs={{0,12},{1,13},{2,14},{3,15},{4,8},{5,9},{6,10},{7,11},{8,4},{9,5},... | collective-permute-start | bytes 215048 | tf_op jit(solution)/shard_map/ppermute | solution.py:510
  109.2 3.4 %collective-permute-done.13.got_ref = bf16[280,128]{1,0:T(8,128)(2,1)S(1)} collective-permute-done((bf16[280,128]{1,0:T(8,128)(2,1)S(1)}, bf16[280,128]{1,0:T(8,128)(2,1)S(1)}, u32[]{:S(2)}, u32[]{:S(2)}) %collective-permute-start.13) | collective-permute-done | bytes 71712 | tf_op jit(solution)/shard_map/ppermute | solution.py:510
  112.6 1.0 shard_map.126
  (54 shorter events, 6.5 us)
Async XLA Ops:
  0.6 20.3 %copy-start.2 = (f32[64,64]{1,0:T(8,128)S(1)}, f32[64,64]{1,0:T(8,128)}, u32[]{:S(2)}) copy-start(f32[64,64]{1,0:T(8,128)} %cot_ref.1) | copy-start | bytes 49156
  0.6 20.3 %copy-start = (bf16[32,64,64]{2,1,0:T(8,128)(2,1)S(1)}, bf16[32,64,64]{2,1,0:T(8,128)(2,1)}, u32[]{:S(2)}) copy-start(bf16[32,64,64]{2,1,0:T(8,128)(2,1)} %pair_ref.1) | copy-start | bytes 786436
  0.7 20.3 %collective-permute-start = (f32[64,64]{1,0:T(8,128)}, f32[64,64]{1,0:T(8,128)S(1)}, u32[]{:S(2)}, u32[]{:S(2)}) collective-permute-start(f32[64,64]{1,0:T(8,128)} %cot_ref.1), channel_id=1, source_target_pairs={{0,0},{1,16},{2,32},{3,48},{4,64},{5,80},{6,96},{7,112},{8,128},{9... | collective-permute-start | bytes 49160 | tf_op jit(solution)/shard_map/ppermute | solution.py:456
  6.9 36.6 %all-to-all-start = ((bf16[256,4,128]{2,1,0:T(4,128)(2,1)}), bf16[256,4,128]{2,1,0:T(4,128)(2,1)S(1)}, u32[]{:S(2)}, u32[]{:S(2)}) async-start(bf16[256,4,128]{2,1,0:T(4,128)(2,1)} %shard_map.120), calls=%async_computation | async-start | bytes 524288 | tf_op jit(solution)/shard_map/all_to_all | solution.py:460
  21.5 22.0 %copy-start.1 = (bf16[3,32,288]{2,1,0:T(8,128)(2,1)S(1)}, bf16[3,32,288]{2,1,0:T(8,128)(2,1)}, u32[]{:S(2)}) copy-start(bf16[3,32,288]{2,1,0:T(8,128)(2,1)} %forward_ref.1) | copy-start | bytes 165892
  21.5 22.0 %copy-start.3 = (bf16[128,128]{1,0:T(8,128)(2,1)S(1)}, bf16[128,128]{1,0:T(8,128)(2,1)}, u32[]{:S(2)}) copy-start(bf16[128,128]{1,0:T(8,128)(2,1)} %w_left_ref.3) | copy-start | bytes 98308
  21.5 22.0 %copy-start.4 = (bf16[128,128]{1,0:T(8,128)(2,1)S(1)}, bf16[128,128]{1,0:T(8,128)(2,1)}, u32[]{:S(2)}) copy-start(bf16[128,128]{1,0:T(8,128)(2,1)} %w_right_ref.3) | copy-start | bytes 98308
  21.5 22.0 %copy-start.5 = (bf16[32,128]{1,0:T(8,128)(2,1)S(1)}, bf16[32,128]{1,0:T(8,128)(2,1)}, u32[]{:S(2)}) copy-start(bf16[32,128]{1,0:T(8,128)(2,1)} %w_in_ref.3) | copy-start | bytes 24580
  21.5 12.2 %collective-permute-start.1 = (bf16[17,32,128]{2,1,0:T(8,128)(2,1)S(1)}, bf16[17,32,128]{2,1,0:T(8,128)(2,1)S(1)}, u32[]{:S(2)}, u32[]{:S(2)}) collective-permute-start(bf16[17,32,128]{2,1,0:T(8,128)(2,1)S(1)} %get-tuple-element.28), channel_id=1, source_target_pairs={{0,1},{1,2},{2,3},{3,4},{4,5},{5,6},{6,7},{7,8},{8,9},{9,10},{10,1... | collective-permute-start | bytes 417800 | tf_op jit(solution)/shard_map/ppermute | solution.py:471
  26.6 10.0 %collective-permute-start.2 = (bf16[17,32,128]{2,1,0:T(8,128)(2,1)S(1)}, bf16[17,32,128]{2,1,0:T(8,128)(2,1)S(1)}, u32[]{:S(2)}, u32[]{:S(2)}) collective-permute-start(bf16[17,32,128]{2,1,0:T(8,128)(2,1)S(1)} %get-tuple-element.29), channel_id=1, source_target_pairs={{1,0},{2,1},{3,2},{4,3},{5,4},{6,5},{7,6},{8,7},{9,8},{10,9},{11,1... | collective-permute-start | bytes 417800 | tf_op jit(solution)/shard_map/ppermute | solution.py:472
  37.0 11.1 %collective-permute-start.3 = (bf16[34,32,128]{2,1,0:T(8,128)(2,1)S(1)}, bf16[34,32,128]{2,1,0:T(8,128)(2,1)S(1)}, u32[]{:S(2)}, u32[]{:S(2)}) collective-permute-start(bf16[34,32,128]{2,1,0:T(8,128)(2,1)S(1)} %get-tuple-element.30.part2_ref), channel_id=1, source_target_pairs={{0,16},{16,32},{32,48},{48,64},{64,80},{80,96},{96,112},{112,128},... | collective-permute-start | bytes 835592 | tf_op jit(solution)/shard_map/ppermute | solution.py:477
  38.9 9.1 %collective-permute-start.4 = (bf16[34,32,128]{2,1,0:T(8,128)(2,1)S(1)}, bf16[34,32,128]{2,1,0:T(8,128)(2,1)S(1)}, u32[]{:S(2)}, u32[]{:S(2)}) collective-permute-start(bf16[34,32,128]{2,1,0:T(8,128)(2,1)S(1)} %get-tuple-element.31.part1_ref), channel_id=1, source_target_pairs={{16,0},{32,16},{48,32},{64,48},{80,64},{96,80},{112,96},{128,112},... | collective-permute-start | bytes 835592 | tf_op jit(solution)/shard_map/ppermute | solution.py:478
  65.7 1.5 %collective-permute-start.5 = (bf16[216,128]{1,0:T(8,128)(2,1)S(1)}, bf16[216,128]{1,0:T(8,128)(2,1)S(1)}, u32[]{:S(2)}, u32[]{:S(2)}) collective-permute-start(bf16[216,128]{1,0:T(8,128)(2,1)S(1)} %get-tuple-element.37), channel_id=1, source_target_pairs={{0,16},{1,17},{2,18},{3,19},{4,20},{5,21},{6,22},{7,23},{8,24},{9,... | collective-permute-start | bytes 165896 | tf_op jit(solution)/shard_map/ppermute | solution.py:510
  67.2 6.7 %collective-permute-start.7 = (bf16[216,128]{1,0:T(8,128)(2,1)S(1)}, bf16[216,128]{1,0:T(8,128)(2,1)S(1)}, u32[]{:S(2)}, u32[]{:S(2)}) collective-permute-start(bf16[216,128]{1,0:T(8,128)(2,1)S(1)} %add_convert_fusion.6), channel_id=1, source_target_pairs={{0,32},{1,33},{2,34},{3,35},{4,36},{5,37},{6,38},{7,39},{8,40},{9,... | collective-permute-start | bytes 165896 | tf_op jit(solution)/shard_map/ppermute | solution.py:510
  73.9 4.6 %collective-permute-start.8 = (bf16[280,128]{1,0:T(8,128)(2,1)S(1)}, bf16[280,128]{1,0:T(8,128)(2,1)S(1)}, u32[]{:S(2)}, u32[]{:S(2)}) collective-permute-start(bf16[280,128]{1,0:T(8,128)(2,1)S(1)} %pad_maximum_fusion), channel_id=1, source_target_pairs={{0,64},{1,65},{2,66},{3,67},{4,68},{5,69},{6,70},{7,71},{8,72},{9,... | collective-permute-start | bytes 215048 | tf_op jit(solution)/shard_map/ppermute | solution.py:510
  78.6 4.4 %collective-permute-start.9 = (bf16[280,128]{1,0:T(8,128)(2,1)S(1)}, bf16[280,128]{1,0:T(8,128)(2,1)S(1)}, u32[]{:S(2)}, u32[]{:S(2)}) collective-permute-start(bf16[280,128]{1,0:T(8,128)(2,1)S(1)} %add_convert_fusion.3), channel_id=1, source_target_pairs={{0,192},{1,193},{2,194},{3,195},{4,196},{5,197},{6,198},{7,199},{8... | collective-permute-start | bytes 215048 | tf_op jit(solution)/shard_map/ppermute | solution.py:510
  79.9 5.3 %collective-permute-start.6 = (bf16[64,128]{1,0:T(8,128)(2,1)S(1)}, bf16[64,128]{1,0:T(8,128)(2,1)S(1)}, u32[]{:S(2)}, u32[]{:S(2)}) collective-permute-start(bf16[64,128]{1,0:T(8,128)(2,1)S(1)} %get-tuple-element.42), channel_id=1, source_target_pairs={{0,1},{1,0},{2,3},{3,2},{4,5},{5,4},{6,7},{7,6},{8,9},{9,8},{10,11... | collective-permute-start | bytes 49160 | tf_op jit(solution)/shard_map/ppermute | solution.py:510
  83.0 5.5 %collective-permute-start.10 = (bf16[216,128]{1,0:T(8,128)(2,1)S(1)}, bf16[216,128]{1,0:T(8,128)(2,1)S(1)}, u32[]{:S(2)}, u32[]{:S(2)}) collective-permute-start(bf16[216,128]{1,0:T(8,128)(2,1)S(1)} %slice.8), channel_id=1, source_target_pairs={{0,33},{1,32},{2,35},{3,34},{4,37},{5,36},{6,39},{7,38},{8,41},{9,... | collective-permute-start | bytes 165896 | tf_op jit(solution)/shard_map/ppermute | solution.py:510
  88.5 8.8 %collective-permute-start.11 = (bf16[280,128]{1,0:T(8,128)(2,1)S(1)}, bf16[280,128]{1,0:T(8,128)(2,1)S(1)}, u32[]{:S(2)}, u32[]{:S(2)}) collective-permute-start(bf16[280,128]{1,0:T(8,128)(2,1)S(1)} %pad_maximum_fusion.1), channel_id=1, source_target_pairs={{0,2},{1,3},{2,0},{3,1},{4,6},{5,7},{6,4},{7,5},{8,10},{9,11},{10,... | collective-permute-start | bytes 215048 | tf_op jit(solution)/shard_map/ppermute | solution.py:510
  88.6 20.6 %collective-permute-start.16 = (f32[64,64]{1,0:T(8,128)S(1)}, f32[64,64]{1,0:T(8,128)S(1)}, u32[]{:S(2)}, u32[]{:S(2)}) collective-permute-start(f32[64,64]{1,0:T(8,128)S(1)} %get-tuple-element.45.direct_ref), channel_id=1, source_target_pairs={{0,0},{1,16},{2,32},{3,48},{4,64},{5,80},{6,96},{7,112},{8,128},{9... | collective-permute-start | bytes 49160 | tf_op jit(solution)/shard_map/ppermute | solution.py:515
  95.1 3.1 %collective-permute-start.14 = (bf16[64,128]{1,0:T(8,128)(2,1)S(1)}, bf16[64,128]{1,0:T(8,128)(2,1)S(1)}, u32[]{:S(2)}, u32[]{:S(2)}) collective-permute-start(bf16[64,128]{1,0:T(8,128)(2,1)S(1)} %slice.9), channel_id=1, source_target_pairs={{0,16},{1,17},{2,18},{3,19},{4,20},{5,21},{6,22},{7,23},{8,24},{9,... | collective-permute-start | bytes 49160 | tf_op jit(solution)/shard_map/ppermute | solution.py:510
  97.4 5.8 %collective-permute-start.12 = (bf16[280,128]{1,0:T(8,128)(2,1)S(1)}, bf16[280,128]{1,0:T(8,128)(2,1)S(1)}, u32[]{:S(2)}, u32[]{:S(2)}) collective-permute-start(bf16[280,128]{1,0:T(8,128)(2,1)S(1)} %add_convert_fusion.1), channel_id=1, source_target_pairs={{0,4},{1,5},{2,6},{3,7},{4,0},{5,1},{6,2},{7,3},{8,12},{9,13},{10,... | collective-permute-start | bytes 215048 | tf_op jit(solution)/shard_map/ppermute | solution.py:510
  98.2 11.0 %collective-permute-start.15 = (bf16[64,128]{1,0:T(8,128)(2,1)S(1)}, bf16[64,128]{1,0:T(8,128)(2,1)S(1)}, u32[]{:S(2)}, u32[]{:S(2)}) collective-permute-start(bf16[64,128]{1,0:T(8,128)(2,1)S(1)} %add_convert_fusion.8), channel_id=1, source_target_pairs={{0,32},{1,33},{2,34},{3,35},{4,36},{5,37},{6,38},{7,39},{8,40},{9,... | collective-permute-start | bytes 49160 | tf_op jit(solution)/shard_map/ppermute | solution.py:510
  103.2 9.4 %collective-permute-start.13 = (bf16[280,128]{1,0:T(8,128)(2,1)S(1)}, bf16[280,128]{1,0:T(8,128)(2,1)S(1)}, u32[]{:S(2)}, u32[]{:S(2)}) collective-permute-start(bf16[280,128]{1,0:T(8,128)(2,1)S(1)} %add_convert_fusion.mine_ref), channel_id=1, source_target_pairs={{0,12},{1,13},{2,14},{3,15},{4,8},{5,9},{6,10},{7,11},{8,4},{9,5},... | collective-permute-start | bytes 215048 | tf_op jit(solution)/shard_map/ppermute | solution.py:510
  (3 other events, 18.8 us)

commit v6 on v5

--- a/solution.py
+++ b/solution.py
@@ -172,7 +172,8 @@
         return carry
 
     blocks = (last - first) // rows
-    lax.fori_loop(1, blocks, body, 0)
+    for step in range(1, blocks):
+        body(step, 0)
     use(last - rows)
     return blocks - 1
 

time: 114 us -> 108 us (0.947)
  Pallas kernels: 29.1 us -> 22.8 us
    pallas_call x1, Pallas kernels: 17.5 us -> 12 us  [on_device(): call(main_kernel, [shape(TILE, TILE), shape(216, 128, dtype=BF16), shape(...]
where the time goes in v6:
time: 108 us; the launch traced here: 107 us
  starting transfers between devices  56.3 us (52%)
  waiting for transfers between devices  26 us (24%)
  Pallas kernels  22.8 us (21%)
    ppermute x11, waiting for transfers between devices, flipped(): return lax.ppermute(value, ('row', 'col'), pairs)  19.4 us
    ppermute x11, starting transfers between devices, flipped(): return lax.ppermute(value, ('row', 'col'), pairs)  16 us
    all_to_all x1, starting transfers between devices, on_device(): gathered = lax.all_to_all(sent, ('row', 'col'), 0, 0)  14 us
    pallas_call x1, Pallas kernels, on_device(): call(main_kernel, [shape(TILE, TILE), shape(216, 128, dtype=BF16), shape(...  12 us
    ppermute x1, starting transfers between devices, on_device(): direct_other = lax.ppermute(direct, ('row', 'col'), swap)  6.49 us
    ppermute x1, starting transfers between devices, on_device(): from_left = lax.ppermute(right_edge, 'col', up)  5.04 us
    ppermute x1, starting transfers between devices, on_device(): mirrored = lax.ppermute(cotangent, ('row', 'col'), swap)  4.77 us
    ppermute x1, starting transfers between devices, on_device(): below = lax.ppermute(upper, 'row', down)  4.69 us
  transfers between devices with their start and end apart: 18, of which 10 were waited for; matrix products, arithmetic and copies ran while one was open for 0% of the time, Pallas kernels for 9%

profile of v6, /device:TPU:40, one launch (start us, length us, event | category | flops | bytes accessed | tf_op | source)
XLA Modules:
  0.0 107.2 jit_solution(14449633463685812383)
XLA Ops:
  0.7 4.8 %collective-permute-start = (f32[64,64]{1,0:T(8,128)}, f32[64,64]{1,0:T(8,128)S(1)}, u32[]{:S(2)}, u32[]{:S(2)}) collective-permute-start(f32[64,64]{1,0:T(8,128)} %cot_ref.1), channel_id=1, source_target_pairs={{0,0},{1,16},{2,32},{3,48},{4,64},{5,80},{6,96},{7,112},{8,128},{9... | collective-permute-start | bytes 49160 | tf_op jit(solution)/shard_map/ppermute | solution.py:457
  6.9 14.0 %all-to-all-start = ((bf16[256,4,128]{2,1,0:T(4,128)(2,1)}), bf16[256,4,128]{2,1,0:T(4,128)(2,1)S(1)}, u32[]{:S(2)}, u32[]{:S(2)}) async-start(bf16[256,4,128]{2,1,0:T(4,128)(2,1)} %shard_map.120), calls=%async_computation | async-start | bytes 524288 | tf_op jit(solution)/shard_map/all_to_all | solution.py:461
  21.5 5.0 %collective-permute-start.1 = (bf16[17,32,128]{2,1,0:T(8,128)(2,1)S(1)}, bf16[17,32,128]{2,1,0:T(8,128)(2,1)S(1)}, u32[]{:S(2)}, u32[]{:S(2)}) collective-permute-start(bf16[17,32,128]{2,1,0:T(8,128)(2,1)S(1)} %get-tuple-element.28), channel_id=1, source_target_pairs={{0,1},{1,2},{2,3},{3,4},{4,5},{5,6},{6,7},{7,8},{8,9},{9,10},{10,1... | collective-permute-start | bytes 417800 | tf_op jit(solution)/shard_map/ppermute | solution.py:472
  26.6 3.3 %collective-permute-start.2 = (bf16[17,32,128]{2,1,0:T(8,128)(2,1)S(1)}, bf16[17,32,128]{2,1,0:T(8,128)(2,1)S(1)}, u32[]{:S(2)}, u32[]{:S(2)}) collective-permute-start(bf16[17,32,128]{2,1,0:T(8,128)(2,1)S(1)} %get-tuple-element.29), channel_id=1, source_target_pairs={{1,0},{2,1},{3,2},{4,3},{5,4},{6,5},{7,6},{8,7},{9,8},{10,9},{11,1... | collective-permute-start | bytes 417800 | tf_op jit(solution)/shard_map/ppermute | solution.py:473
  30.0 3.7 %collective-permute-done.1.from_left_ref = bf16[17,32,128]{2,1,0:T(8,128)(2,1)S(1)} collective-permute-done((bf16[17,32,128]{2,1,0:T(8,128)(2,1)S(1)}, bf16[17,32,128]{2,1,0:T(8,128)(2,1)S(1)}, u32[]{:S(2)}, u32[]{:S(2)}) %collective-permute-start.1) | collective-permute-done | bytes 139296 | tf_op jit(solution)/shard_map/ppermute | solution.py:472
  33.7 2.9 %collective-permute-done.2.from_right_ref = bf16[17,32,128]{2,1,0:T(8,128)(2,1)S(1)} collective-permute-done((bf16[17,32,128]{2,1,0:T(8,128)(2,1)S(1)}, bf16[17,32,128]{2,1,0:T(8,128)(2,1)S(1)}, u32[]{:S(2)}, u32[]{:S(2)}) %collective-permute-start.2) | collective-permute-done | bytes 139296 | tf_op jit(solution)/shard_map/ppermute | solution.py:473
  37.0 2.0 %collective-permute-start.3 = (bf16[34,32,128]{2,1,0:T(8,128)(2,1)S(1)}, bf16[34,32,128]{2,1,0:T(8,128)(2,1)S(1)}, u32[]{:S(2)}, u32[]{:S(2)}) collective-permute-start(bf16[34,32,128]{2,1,0:T(8,128)(2,1)S(1)} %get-tuple-element.30.part2_ref), channel_id=1, source_target_pairs={{0,16},{16,32},{32,48},{48,64},{64,80},{80,96},{96,112},{112,128},... | collective-permute-start | bytes 835592 | tf_op jit(solution)/shard_map/ppermute | solution.py:478
  38.9 4.7 %collective-permute-start.4 = (bf16[34,32,128]{2,1,0:T(8,128)(2,1)S(1)}, bf16[34,32,128]{2,1,0:T(8,128)(2,1)S(1)}, u32[]{:S(2)}, u32[]{:S(2)}) collective-permute-start(bf16[34,32,128]{2,1,0:T(8,128)(2,1)S(1)} %get-tuple-element.31.part1_ref), channel_id=1, source_target_pairs={{16,0},{32,16},{48,32},{64,48},{80,64},{96,80},{112,96},{128,112},... | collective-permute-start | bytes 835592 | tf_op jit(solution)/shard_map/ppermute | solution.py:479
  43.7 4.5 %shard_map.121 = (f32[128,32,128]{2,1,0:T(8,128)S(1)}, f32[128,128]{1,0:T(8,128)S(1)}, f32[128,128]{1,0:T(8,128)S(1)}, bf16[3,32,288]{2,1,0:T(8,128)(2,1)S(1)}) custom-call(s32[8]{0:T(128)S(1)} %pad_add_fusion.place_ref, bf16[256,4,128]{2,1,0:T(4,128)(2,1)S(1)} %all-to-all-done.feat_ref, bf16[128,128]{1,0:T(8,128)(2,1)S(1)} %copy-done.3, ...), custom_call_target="tpu_custom_call" | custom-call | flops 6000000000 | bytes 18000000 | tf_op jit(solution)/shard_map/pallas_call | solution.py:481
  48.3 12.0 %shard_map.124 = (f32[64,64]{1,0:T(8,128)S(1)}, bf16[216,128]{1,0:T(8,128)(2,1)S(1)}, f32[80,32,128]{2,1,0:T(8,128)S(1)}, bf16[80,32,128]{2,1,0:T(8,128)(2,1)S(1)}) custom-call(s32[8]{0:T(128)S(1)} %pad_add_fusion.place_ref, f32[128,32,128]{2,1,0:T(8,128)S(1)} %get-tuple-element.25.mixed_ref, bf16[34,32,128]{2,1,0:T(8,128)(2,1)S(1)} %collective-permute-done.3.part0_ref, ...), custom_call_target="tpu_custom_call" | custom-call | flops 24000000000 | bytes 72000000 | tf_op jit(solution)/shard_map/pallas_call | solution.py:492
  61.7 2.5 %collective-permute-start.7 = (bf16[216,128]{1,0:T(8,128)(2,1)S(1)}, bf16[216,128]{1,0:T(8,128)(2,1)S(1)}, u32[]{:S(2)}, u32[]{:S(2)}) collective-permute-start(bf16[216,128]{1,0:T(8,128)(2,1)S(1)} %add_convert_fusion.6), channel_id=1, source_target_pairs={{0,32},{1,33},{2,34},{3,35},{4,36},{5,37},{6,38},{7,39},{8,40},{9,... | collective-permute-start | bytes 165896 | tf_op jit(solution)/shard_map/ppermute | solution.py:511
  64.2 3.7 %shard_map.125 = (bf16[64,128]{1,0:T(8,128)(2,1)S(1)}, bf16[64,128]{1,0:T(8,128)(2,1)S(1)}) custom-call(s32[8]{0:T(128)S(1)} %pad_add_fusion.place_ref, f32[80,32,128]{2,1,0:T(8,128)S(1)} %get-tuple-element.38.grad_ref, bf16[80,32,128]{2,1,0:T(8,128)(2,1)S(1)} %get-tuple-element.39.round_ref, f32[128,128]{1,0:T(8,128)S(1)} %get-tuple-element.40.rows_ref, ...), custom_call_target="tpu_custom_call" | custom-call | flops 7000000000 | bytes 21000000 | tf_op jit(solution)/shard_map/pallas_call | solution.py:522
  68.5 3.8 %collective-permute-done.8 = bf16[280,128]{1,0:T(8,128)(2,1)S(1)} collective-permute-done((bf16[280,128]{1,0:T(8,128)(2,1)S(1)}, bf16[280,128]{1,0:T(8,128)(2,1)S(1)}, u32[]{:S(2)}, u32[]{:S(2)}) %collective-permute-start.8) | collective-permute-done | bytes 71712 | tf_op jit(solution)/shard_map/ppermute | solution.py:511
  72.3 1.3 %collective-permute-start.9 = (bf16[280,128]{1,0:T(8,128)(2,1)S(1)}, bf16[280,128]{1,0:T(8,128)(2,1)S(1)}, u32[]{:S(2)}, u32[]{:S(2)}) collective-permute-start(bf16[280,128]{1,0:T(8,128)(2,1)S(1)} %add_convert_fusion.3), channel_id=1, source_target_pairs={{0,192},{1,193},{2,194},{3,195},{4,196},{5,197},{6,198},{7,199},{8... | collective-permute-start | bytes 215048 | tf_op jit(solution)/shard_map/ppermute | solution.py:511
  73.7 1.4 %collective-permute-start.6 = (bf16[64,128]{1,0:T(8,128)(2,1)S(1)}, bf16[64,128]{1,0:T(8,128)(2,1)S(1)}, u32[]{:S(2)}, u32[]{:S(2)}) collective-permute-start(bf16[64,128]{1,0:T(8,128)(2,1)S(1)} %get-tuple-element.42), channel_id=1, source_target_pairs={{0,1},{1,0},{2,3},{3,2},{4,5},{5,4},{6,7},{7,6},{8,9},{9,8},{10,11... | collective-permute-start | bytes 49160 | tf_op jit(solution)/shard_map/ppermute | solution.py:511
  75.1 1.7 %collective-permute-done.9 = bf16[280,128]{1,0:T(8,128)(2,1)S(1)} collective-permute-done((bf16[280,128]{1,0:T(8,128)(2,1)S(1)}, bf16[280,128]{1,0:T(8,128)(2,1)S(1)}, u32[]{:S(2)}, u32[]{:S(2)}) %collective-permute-start.9) | collective-permute-done | bytes 71712 | tf_op jit(solution)/shard_map/ppermute | solution.py:511
  77.3 1.7 %collective-permute-done.6 = bf16[64,128]{1,0:T(8,128)(2,1)S(1)} collective-permute-done((bf16[64,128]{1,0:T(8,128)(2,1)S(1)}, bf16[64,128]{1,0:T(8,128)(2,1)S(1)}, u32[]{:S(2)}, u32[]{:S(2)}) %collective-permute-start.6) | collective-permute-done | bytes 16416 | tf_op jit(solution)/shard_map/ppermute | solution.py:511
  79.0 3.2 %collective-permute-done.10 = bf16[216,128]{1,0:T(8,128)(2,1)S(1)} collective-permute-done((bf16[216,128]{1,0:T(8,128)(2,1)S(1)}, bf16[216,128]{1,0:T(8,128)(2,1)S(1)}, u32[]{:S(2)}, u32[]{:S(2)}) %collective-permute-start.10) | collective-permute-done | bytes 55328 | tf_op jit(solution)/shard_map/ppermute | solution.py:511
  82.4 6.5 %collective-permute-start.16 = (f32[64,64]{1,0:T(8,128)S(1)}, f32[64,64]{1,0:T(8,128)S(1)}, u32[]{:S(2)}, u32[]{:S(2)}) collective-permute-start(f32[64,64]{1,0:T(8,128)S(1)} %get-tuple-element.45.direct_ref), channel_id=1, source_target_pairs={{0,0},{1,16},{2,32},{3,48},{4,64},{5,80},{6,96},{7,112},{8,128},{9... | collective-permute-start | bytes 49160 | tf_op jit(solution)/shard_map/ppermute | solution.py:516
  88.9 2.5 %collective-permute-start.14 = (bf16[64,128]{1,0:T(8,128)(2,1)S(1)}, bf16[64,128]{1,0:T(8,128)(2,1)S(1)}, u32[]{:S(2)}, u32[]{:S(2)}) collective-permute-start(bf16[64,128]{1,0:T(8,128)(2,1)S(1)} %slice.9), channel_id=1, source_target_pairs={{0,16},{1,17},{2,18},{3,19},{4,20},{5,21},{6,22},{7,23},{8,24},{9,... | collective-permute-start | bytes 49160 | tf_op jit(solution)/shard_map/ppermute | solution.py:511
  92.6 4.6 %collective-permute-done.12 = bf16[280,128]{1,0:T(8,128)(2,1)S(1)} collective-permute-done((bf16[280,128]{1,0:T(8,128)(2,1)S(1)}, bf16[280,128]{1,0:T(8,128)(2,1)S(1)}, u32[]{:S(2)}, u32[]{:S(2)}) %collective-permute-start.12) | collective-permute-done | bytes 71712 | tf_op jit(solution)/shard_map/ppermute | solution.py:511
  97.2 5.9 %collective-permute-start.13 = (bf16[280,128]{1,0:T(8,128)(2,1)S(1)}, bf16[280,128]{1,0:T(8,128)(2,1)S(1)}, u32[]{:S(2)}, u32[]{:S(2)}) collective-permute-start(bf16[280,128]{1,0:T(8,128)(2,1)S(1)} %add_convert_fusion.mine_ref), channel_id=1, source_target_pairs={{0,12},{1,13},{2,14},{3,15},{4,8},{5,9},{6,10},{7,11},{8,4},{9,5},... | collective-permute-start | bytes 215048 | tf_op jit(solution)/shard_map/ppermute | solution.py:511
  103.2 3.1 %collective-permute-done.13.got_ref = bf16[280,128]{1,0:T(8,128)(2,1)S(1)} collective-permute-done((bf16[280,128]{1,0:T(8,128)(2,1)S(1)}, bf16[280,128]{1,0:T(8,128)(2,1)S(1)}, u32[]{:S(2)}, u32[]{:S(2)}) %collective-permute-start.13) | collective-permute-done | bytes 71712 | tf_op jit(solution)/shard_map/ppermute | solution.py:511
  106.2 1.0 shard_map.126
  (54 shorter events, 6.4 us)
Async XLA Ops:
  0.6 20.3 %copy-start.2 = (f32[64,64]{1,0:T(8,128)S(1)}, f32[64,64]{1,0:T(8,128)}, u32[]{:S(2)}) copy-start(f32[64,64]{1,0:T(8,128)} %cot_ref.1) | copy-start | bytes 49156
  0.6 20.3 %copy-start = (bf16[32,64,64]{2,1,0:T(8,128)(2,1)S(1)}, bf16[32,64,64]{2,1,0:T(8,128)(2,1)}, u32[]{:S(2)}) copy-start(bf16[32,64,64]{2,1,0:T(8,128)(2,1)} %pair_ref.1) | copy-start | bytes 786436
  0.7 20.3 %collective-permute-start = (f32[64,64]{1,0:T(8,128)}, f32[64,64]{1,0:T(8,128)S(1)}, u32[]{:S(2)}, u32[]{:S(2)}) collective-permute-start(f32[64,64]{1,0:T(8,128)} %cot_ref.1), channel_id=1, source_target_pairs={{0,0},{1,16},{2,32},{3,48},{4,64},{5,80},{6,96},{7,112},{8,128},{9... | collective-permute-start | bytes 49160 | tf_op jit(solution)/shard_map/ppermute | solution.py:457
  6.9 36.8 %all-to-all-start = ((bf16[256,4,128]{2,1,0:T(4,128)(2,1)}), bf16[256,4,128]{2,1,0:T(4,128)(2,1)S(1)}, u32[]{:S(2)}, u32[]{:S(2)}) async-start(bf16[256,4,128]{2,1,0:T(4,128)(2,1)} %shard_map.120), calls=%async_computation | async-start | bytes 524288 | tf_op jit(solution)/shard_map/all_to_all | solution.py:461
  21.5 22.2 %copy-start.1 = (bf16[3,32,288]{2,1,0:T(8,128)(2,1)S(1)}, bf16[3,32,288]{2,1,0:T(8,128)(2,1)}, u32[]{:S(2)}) copy-start(bf16[3,32,288]{2,1,0:T(8,128)(2,1)} %forward_ref.1) | copy-start | bytes 165892
  21.5 22.2 %copy-start.3 = (bf16[128,128]{1,0:T(8,128)(2,1)S(1)}, bf16[128,128]{1,0:T(8,128)(2,1)}, u32[]{:S(2)}) copy-start(bf16[128,128]{1,0:T(8,128)(2,1)} %w_left_ref.3) | copy-start | bytes 98308
  21.5 22.2 %copy-start.4 = (bf16[128,128]{1,0:T(8,128)(2,1)S(1)}, bf16[128,128]{1,0:T(8,128)(2,1)}, u32[]{:S(2)}) copy-start(bf16[128,128]{1,0:T(8,128)(2,1)} %w_right_ref.3) | copy-start | bytes 98308
  21.5 22.2 %copy-start.5 = (bf16[32,128]{1,0:T(8,128)(2,1)S(1)}, bf16[32,128]{1,0:T(8,128)(2,1)}, u32[]{:S(2)}) copy-start(bf16[32,128]{1,0:T(8,128)(2,1)} %w_in_ref.3) | copy-start | bytes 24580
  21.5 12.2 %collective-permute-start.1 = (bf16[17,32,128]{2,1,0:T(8,128)(2,1)S(1)}, bf16[17,32,128]{2,1,0:T(8,128)(2,1)S(1)}, u32[]{:S(2)}, u32[]{:S(2)}) collective-permute-start(bf16[17,32,128]{2,1,0:T(8,128)(2,1)S(1)} %get-tuple-element.28), channel_id=1, source_target_pairs={{0,1},{1,2},{2,3},{3,4},{4,5},{5,6},{6,7},{7,8},{8,9},{9,10},{10,1... | collective-permute-start | bytes 417800 | tf_op jit(solution)/shard_map/ppermute | solution.py:472
  26.6 10.0 %collective-permute-start.2 = (bf16[17,32,128]{2,1,0:T(8,128)(2,1)S(1)}, bf16[17,32,128]{2,1,0:T(8,128)(2,1)S(1)}, u32[]{:S(2)}, u32[]{:S(2)}) collective-permute-start(bf16[17,32,128]{2,1,0:T(8,128)(2,1)S(1)} %get-tuple-element.29), channel_id=1, source_target_pairs={{1,0},{2,1},{3,2},{4,3},{5,4},{6,5},{7,6},{8,7},{9,8},{10,9},{11,1... | collective-permute-start | bytes 417800 | tf_op jit(solution)/shard_map/ppermute | solution.py:473
  37.0 11.2 %collective-permute-start.3 = (bf16[34,32,128]{2,1,0:T(8,128)(2,1)S(1)}, bf16[34,32,128]{2,1,0:T(8,128)(2,1)S(1)}, u32[]{:S(2)}, u32[]{:S(2)}) collective-permute-start(bf16[34,32,128]{2,1,0:T(8,128)(2,1)S(1)} %get-tuple-element.30.part2_ref), channel_id=1, source_target_pairs={{0,16},{16,32},{32,48},{48,64},{64,80},{80,96},{96,112},{112,128},... | collective-permute-start | bytes 835592 | tf_op jit(solution)/shard_map/ppermute | solution.py:478
  38.9 9.3 %collective-permute-start.4 = (bf16[34,32,128]{2,1,0:T(8,128)(2,1)S(1)}, bf16[34,32,128]{2,1,0:T(8,128)(2,1)S(1)}, u32[]{:S(2)}, u32[]{:S(2)}) collective-permute-start(bf16[34,32,128]{2,1,0:T(8,128)(2,1)S(1)} %get-tuple-element.31.part1_ref), channel_id=1, source_target_pairs={{16,0},{32,16},{48,32},{64,48},{80,64},{96,80},{112,96},{128,112},... | collective-permute-start | bytes 835592 | tf_op jit(solution)/shard_map/ppermute | solution.py:479
  60.3 1.3 %collective-permute-start.5 = (bf16[216,128]{1,0:T(8,128)(2,1)S(1)}, bf16[216,128]{1,0:T(8,128)(2,1)S(1)}, u32[]{:S(2)}, u32[]{:S(2)}) collective-permute-start(bf16[216,128]{1,0:T(8,128)(2,1)S(1)} %get-tuple-element.37), channel_id=1, source_target_pairs={{0,16},{1,17},{2,18},{3,19},{4,20},{5,21},{6,22},{7,23},{8,24},{9,... | collective-permute-start | bytes 165896 | tf_op jit(solution)/shard_map/ppermute | solution.py:511
  61.7 6.1 %collective-permute-start.7 = (bf16[216,128]{1,0:T(8,128)(2,1)S(1)}, bf16[216,128]{1,0:T(8,128)(2,1)S(1)}, u32[]{:S(2)}, u32[]{:S(2)}) collective-permute-start(bf16[216,128]{1,0:T(8,128)(2,1)S(1)} %add_convert_fusion.6), channel_id=1, source_target_pairs={{0,32},{1,33},{2,34},{3,35},{4,36},{5,37},{6,38},{7,39},{8,40},{9,... | collective-permute-start | bytes 165896 | tf_op jit(solution)/shard_map/ppermute | solution.py:511
  67.9 4.4 %collective-permute-start.8 = (bf16[280,128]{1,0:T(8,128)(2,1)S(1)}, bf16[280,128]{1,0:T(8,128)(2,1)S(1)}, u32[]{:S(2)}, u32[]{:S(2)}) collective-permute-start(bf16[280,128]{1,0:T(8,128)(2,1)S(1)} %pad_maximum_fusion), channel_id=1, source_target_pairs={{0,64},{1,65},{2,66},{3,67},{4,68},{5,69},{6,70},{7,71},{8,72},{9,... | collective-permute-start | bytes 215048 | tf_op jit(solution)/shard_map/ppermute | solution.py:511
  72.3 4.4 %collective-permute-start.9 = (bf16[280,128]{1,0:T(8,128)(2,1)S(1)}, bf16[280,128]{1,0:T(8,128)(2,1)S(1)}, u32[]{:S(2)}, u32[]{:S(2)}) collective-permute-start(bf16[280,128]{1,0:T(8,128)(2,1)S(1)} %add_convert_fusion.3), channel_id=1, source_target_pairs={{0,192},{1,193},{2,194},{3,195},{4,196},{5,197},{6,198},{7,199},{8... | collective-permute-start | bytes 215048 | tf_op jit(solution)/shard_map/ppermute | solution.py:511
  73.7 5.3 %collective-permute-start.6 = (bf16[64,128]{1,0:T(8,128)(2,1)S(1)}, bf16[64,128]{1,0:T(8,128)(2,1)S(1)}, u32[]{:S(2)}, u32[]{:S(2)}) collective-permute-start(bf16[64,128]{1,0:T(8,128)(2,1)S(1)} %get-tuple-element.42), channel_id=1, source_target_pairs={{0,1},{1,0},{2,3},{3,2},{4,5},{5,4},{6,7},{7,6},{8,9},{9,8},{10,11... | collective-permute-start | bytes 49160 | tf_op jit(solution)/shard_map/ppermute | solution.py:511
  76.8 5.5 %collective-permute-start.10 = (bf16[216,128]{1,0:T(8,128)(2,1)S(1)}, bf16[216,128]{1,0:T(8,128)(2,1)S(1)}, u32[]{:S(2)}, u32[]{:S(2)}) collective-permute-start(bf16[216,128]{1,0:T(8,128)(2,1)S(1)} %slice.8), channel_id=1, source_target_pairs={{0,33},{1,32},{2,35},{3,34},{4,37},{5,36},{6,39},{7,38},{8,41},{9,... | collective-permute-start | bytes 165896 | tf_op jit(solution)/shard_map/ppermute | solution.py:511
  82.3 9.1 %collective-permute-start.11 = (bf16[280,128]{1,0:T(8,128)(2,1)S(1)}, bf16[280,128]{1,0:T(8,128)(2,1)S(1)}, u32[]{:S(2)}, u32[]{:S(2)}) collective-permute-start(bf16[280,128]{1,0:T(8,128)(2,1)S(1)} %pad_maximum_fusion.1), channel_id=1, source_target_pairs={{0,2},{1,3},{2,0},{3,1},{4,6},{5,7},{6,4},{7,5},{8,10},{9,11},{10,... | collective-permute-start | bytes 215048 | tf_op jit(solution)/shard_map/ppermute | solution.py:511
  82.4 20.8 %collective-permute-start.16 = (f32[64,64]{1,0:T(8,128)S(1)}, f32[64,64]{1,0:T(8,128)S(1)}, u32[]{:S(2)}, u32[]{:S(2)}) collective-permute-start(f32[64,64]{1,0:T(8,128)S(1)} %get-tuple-element.45.direct_ref), channel_id=1, source_target_pairs={{0,0},{1,16},{2,32},{3,48},{4,64},{5,80},{6,96},{7,112},{8,128},{9... | collective-permute-start | bytes 49160 | tf_op jit(solution)/shard_map/ppermute | solution.py:516
  88.9 3.3 %collective-permute-start.14 = (bf16[64,128]{1,0:T(8,128)(2,1)S(1)}, bf16[64,128]{1,0:T(8,128)(2,1)S(1)}, u32[]{:S(2)}, u32[]{:S(2)}) collective-permute-start(bf16[64,128]{1,0:T(8,128)(2,1)S(1)} %slice.9), channel_id=1, source_target_pairs={{0,16},{1,17},{2,18},{3,19},{4,20},{5,21},{6,22},{7,23},{8,24},{9,... | collective-permute-start | bytes 49160 | tf_op jit(solution)/shard_map/ppermute | solution.py:511
  91.4 5.8 %collective-permute-start.12 = (bf16[280,128]{1,0:T(8,128)(2,1)S(1)}, bf16[280,128]{1,0:T(8,128)(2,1)S(1)}, u32[]{:S(2)}, u32[]{:S(2)}) collective-permute-start(bf16[280,128]{1,0:T(8,128)(2,1)S(1)} %add_convert_fusion.1), channel_id=1, source_target_pairs={{0,4},{1,5},{2,6},{3,7},{4,0},{5,1},{6,2},{7,3},{8,12},{9,13},{10,... | collective-permute-start | bytes 215048 | tf_op jit(solution)/shard_map/ppermute | solution.py:511
  92.2 10.9 %collective-permute-start.15 = (bf16[64,128]{1,0:T(8,128)(2,1)S(1)}, bf16[64,128]{1,0:T(8,128)(2,1)S(1)}, u32[]{:S(2)}, u32[]{:S(2)}) collective-permute-start(bf16[64,128]{1,0:T(8,128)(2,1)S(1)} %add_convert_fusion.8), channel_id=1, source_target_pairs={{0,32},{1,33},{2,34},{3,35},{4,36},{5,37},{6,38},{7,39},{8,40},{9,... | collective-permute-start | bytes 49160 | tf_op jit(solution)/shard_map/ppermute | solution.py:511
  97.2 9.0 %collective-permute-start.13 = (bf16[280,128]{1,0:T(8,128)(2,1)S(1)}, bf16[280,128]{1,0:T(8,128)(2,1)S(1)}, u32[]{:S(2)}, u32[]{:S(2)}) collective-permute-start(bf16[280,128]{1,0:T(8,128)(2,1)S(1)} %add_convert_fusion.mine_ref), channel_id=1, source_target_pairs={{0,12},{1,13},{2,14},{3,15},{4,8},{5,9},{6,10},{7,11},{8,4},{9,5},... | collective-permute-start | bytes 215048 | tf_op jit(solution)/shard_map/ppermute | solution.py:511
  (3 other events, 19.0 us)

commit v7 on v6

--- a/solution.py
+++ b/solution.py
@@ -234,7 +234,8 @@
             activate(0, base, (mixed_ref[pl.ds(base, ROWS)] + given).astype(BF16))
             return carry
 
-        lax.fori_loop(0, HALO // ROWS, start, 0)
+        for step in range(HALO // ROWS):
+            start(step, 0)
 
     def next_state(base):
         block = pl.ds(base, ROWS)
@@ -336,7 +337,10 @@
         weight_terms(0, masked0_ref, step)
     terms = jnp.concatenate([total_ref[layer] for layer in range(3)], axis=0)
     spare = jnp.concatenate([terms[216:288, 32 * k : 32 * k + 32] for k in range(3)], axis=0)
-    terms_ref[...] = jnp.concatenate([terms[0:216], spare], axis=1).astype(BF16)
+    terms_ref[0:208, :] = jnp.concatenate([terms[0:208], spare[0:208]], axis=1).astype(BF16)
+    terms_ref[208:224, :] = jnp.concatenate(
+        [jnp.concatenate([terms[208:216], spare[208:216]], axis=1), jnp.zeros((8, 128), F32)], axis=0
+    ).astype(BF16)
 
 
 def last_kernel(
@@ -391,6 +395,7 @@
 
 
 def finish_kernel(
+    place_ref,
     mine_ref,
     got_ref,
     col_ref,
@@ -404,7 +409,10 @@
     conv_ref,
 ):
     logits_ref[...] = 0.5 * (direct_ref[...] + other_ref[...].T)
-    total = mine_ref[...].astype(F32) + got_ref[...].astype(F32)
+    total = mine_ref[...].astype(F32)
+    mine = total[TILE:]
+    other = got_ref[...].astype(F32)
+    second = place_ref[0] % 2 == 1
     for value, weight_ref, out_ref in (
         (total[0:TILE], w_left_ref, grad_rows_ref),
         (col_ref[...].astype(F32), w_right_ref, grad_cols_ref),
@@ -416,7 +424,9 @@
             precision=lax.Precision.HIGHEST,
             preferred_element_type=F32,
         )
-    terms = total[TILE:] * (1.0 / 1024.0)
+    terms = jnp.concatenate(
+        [jnp.where(second, other, mine), jnp.where(second, mine, other)], axis=0
+    )[0:216] * (1.0 / 1024.0)
     spare = jnp.concatenate([terms[72 * k : 72 * k + 72, 96:128] for k in range(3)], axis=1)
     terms = jnp.concatenate([terms[:, 0:96], spare], axis=0)
     for layer in range(3):
@@ -491,7 +501,7 @@
     big = (WIDE, CH, WIDE)
     direct, terms, grad, rounded = call(
         main_kernel,
-        [shape(TILE, TILE), shape(216, 128, dtype=BF16), shape(80, CH, WIDE), shape(80, CH, WIDE, dtype=BF16)],
+        [shape(TILE, TILE), shape(224, 128, dtype=BF16), shape(80, CH, WIDE), shape(80, CH, WIDE, dtype=BF16)],
         [SMEM] + [VMEM] * 8,
         [pltpu.VMEM(big, BF16)] * 4
         + [pltpu.VMEM(big, F32)]
@@ -514,7 +524,11 @@
         return (value.astype(F32) + flipped(value, row_bits, col_bits).astype(F32)).astype(BF16)
 
     direct_other = lax.ppermute(direct, ("row", "col"), swap)
-    terms = summed(terms, 1, 0)
+    second = row_at % 2 == 1
+    terms = jnp.where(second, terms[112:], terms[:112]).astype(F32) + flipped(
+        jnp.where(second, terms[:112], terms[112:]), 1, 0
+    ).astype(F32)
+    terms = terms.astype(BF16)
     grad, rounded, row_project, col_project, terms = lax.optimization_barrier(
         (grad, rounded, row_project, col_project, terms)
     )
@@ -543,12 +557,13 @@
     packed = summed(packed, 0, 2)
     col_part = summed(col_part, 2, 0)
     packed = summed(packed, 0, 4)
+    packed = summed(packed, 0, 12)
     return tuple(
         call(
             finish_kernel,
             [shape(TILE, TILE), shape(TILE, 128), shape(TILE, 128), shape(3, CH, 288)],
-            [VMEM] * 7,
-        )(packed, flipped(packed, 0, 12), col_part, w_left, w_right, direct, direct_other)
+            [SMEM] + [VMEM] * 7,
+        )(place, packed, flipped(packed[TILE:], 1, 0), col_part, w_left, w_right, direct, direct_other)
     )
 
 

time: 108 us -> 106 us (0.981)
  the two profiles are of different devices: /device:TPU:40 before, /device:TPU:1 now
where the time goes in v7:
time: 106 us
  starting transfers between devices  61.9 us (58%)
  Pallas kernels  22.4 us (21%)
  waiting for transfers between devices  19.1 us (18%)
    ppermute x12, starting transfers between devices, flipped(): return lax.ppermute(value, ('row', 'col'), pairs)  21.7 us
    all_to_all x1, starting transfers between devices, on_device(): gathered = lax.all_to_all(sent, ('row', 'col'), 0, 0)  14 us
    pallas_call x1, Pallas kernels, on_device(): call(main_kernel, [shape(TILE, TILE), shape(224, 128, dtype=BF16), shape(...  11 us
    ppermute x12, waiting for transfers between devices, flipped(): return lax.ppermute(value, ('row', 'col'), pairs)  9.96 us
    ppermute x1, starting transfers between devices, on_device(): direct_other = lax.ppermute(direct, ('row', 'col'), swap)  8.3 us
    ppermute x1, starting transfers between devices, on_device(): mirrored = lax.ppermute(cotangent, ('row', 'col'), swap)  6.17 us
    ppermute x1, starting transfers between devices, on_device(): from_left = lax.ppermute(right_edge, 'col', up)  4.93 us
    ppermute x1, waiting for transfers between devices, on_device(): from_right = lax.ppermute(left_edge, 'col', down)  4.9 us
  transfers between devices with their start and end apart: 19, of which 11 were waited for; matrix products, arithmetic and copies ran while one was open for 0% of the time, Pallas kernels for 9%

profile of v7, /device:TPU:1, one launch (start us, length us, event | category | flops | bytes accessed | tf_op | source)
XLA Modules:
  0.0 105.5 jit_solution(265474455727012612)
XLA Ops:
  0.7 6.2 %collective-permute-start = (f32[64,64]{1,0:T(8,128)}, f32[64,64]{1,0:T(8,128)S(1)}, u32[]{:S(2)}, u32[]{:S(2)}) collective-permute-start(f32[64,64]{1,0:T(8,128)} %cot_ref.1), channel_id=1, source_target_pairs={{0,0},{1,16},{2,32},{3,48},{4,64},{5,80},{6,96},{7,112},{8,128},{9... | collective-permute-start | bytes 49160 | tf_op jit(solution)/shard_map/ppermute | solution.py:467
  8.3 14.0 %all-to-all-start = ((bf16[256,4,128]{2,1,0:T(4,128)(2,1)}), bf16[256,4,128]{2,1,0:T(4,128)(2,1)S(1)}, u32[]{:S(2)}, u32[]{:S(2)}) async-start(bf16[256,4,128]{2,1,0:T(4,128)(2,1)} %shard_map.120), calls=%async_computation | async-start | bytes 524288 | tf_op jit(solution)/shard_map/all_to_all | solution.py:471
  22.8 4.9 %collective-permute-start.1 = (bf16[17,32,128]{2,1,0:T(8,128)(2,1)S(1)}, bf16[17,32,128]{2,1,0:T(8,128)(2,1)S(1)}, u32[]{:S(2)}, u32[]{:S(2)}) collective-permute-start(bf16[17,32,128]{2,1,0:T(8,128)(2,1)S(1)} %get-tuple-element.28), channel_id=1, source_target_pairs={{0,1},{1,2},{2,3},{3,4},{4,5},{5,6},{6,7},{7,8},{8,9},{9,10},{10,1... | collective-permute-start | bytes 417800 | tf_op jit(solution)/shard_map/ppermute | solution.py:482
  29.2 2.0 %collective-permute-done.1.from_left_ref = bf16[17,32,128]{2,1,0:T(8,128)(2,1)S(1)} collective-permute-done((bf16[17,32,128]{2,1,0:T(8,128)(2,1)S(1)}, bf16[17,32,128]{2,1,0:T(8,128)(2,1)S(1)}, u32[]{:S(2)}, u32[]{:S(2)}) %collective-permute-start.1) | collective-permute-done | bytes 139296 | tf_op jit(solution)/shard_map/ppermute | solution.py:482
  31.2 4.9 %collective-permute-done.2.from_right_ref = bf16[17,32,128]{2,1,0:T(8,128)(2,1)S(1)} collective-permute-done((bf16[17,32,128]{2,1,0:T(8,128)(2,1)S(1)}, bf16[17,32,128]{2,1,0:T(8,128)(2,1)S(1)}, u32[]{:S(2)}, u32[]{:S(2)}) %collective-permute-start.2) | collective-permute-done | bytes 139296 | tf_op jit(solution)/shard_map/ppermute | solution.py:483
  36.4 3.5 %collective-permute-start.3 = (bf16[34,32,128]{2,1,0:T(8,128)(2,1)S(1)}, bf16[34,32,128]{2,1,0:T(8,128)(2,1)S(1)}, u32[]{:S(2)}, u32[]{:S(2)}) collective-permute-start(bf16[34,32,128]{2,1,0:T(8,128)(2,1)S(1)} %get-tuple-element.30.part2_ref), channel_id=1, source_target_pairs={{0,16},{16,32},{32,48},{48,64},{64,80},{80,96},{96,112},{112,128},... | collective-permute-start | bytes 835592 | tf_op jit(solution)/shard_map/ppermute | solution.py:488
  39.9 2.1 %collective-permute-start.4 = (bf16[34,32,128]{2,1,0:T(8,128)(2,1)S(1)}, bf16[34,32,128]{2,1,0:T(8,128)(2,1)S(1)}, u32[]{:S(2)}, u32[]{:S(2)}) collective-permute-start(bf16[34,32,128]{2,1,0:T(8,128)(2,1)S(1)} %get-tuple-element.31.part1_ref), channel_id=1, source_target_pairs={{16,0},{32,16},{48,32},{64,48},{80,64},{96,80},{112,96},{128,112},... | collective-permute-start | bytes 835592 | tf_op jit(solution)/shard_map/ppermute | solution.py:489
  42.1 4.5 %shard_map.121 = (f32[128,32,128]{2,1,0:T(8,128)S(1)}, f32[128,128]{1,0:T(8,128)S(1)}, f32[128,128]{1,0:T(8,128)S(1)}, bf16[3,32,288]{2,1,0:T(8,128)(2,1)S(1)}) custom-call(s32[8]{0:T(128)S(1)} %pad_add_fusion.place_ref, bf16[256,4,128]{2,1,0:T(4,128)(2,1)S(1)} %all-to-all-done.feat_ref, bf16[128,128]{1,0:T(8,128)(2,1)S(1)} %copy-done.3, ...), custom_call_target="tpu_custom_call" | custom-call | flops 6000000000 | bytes 18000000 | tf_op jit(solution)/shard_map/pallas_call | solution.py:491
  46.6 2.3 %collective-permute-done.4.part3_ref = bf16[34,32,128]{2,1,0:T(8,128)(2,1)S(1)} collective-permute-done((bf16[34,32,128]{2,1,0:T(8,128)(2,1)S(1)}, bf16[34,32,128]{2,1,0:T(8,128)(2,1)S(1)}, u32[]{:S(2)}, u32[]{:S(2)}) %collective-permute-start.4) | collective-permute-done | bytes 278560 | tf_op jit(solution)/shard_map/ppermute | solution.py:489
  49.0 11.0 %shard_map.124 = (f32[64,64]{1,0:T(8,128)S(1)}, bf16[224,128]{1,0:T(8,128)(2,1)S(1)}, f32[80,32,128]{2,1,0:T(8,128)S(1)}, bf16[80,32,128]{2,1,0:T(8,128)(2,1)S(1)}) custom-call(s32[8]{0:T(128)S(1)} %pad_add_fusion.place_ref, f32[128,32,128]{2,1,0:T(8,128)S(1)} %get-tuple-element.25.mixed_ref, bf16[34,32,128]{2,1,0:T(8,128)(2,1)S(1)} %collective-permute-done.3.part0_ref, ...), custom_call_target="tpu_custom_call" | custom-call | flops 24000000000 | bytes 72000000 | tf_op jit(solution)/shard_map/pallas_call | solution.py:502
  61.3 2.2 %collective-permute-start.7 = (bf16[112,128]{1,0:T(8,128)(2,1)S(1)}, bf16[112,128]{1,0:T(8,128)(2,1)S(1)}, u32[]{:S(2)}, u32[]{:S(2)}) collective-permute-start(bf16[112,128]{1,0:T(8,128)(2,1)S(1)} %add_convert_fusion.7), channel_id=1, source_target_pairs={{0,32},{1,33},{2,34},{3,35},{4,36},{5,37},{6,38},{7,39},{8,40},{9,... | collective-permute-start | bytes 86024 | tf_op jit(solution)/shard_map/ppermute | solution.py:521
  63.5 3.7 %shard_map.125 = (bf16[64,128]{1,0:T(8,128)(2,1)S(1)}, bf16[64,128]{1,0:T(8,128)(2,1)S(1)}) custom-call(s32[8]{0:T(128)S(1)} %pad_add_fusion.place_ref, f32[80,32,128]{2,1,0:T(8,128)S(1)} %get-tuple-element.38.grad_ref, bf16[80,32,128]{2,1,0:T(8,128)(2,1)S(1)} %get-tuple-element.39.round_ref, f32[128,128]{1,0:T(8,128)S(1)} %get-tuple-element.40.rows_ref, ...), custom_call_target="tpu_custom_call" | custom-call | flops 7000000000 | bytes 21000000 | tf_op jit(solution)/shard_map/pallas_call | solution.py:536
  67.2 1.3 %collective-permute-start.8 = (bf16[176,128]{1,0:T(8,128)(2,1)S(1)}, bf16[176,128]{1,0:T(8,128)(2,1)S(1)}, u32[]{:S(2)}, u32[]{:S(2)}) collective-permute-start(bf16[176,128]{1,0:T(8,128)(2,1)S(1)} %pad_maximum_fusion), channel_id=1, source_target_pairs={{0,64},{1,65},{2,66},{3,67},{4,68},{5,69},{6,70},{7,71},{8,72},{9,... | collective-permute-start | bytes 135176 | tf_op jit(solution)/shard_map/ppermute | solution.py:521
  68.5 1.7 %collective-permute-done.8 = bf16[176,128]{1,0:T(8,128)(2,1)S(1)} collective-permute-done((bf16[176,128]{1,0:T(8,128)(2,1)S(1)}, bf16[176,128]{1,0:T(8,128)(2,1)S(1)}, u32[]{:S(2)}, u32[]{:S(2)}) %collective-permute-start.8) | collective-permute-done | bytes 45088 | tf_op jit(solution)/shard_map/ppermute | solution.py:521
  70.2 1.4 %collective-permute-start.9 = (bf16[176,128]{1,0:T(8,128)(2,1)S(1)}, bf16[176,128]{1,0:T(8,128)(2,1)S(1)}, u32[]{:S(2)}, u32[]{:S(2)}) collective-permute-start(bf16[176,128]{1,0:T(8,128)(2,1)S(1)} %add_convert_fusion.4), channel_id=1, source_target_pairs={{0,192},{1,193},{2,194},{3,195},{4,196},{5,197},{6,198},{7,199},{8... | collective-permute-start | bytes 135176 | tf_op jit(solution)/shard_map/ppermute | solution.py:521
  71.6 2.2 %collective-permute-start.6 = (bf16[64,128]{1,0:T(8,128)(2,1)S(1)}, bf16[64,128]{1,0:T(8,128)(2,1)S(1)}, u32[]{:S(2)}, u32[]{:S(2)}) collective-permute-start(bf16[64,128]{1,0:T(8,128)(2,1)S(1)} %get-tuple-element.42), channel_id=1, source_target_pairs={{0,1},{1,0},{2,3},{3,2},{4,5},{5,4},{6,7},{7,6},{8,9},{9,8},{10,11... | collective-permute-start | bytes 49160 | tf_op jit(solution)/shard_map/ppermute | solution.py:521
  75.7 2.7 %collective-permute-done.10 = bf16[112,128]{1,0:T(8,128)(2,1)S(1)} collective-permute-done((bf16[112,128]{1,0:T(8,128)(2,1)S(1)}, bf16[112,128]{1,0:T(8,128)(2,1)S(1)}, u32[]{:S(2)}, u32[]{:S(2)}) %collective-permute-start.10) | collective-permute-done | bytes 28704 | tf_op jit(solution)/shard_map/ppermute | solution.py:521
  78.5 2.5 %collective-permute-start.11 = (bf16[176,128]{1,0:T(8,128)(2,1)S(1)}, bf16[176,128]{1,0:T(8,128)(2,1)S(1)}, u32[]{:S(2)}, u32[]{:S(2)}) collective-permute-start(bf16[176,128]{1,0:T(8,128)(2,1)S(1)} %pad_maximum_fusion.1), channel_id=1, source_target_pairs={{0,2},{1,3},{2,0},{3,1},{4,6},{5,7},{6,4},{7,5},{8,10},{9,11},{10,... | collective-permute-start | bytes 135176 | tf_op jit(solution)/shard_map/ppermute | solution.py:521
  81.0 1.4 %collective-permute-done.11 = bf16[176,128]{1,0:T(8,128)(2,1)S(1)} collective-permute-done((bf16[176,128]{1,0:T(8,128)(2,1)S(1)}, bf16[176,128]{1,0:T(8,128)(2,1)S(1)}, u32[]{:S(2)}, u32[]{:S(2)}) %collective-permute-start.11) | collective-permute-done | bytes 45088 | tf_op jit(solution)/shard_map/ppermute | solution.py:521
  82.4 3.6 %collective-permute-start.12 = (bf16[176,128]{1,0:T(8,128)(2,1)S(1)}, bf16[176,128]{1,0:T(8,128)(2,1)S(1)}, u32[]{:S(2)}, u32[]{:S(2)}) collective-permute-start(bf16[176,128]{1,0:T(8,128)(2,1)S(1)} %add_convert_fusion.2), channel_id=1, source_target_pairs={{0,4},{1,5},{2,6},{3,7},{4,0},{5,1},{6,2},{7,3},{8,12},{9,13},{10,... | collective-permute-start | bytes 135176 | tf_op jit(solution)/shard_map/ppermute | solution.py:521
  86.0 8.3 %collective-permute-start.17 = (f32[64,64]{1,0:T(8,128)S(1)}, f32[64,64]{1,0:T(8,128)S(1)}, u32[]{:S(2)}, u32[]{:S(2)}) collective-permute-start(f32[64,64]{1,0:T(8,128)S(1)} %get-tuple-element.45.direct_ref), channel_id=1, source_target_pairs={{0,0},{1,16},{2,32},{3,48},{4,64},{5,80},{6,96},{7,112},{8,128},{9... | collective-permute-start | bytes 49160 | tf_op jit(solution)/shard_map/ppermute | solution.py:526
  94.4 4.7 %collective-permute-start.13 = (bf16[176,128]{1,0:T(8,128)(2,1)S(1)}, bf16[176,128]{1,0:T(8,128)(2,1)S(1)}, u32[]{:S(2)}, u32[]{:S(2)}) collective-permute-start(bf16[176,128]{1,0:T(8,128)(2,1)S(1)} %add_convert_fusion.1), channel_id=1, source_target_pairs={{0,12},{1,13},{2,14},{3,15},{4,8},{5,9},{6,10},{7,11},{8,4},{9,5},... | collective-permute-start | bytes 135176 | tf_op jit(solution)/shard_map/ppermute | solution.py:521
  99.2 1.9 %collective-permute-start.16 = (bf16[64,128]{1,0:T(8,128)(2,1)S(1)}, bf16[64,128]{1,0:T(8,128)(2,1)S(1)}, u32[]{:S(2)}, u32[]{:S(2)}) collective-permute-start(bf16[64,128]{1,0:T(8,128)(2,1)S(1)} %add_convert_fusion.9), channel_id=1, source_target_pairs={{0,32},{1,33},{2,34},{3,35},{4,36},{5,37},{6,38},{7,39},{8,40},{9,... | collective-permute-start | bytes 49160 | tf_op jit(solution)/shard_map/ppermute | solution.py:521
  104.0 1.5 %shard_map.126 = (f32[64,64]{1,0:T(8,128)}, f32[64,128]{1,0:T(8,128)}, f32[64,128]{1,0:T(8,128)}, f32[3,32,288]{2,1,0:T(8,128)}) custom-call(s32[8]{0:T(128)S(1)} %pad_add_fusion.place_ref, bf16[176,128]{1,0:T(8,128)(2,1)S(1)} %add_convert_fusion.mine_ref, bf16[112,128]{1,0:T(8,128)(2,1)S(1)} %collective-permute-done.14.got_ref, ...), custom_call_target="tpu_custom_call" | custom-call | flops 1000000000 | bytes 3000000 | tf_op jit(solution)/shard_map/pallas_call | solution.py:562
  (59 shorter events, 10.1 us)
Async XLA Ops:
  0.6 21.6 %copy-start.2 = (f32[64,64]{1,0:T(8,128)S(1)}, f32[64,64]{1,0:T(8,128)}, u32[]{:S(2)}) copy-start(f32[64,64]{1,0:T(8,128)} %cot_ref.1) | copy-start | bytes 49156
  0.6 21.6 %copy-start = (bf16[32,64,64]{2,1,0:T(8,128)(2,1)S(1)}, bf16[32,64,64]{2,1,0:T(8,128)(2,1)}, u32[]{:S(2)}) copy-start(bf16[32,64,64]{2,1,0:T(8,128)(2,1)} %pair_ref.1) | copy-start | bytes 786436
  0.7 21.6 %collective-permute-start = (f32[64,64]{1,0:T(8,128)}, f32[64,64]{1,0:T(8,128)S(1)}, u32[]{:S(2)}, u32[]{:S(2)}) collective-permute-start(f32[64,64]{1,0:T(8,128)} %cot_ref.1), channel_id=1, source_target_pairs={{0,0},{1,16},{2,32},{3,48},{4,64},{5,80},{6,96},{7,112},{8,128},{9... | collective-permute-start | bytes 49160 | tf_op jit(solution)/shard_map/ppermute | solution.py:467
  8.3 33.8 %all-to-all-start = ((bf16[256,4,128]{2,1,0:T(4,128)(2,1)}), bf16[256,4,128]{2,1,0:T(4,128)(2,1)S(1)}, u32[]{:S(2)}, u32[]{:S(2)}) async-start(bf16[256,4,128]{2,1,0:T(4,128)(2,1)} %shard_map.120), calls=%async_computation | async-start | bytes 524288 | tf_op jit(solution)/shard_map/all_to_all | solution.py:471
  22.8 19.3 %copy-start.1 = (bf16[3,32,288]{2,1,0:T(8,128)(2,1)S(1)}, bf16[3,32,288]{2,1,0:T(8,128)(2,1)}, u32[]{:S(2)}) copy-start(bf16[3,32,288]{2,1,0:T(8,128)(2,1)} %forward_ref.1) | copy-start | bytes 165892
  22.8 19.3 %copy-start.3 = (bf16[128,128]{1,0:T(8,128)(2,1)S(1)}, bf16[128,128]{1,0:T(8,128)(2,1)}, u32[]{:S(2)}) copy-start(bf16[128,128]{1,0:T(8,128)(2,1)} %w_left_ref.3) | copy-start | bytes 98308
  22.8 19.3 %copy-start.4 = (bf16[128,128]{1,0:T(8,128)(2,1)S(1)}, bf16[128,128]{1,0:T(8,128)(2,1)}, u32[]{:S(2)}) copy-start(bf16[128,128]{1,0:T(8,128)(2,1)} %w_right_ref.3) | copy-start | bytes 98308
  22.8 8.3 %collective-permute-start.1 = (bf16[17,32,128]{2,1,0:T(8,128)(2,1)S(1)}, bf16[17,32,128]{2,1,0:T(8,128)(2,1)S(1)}, u32[]{:S(2)}, u32[]{:S(2)}) collective-permute-start(bf16[17,32,128]{2,1,0:T(8,128)(2,1)S(1)} %get-tuple-element.28), channel_id=1, source_target_pairs={{0,1},{1,2},{2,3},{3,4},{4,5},{5,6},{6,7},{7,8},{8,9},{9,10},{10,1... | collective-permute-start | bytes 417800 | tf_op jit(solution)/shard_map/ppermute | solution.py:482
  27.8 8.3 %collective-permute-start.2 = (bf16[17,32,128]{2,1,0:T(8,128)(2,1)S(1)}, bf16[17,32,128]{2,1,0:T(8,128)(2,1)S(1)}, u32[]{:S(2)}, u32[]{:S(2)}) collective-permute-start(bf16[17,32,128]{2,1,0:T(8,128)(2,1)S(1)} %get-tuple-element.29), channel_id=1, source_target_pairs={{1,0},{2,1},{3,2},{4,3},{5,4},{6,5},{7,6},{8,7},{9,8},{10,9},{11,1... | collective-permute-start | bytes 417800 | tf_op jit(solution)/shard_map/ppermute | solution.py:483
  36.4 10.2 %collective-permute-start.3 = (bf16[34,32,128]{2,1,0:T(8,128)(2,1)S(1)}, bf16[34,32,128]{2,1,0:T(8,128)(2,1)S(1)}, u32[]{:S(2)}, u32[]{:S(2)}) collective-permute-start(bf16[34,32,128]{2,1,0:T(8,128)(2,1)S(1)} %get-tuple-element.30.part2_ref), channel_id=1, source_target_pairs={{0,16},{16,32},{32,48},{48,64},{64,80},{80,96},{96,112},{112,128},... | collective-permute-start | bytes 835592 | tf_op jit(solution)/shard_map/ppermute | solution.py:488
  39.9 9.0 %collective-permute-start.4 = (bf16[34,32,128]{2,1,0:T(8,128)(2,1)S(1)}, bf16[34,32,128]{2,1,0:T(8,128)(2,1)S(1)}, u32[]{:S(2)}, u32[]{:S(2)}) collective-permute-start(bf16[34,32,128]{2,1,0:T(8,128)(2,1)S(1)} %get-tuple-element.31.part1_ref), channel_id=1, source_target_pairs={{16,0},{32,16},{48,32},{64,48},{80,64},{96,80},{112,96},{128,112},... | collective-permute-start | bytes 835592 | tf_op jit(solution)/shard_map/ppermute | solution.py:489
  60.0 1.3 %collective-permute-start.5 = (bf16[112,128]{1,0:T(8,128)(2,1)S(1)}, bf16[112,128]{1,0:T(8,128)(2,1)S(1)}, u32[]{:S(2)}, u32[]{:S(2)}) collective-permute-start(bf16[112,128]{1,0:T(8,128)(2,1)S(1)} %broadcast_select_fusion), channel_id=1, source_target_pairs={{0,16},{1,17},{2,18},{3,19},{4,20},{5,21},{6,22},{7,23},{8,24},{9,... | collective-permute-start | bytes 86024 | tf_op jit(solution)/shard_map/ppermute | solution.py:521
  61.3 5.9 %collective-permute-start.7 = (bf16[112,128]{1,0:T(8,128)(2,1)S(1)}, bf16[112,128]{1,0:T(8,128)(2,1)S(1)}, u32[]{:S(2)}, u32[]{:S(2)}) collective-permute-start(bf16[112,128]{1,0:T(8,128)(2,1)S(1)} %add_convert_fusion.7), channel_id=1, source_target_pairs={{0,32},{1,33},{2,34},{3,35},{4,36},{5,37},{6,38},{7,39},{8,40},{9,... | collective-permute-start | bytes 86024 | tf_op jit(solution)/shard_map/ppermute | solution.py:521
  67.2 3.0 %collective-permute-start.8 = (bf16[176,128]{1,0:T(8,128)(2,1)S(1)}, bf16[176,128]{1,0:T(8,128)(2,1)S(1)}, u32[]{:S(2)}, u32[]{:S(2)}) collective-permute-start(bf16[176,128]{1,0:T(8,128)(2,1)S(1)} %pad_maximum_fusion), channel_id=1, source_target_pairs={{0,64},{1,65},{2,66},{3,67},{4,68},{5,69},{6,70},{7,71},{8,72},{9,... | collective-permute-start | bytes 135176 | tf_op jit(solution)/shard_map/ppermute | solution.py:521
  70.2 4.2 %collective-permute-start.9 = (bf16[176,128]{1,0:T(8,128)(2,1)S(1)}, bf16[176,128]{1,0:T(8,128)(2,1)S(1)}, u32[]{:S(2)}, u32[]{:S(2)}) collective-permute-start(bf16[176,128]{1,0:T(8,128)(2,1)S(1)} %add_convert_fusion.4), channel_id=1, source_target_pairs={{0,192},{1,193},{2,194},{3,195},{4,196},{5,197},{6,198},{7,199},{8... | collective-permute-start | bytes 135176 | tf_op jit(solution)/shard_map/ppermute | solution.py:521
  71.6 4.1 %collective-permute-start.6 = (bf16[64,128]{1,0:T(8,128)(2,1)S(1)}, bf16[64,128]{1,0:T(8,128)(2,1)S(1)}, u32[]{:S(2)}, u32[]{:S(2)}) collective-permute-start(bf16[64,128]{1,0:T(8,128)(2,1)S(1)} %get-tuple-element.42), channel_id=1, source_target_pairs={{0,1},{1,0},{2,3},{3,2},{4,5},{5,4},{6,7},{7,6},{8,9},{9,8},{10,11... | collective-permute-start | bytes 49160 | tf_op jit(solution)/shard_map/ppermute | solution.py:521
  74.5 4.0 %collective-permute-start.10 = (bf16[112,128]{1,0:T(8,128)(2,1)S(1)}, bf16[112,128]{1,0:T(8,128)(2,1)S(1)}, u32[]{:S(2)}, u32[]{:S(2)}) collective-permute-start(bf16[112,128]{1,0:T(8,128)(2,1)S(1)} %slice.22), channel_id=1, source_target_pairs={{0,33},{1,32},{2,35},{3,34},{4,37},{5,36},{6,39},{7,38},{8,41},{9,... | collective-permute-start | bytes 86024 | tf_op jit(solution)/shard_map/ppermute | solution.py:521
  78.5 3.9 %collective-permute-start.11 = (bf16[176,128]{1,0:T(8,128)(2,1)S(1)}, bf16[176,128]{1,0:T(8,128)(2,1)S(1)}, u32[]{:S(2)}, u32[]{:S(2)}) collective-permute-start(bf16[176,128]{1,0:T(8,128)(2,1)S(1)} %pad_maximum_fusion.1), channel_id=1, source_target_pairs={{0,2},{1,3},{2,0},{3,1},{4,6},{5,7},{6,4},{7,5},{8,10},{9,11},{10,... | collective-permute-start | bytes 135176 | tf_op jit(solution)/shard_map/ppermute | solution.py:521
  82.4 12.0 %collective-permute-start.12 = (bf16[176,128]{1,0:T(8,128)(2,1)S(1)}, bf16[176,128]{1,0:T(8,128)(2,1)S(1)}, u32[]{:S(2)}, u32[]{:S(2)}) collective-permute-start(bf16[176,128]{1,0:T(8,128)(2,1)S(1)} %add_convert_fusion.2), channel_id=1, source_target_pairs={{0,4},{1,5},{2,6},{3,7},{4,0},{5,1},{6,2},{7,3},{8,12},{9,13},{10,... | collective-permute-start | bytes 135176 | tf_op jit(solution)/shard_map/ppermute | solution.py:521
  86.0 17.1 %collective-permute-start.17 = (f32[64,64]{1,0:T(8,128)S(1)}, f32[64,64]{1,0:T(8,128)S(1)}, u32[]{:S(2)}, u32[]{:S(2)}) collective-permute-start(f32[64,64]{1,0:T(8,128)S(1)} %get-tuple-element.45.direct_ref), channel_id=1, source_target_pairs={{0,0},{1,16},{2,32},{3,48},{4,64},{5,80},{6,96},{7,112},{8,128},{9... | collective-permute-start | bytes 49160 | tf_op jit(solution)/shard_map/ppermute | solution.py:526
  94.3 4.8 %collective-permute-start.15 = (bf16[64,128]{1,0:T(8,128)(2,1)S(1)}, bf16[64,128]{1,0:T(8,128)(2,1)S(1)}, u32[]{:S(2)}, u32[]{:S(2)}) collective-permute-start(bf16[64,128]{1,0:T(8,128)(2,1)S(1)} %slice.24), channel_id=1, source_target_pairs={{0,16},{1,17},{2,18},{3,19},{4,20},{5,21},{6,22},{7,23},{8,24},{9,... | collective-permute-start | bytes 49160 | tf_op jit(solution)/shard_map/ppermute | solution.py:521
  94.4 7.7 %collective-permute-start.13 = (bf16[176,128]{1,0:T(8,128)(2,1)S(1)}, bf16[176,128]{1,0:T(8,128)(2,1)S(1)}, u32[]{:S(2)}, u32[]{:S(2)}) collective-permute-start(bf16[176,128]{1,0:T(8,128)(2,1)S(1)} %add_convert_fusion.1), channel_id=1, source_target_pairs={{0,12},{1,13},{2,14},{3,15},{4,8},{5,9},{6,10},{7,11},{8,4},{9,5},... | collective-permute-start | bytes 135176 | tf_op jit(solution)/shard_map/ppermute | solution.py:521
  99.2 4.0 %collective-permute-start.16 = (bf16[64,128]{1,0:T(8,128)(2,1)S(1)}, bf16[64,128]{1,0:T(8,128)(2,1)S(1)}, u32[]{:S(2)}, u32[]{:S(2)}) collective-permute-start(bf16[64,128]{1,0:T(8,128)(2,1)S(1)} %add_convert_fusion.9), channel_id=1, source_target_pairs={{0,32},{1,33},{2,34},{3,35},{4,36},{5,37},{6,38},{7,39},{8,40},{9,... | collective-permute-start | bytes 49160 | tf_op jit(solution)/shard_map/ppermute | solution.py:521
  102.2 1.7 %collective-permute-start.14 = (bf16[112,128]{1,0:T(8,128)(2,1)S(1)}, bf16[112,128]{1,0:T(8,128)(2,1)S(1)}, u32[]{:S(2)}, u32[]{:S(2)}) collective-permute-start(bf16[112,128]{1,0:T(8,128)(2,1)S(1)} %slice.23), channel_id=1, source_target_pairs={{0,16},{1,17},{2,18},{3,19},{4,20},{5,21},{6,22},{7,23},{8,24},{9,... | collective-permute-start | bytes 86024 | tf_op jit(solution)/shard_map/ppermute | solution.py:521
  (4 other events, 35.8 us)
